TPU v7x, 32 devices: a whole 2x2x4 slice. The times are simulated.
32 devices in a mesh: wide: 16 (over z, y, x), narrow: 2 (over core).
Axes of the slice: x: 2, y: 2, z: 4, core: 2. Of those that a mesh axis runs over, the one named last changes fastest.
Arguments:
- tokens: bfloat16 [8192, 768], P(('wide', 'narrow')), may hold values from -6 to 6
- seg_ids: int32 [8192], P(('wide', 'narrow')), may hold values from 0 to 1, as said below
- frame_ids: int32 [8192], P(('wide', 'narrow')), may hold values from 0 to 15, as said below
- patch_ids: int32 [8192], P(('wide', 'narrow')), may hold values from 0 to 15
- timesteps: int32 [64], P(('wide', 'narrow')), may hold values from 0 to 999
- w_ada: bfloat16 [768, 6912], P(('wide', 'narrow')), may hold values from -0.21875 to 0.21875
- b_ada: bfloat16 [6912], P(('wide', 'narrow')), may hold values from -3 to 3
- w_qkv_spatial: bfloat16 [768, 2304], P(('wide', 'narrow')), may hold values from -0.21875 to 0.21875
- w_out_spatial: bfloat16 [768, 768], P(('wide', 'narrow')), may hold values from -0.4375 to 0.4375
- w_qkv_temporal: bfloat16 [768, 2304], P(('wide', 'narrow')), may hold values from -0.21875 to 0.21875
- w_out_temporal: bfloat16 [768, 768], P(('wide', 'narrow')), may hold values from -0.4375 to 0.4375
- w_up: bfloat16 [768, 3072], P(('wide', 'narrow')), may hold values from -0.21875 to 0.21875
- w_down: bfloat16 [3072, 768], P(('wide', 'narrow')), may hold values from -0.109375 to 0.109375
- cotangent: bfloat16 [8192, 768], P(('wide', 'narrow')), may hold values from -6 to 6
Outputs:
- layer_out: bfloat16 [8192, 768], P(('wide', 'narrow'))
- grad_tokens: float32 [8192, 768], P(('wide', 'narrow'))
- grad_w_ada: float32 [768, 6912], P(('wide', 'narrow'))
- grad_b_ada: float32 [6912], P(('wide', 'narrow'))
- grad_qkv_spatial: float32 [768, 2304], P(('wide', 'narrow'))
- grad_out_spatial: float32 [768, 768], P(('wide', 'narrow'))
- grad_qkv_temporal: float32 [768, 2304], P(('wide', 'narrow'))
- grad_out_temporal: float32 [768, 768], P(('wide', 'narrow'))
- grad_w_up: float32 [768, 3072], P(('wide', 'narrow'))
- grad_w_down: float32 [3072, 768], P(('wide', 'narrow'))
Inputs may be any that keep to these rules, and one draw needn't show every extreme that they name: `seg_ids`: on each device its 256 tokens belong to clips numbered from 0 without gaps; each clip has 8 or 16 frames of 16 patches, 16 frames on a device together; each triple of clip, frame and patch number occurs exactly once on a device, in no particular order. `frame_ids`: frame numbers of a clip run from 0 to its frame count minus 1.
All inputs are finite; a program needn't handle non-finite values.
Results may differ from a plain program's by a relative error of at most 0.02.
Values may be sent and summed in bfloat16 or wider, within the bound.
A program may use at most 320 MiB of HBM per device.

v0:
```python
from functools import partial
import math

import jax
import jax.numpy as jnp
from jax import lax
from jax.sharding import PartitionSpec as P

HEADS = 12


EPSILON = 1e-06
FREQ_BASE = 10000.0
MASKED = -1e30


def time_embed(step_ids, width):
    half_width = width // 2
    frequency = jnp.exp(
        -math.log(FREQ_BASE) * jnp.arange(half_width, dtype=jnp.float32) / half_width
    )
    angles = step_ids.astype(jnp.float32)[:, None] * frequency[None, :]
    return jnp.concatenate([jnp.cos(angles), jnp.sin(angles)], axis=1)


def contract_rows(left, right):
    return lax.dot_general(
        left, right, (((0,), (0,)), ((), ())), preferred_element_type=jnp.float32
    )


def contract_cols(left, right):
    return lax.dot_general(
        left, right, (((1,), (1,)), ((), ())), preferred_element_type=jnp.float32
    )


def exact_rows(left, right):
    return lax.dot_general(
        left,
        right,
        (((0,), (0,)), ((), ())),
        precision=lax.Precision.HIGHEST,
        preferred_element_type=jnp.float32,
    )


def layer_norm_apply(stream):
    center = stream - jnp.mean(stream, axis=-1, keepdims=True)
    inverse_deviation = lax.rsqrt(jnp.mean(center * center, axis=-1, keepdims=True) + EPSILON)
    return (center * inverse_deviation, inverse_deviation)


def layer_norm_reverse(normalized_gradient, standardized_input, inverse_deviation, row_scales):
    input_gradient = normalized_gradient * (1.0 + row_scales)
    mean_removed = input_gradient - jnp.mean(input_gradient, axis=-1, keepdims=True)
    return inverse_deviation * (
        mean_removed
        - standardized_input * jnp.mean(input_gradient * standardized_input, axis=-1, keepdims=True)
    )


def sublayer_mod(one_hot, modulation, sublayer, width):
    table = modulation[:, 3 * width * sublayer : 3 * width * (sublayer + 1)]
    rows_mod = jnp.dot(
        one_hot, table, precision=lax.Precision.HIGHEST, preferred_element_type=jnp.float32
    )
    return (rows_mod[:, :width], rows_mod[:, width : 2 * width], rows_mod[:, 2 * width :])


def head_probs(allowed, scale, queries, key_vecs):
    scores = contract_cols(queries, key_vecs) * scale
    scores = jnp.where(allowed, scores, MASKED)
    return jax.nn.softmax(scores, axis=-1)


def head_forward(allowed, scale, item):
    queries, key_vecs, val_vecs = item
    attn_prob = head_probs(allowed, scale, queries, key_vecs)
    return jnp.dot(attn_prob.astype(jnp.bfloat16), val_vecs, preferred_element_type=jnp.float32)


def head_backward(allowed, scale, item):
    queries, key_vecs, val_vecs, grad_att = item
    attn_prob = head_probs(allowed, scale, queries, key_vecs)
    grad_val = contract_rows(attn_prob.astype(jnp.bfloat16), grad_att)
    grad_prob = contract_cols(grad_att, val_vecs)
    grad_score = attn_prob * (grad_prob - jnp.sum(attn_prob * grad_prob, axis=-1, keepdims=True))
    score_low = grad_score.astype(jnp.bfloat16)
    grad_query = jnp.dot(score_low, key_vecs, preferred_element_type=jnp.float32) * scale
    grad_key = contract_rows(score_low, queries) * scale
    return (grad_query, grad_key, grad_val)


def split_heads(qkv_rows, head_count):
    row_count = qkv_rows.shape[0]
    return qkv_rows.reshape(row_count, 3, head_count, -1).transpose(1, 2, 0, 3)


def attention_forward(normed, w_qkv, w_out, allowed, head_count):
    row_count = normed.shape[0]
    qkv_rows = jnp.dot(normed, w_qkv, preferred_element_type=jnp.float32).astype(jnp.bfloat16)
    split_qkv = split_heads(qkv_rows, head_count)
    scale = split_qkv.shape[-1] ** (-0.5)
    attended = lax.map(
        partial(head_forward, allowed, scale), (split_qkv[0], split_qkv[1], split_qkv[2])
    )
    merged = attended.transpose(1, 0, 2).reshape(row_count, -1).astype(jnp.bfloat16)
    branch = jnp.dot(merged, w_out, preferred_element_type=jnp.float32)
    return (branch, qkv_rows, merged)


def attention_backward(grad_branch, qkv_rows, w_qkv, w_out, allowed, head_count):
    row_count = qkv_rows.shape[0]
    grad_merged = contract_cols(grad_branch, w_out).astype(jnp.bfloat16)
    grad_heads = grad_merged.reshape(row_count, head_count, -1).transpose(1, 0, 2)
    split_qkv = split_heads(qkv_rows, head_count)
    scale = split_qkv.shape[-1] ** (-0.5)
    grad_query, grad_key, grad_val = lax.map(
        partial(head_backward, allowed, scale),
        (split_qkv[0], split_qkv[1], split_qkv[2], grad_heads),
    )
    grad_qkv = (
        jnp.stack([grad_query, grad_key, grad_val])
        .transpose(2, 0, 1, 3)
        .reshape(row_count, -1)
        .astype(jnp.bfloat16)
    )
    normalized_gradient = contract_cols(grad_qkv, w_qkv)
    return (normalized_gradient, grad_qkv)


def on_device(
    tokens,
    seg_ids,
    frame_ids,
    patch_ids,
    timesteps,
    w_ada,
    b_ada,
    w_qkv_spatial,
    w_out_spatial,
    w_qkv_temporal,
    w_out_temporal,
    w_up,
    w_down,
    cotangent,
):
    gathered = (
        lax.all_gather(w_ada, ("wide", "narrow"), axis=0, tiled=True),
        lax.all_gather(b_ada, ("wide", "narrow"), axis=0, tiled=True),
        lax.all_gather(w_qkv_spatial, ("wide", "narrow"), axis=0, tiled=True),
        lax.all_gather(w_out_spatial, ("wide", "narrow"), axis=0, tiled=True),
        lax.all_gather(w_qkv_temporal, ("wide", "narrow"), axis=0, tiled=True),
        lax.all_gather(w_out_temporal, ("wide", "narrow"), axis=0, tiled=True),
        lax.all_gather(w_up, ("wide", "narrow"), axis=0, tiled=True),
        lax.all_gather(w_down, ("wide", "narrow"), axis=0, tiled=True),
    )
    width = tokens.shape[1]
    ff_width = w_down.shape[1] * 0 + gathered[7].shape[0]
    head_count = HEADS
    clip_count = timesteps.shape[0]
    cond_low = jax.nn.silu(time_embed(timesteps, width)).astype(jnp.bfloat16)
    modulation = jnp.dot(cond_low, gathered[0], preferred_element_type=jnp.float32) + gathered[
        1
    ].astype(jnp.float32)
    one_hot = (seg_ids[:, None] == jnp.arange(clip_count, dtype=jnp.int32)[None, :]).astype(
        jnp.float32
    )
    offset_first, scale_first, gate_a = sublayer_mod(one_hot, modulation, 0, width)
    offset_second, scale_second, gate_b = sublayer_mod(one_hot, modulation, 1, width)
    offset_third, scale_third, gate_c = sublayer_mod(one_hot, modulation, 2, width)
    same_clip = seg_ids[:, None] == seg_ids[None, :]
    spatial_mask = same_clip & (frame_ids[:, None] == frame_ids[None, :])
    temporal_mask = same_clip & (patch_ids[:, None] == patch_ids[None, :])
    residual_first = tokens.astype(jnp.float32)
    standardized_first, inverse_deviation_first = layer_norm_apply(residual_first)
    normalized_first = (standardized_first * (1.0 + scale_first) + offset_first).astype(
        jnp.bfloat16
    )
    branch_a, qkv_a, merged_a = attention_forward(
        normalized_first, gathered[2], gathered[3], spatial_mask, head_count
    )
    residual_second = residual_first + gate_a * branch_a
    standardized_second, inverse_deviation_second = layer_norm_apply(residual_second)
    normalized_second = (standardized_second * (1.0 + scale_second) + offset_second).astype(
        jnp.bfloat16
    )
    branch_b, qkv_b, merged_b = attention_forward(
        normalized_second, gathered[4], gathered[5], temporal_mask, head_count
    )
    residual_third = residual_second + gate_b * branch_b
    standardized_third, inverse_deviation_third = layer_norm_apply(residual_third)
    normalized_third = (standardized_third * (1.0 + scale_third) + offset_third).astype(
        jnp.bfloat16
    )
    pre_act = jnp.dot(normalized_third, gathered[6], preferred_element_type=jnp.float32)
    act_out, gelu_pull = jax.vjp(jax.nn.gelu, pre_act)
    hidden = act_out.astype(jnp.bfloat16)
    branch_c = jnp.dot(hidden, gathered[7], preferred_element_type=jnp.float32)
    result = residual_third + gate_c * branch_c
    back_weights = (
        lax.all_gather(w_ada, ("wide", "narrow"), axis=0, tiled=True),
        lax.all_gather(b_ada, ("wide", "narrow"), axis=0, tiled=True),
        lax.all_gather(w_qkv_spatial, ("wide", "narrow"), axis=0, tiled=True),
        lax.all_gather(w_out_spatial, ("wide", "narrow"), axis=0, tiled=True),
        lax.all_gather(w_qkv_temporal, ("wide", "narrow"), axis=0, tiled=True),
        lax.all_gather(w_out_temporal, ("wide", "narrow"), axis=0, tiled=True),
        lax.all_gather(w_up, ("wide", "narrow"), axis=0, tiled=True),
        lax.all_gather(w_down, ("wide", "narrow"), axis=0, tiled=True),
    )
    output_gradient = cotangent.astype(jnp.float32)
    gate_gradient_third = output_gradient * branch_c
    grad_branch_c = (gate_c * output_gradient).astype(jnp.bfloat16)
    grad_hidden = contract_cols(grad_branch_c, back_weights[7])
    grad_pre = gelu_pull(grad_hidden)[0].astype(jnp.bfloat16)
    normalized_gradient_third = contract_cols(grad_pre, back_weights[6])
    residual_gradient = output_gradient + layer_norm_reverse(
        normalized_gradient_third, standardized_third, inverse_deviation_third, scale_third
    )
    gate_gradient_second = residual_gradient * branch_b
    grad_branch_b = (gate_b * residual_gradient).astype(jnp.bfloat16)
    normalized_gradient_second, grad_qkv_t = attention_backward(
        grad_branch_b, qkv_b, back_weights[4], back_weights[5], temporal_mask, head_count
    )
    residual_gradient = residual_gradient + layer_norm_reverse(
        normalized_gradient_second, standardized_second, inverse_deviation_second, scale_second
    )
    gate_gradient_first = residual_gradient * branch_a
    grad_branch_a = (gate_a * residual_gradient).astype(jnp.bfloat16)
    normalized_gradient_first, grad_qkv_s = attention_backward(
        grad_branch_a, qkv_a, back_weights[2], back_weights[3], spatial_mask, head_count
    )
    residual_gradient = residual_gradient + layer_norm_reverse(
        normalized_gradient_first, standardized_first, inverse_deviation_first, scale_first
    )
    grad_mod = jnp.concatenate(
        [
            exact_rows(
                one_hot,
                jnp.concatenate(
                    [
                        normalized_gradient_first,
                        normalized_gradient_first * standardized_first,
                        gate_gradient_first,
                    ],
                    axis=1,
                ),
            ),
            exact_rows(
                one_hot,
                jnp.concatenate(
                    [
                        normalized_gradient_second,
                        normalized_gradient_second * standardized_second,
                        gate_gradient_second,
                    ],
                    axis=1,
                ),
            ),
            exact_rows(
                one_hot,
                jnp.concatenate(
                    [
                        normalized_gradient_third,
                        normalized_gradient_third * standardized_third,
                        gate_gradient_third,
                    ],
                    axis=1,
                ),
            ),
        ],
        axis=1,
    )
    grad_mod_low = grad_mod.astype(jnp.bfloat16)
    bias_rows = jnp.sum(grad_mod, axis=0).reshape(width, 9)
    row_share = lax.psum_scatter(
        jnp.concatenate(
            [
                contract_rows(cond_low, grad_mod_low),
                contract_rows(normalized_first, grad_qkv_s),
                contract_rows(merged_a, grad_branch_a),
                contract_rows(normalized_second, grad_qkv_t),
                contract_rows(merged_b, grad_branch_b),
                contract_rows(normalized_third, grad_pre),
                bias_rows,
            ],
            axis=1,
        ),
        ("wide", "narrow"),
        scatter_dimension=0,
        tiled=True,
    )
    down_share = lax.psum_scatter(
        contract_rows(hidden, grad_branch_c), ("wide", "narrow"), scatter_dimension=0, tiled=True
    )
    edges = [
        0,
        9 * width,
        12 * width,
        13 * width,
        16 * width,
        17 * width,
        17 * width + ff_width,
        17 * width + ff_width + 9,
    ]
    pieces = [row_share[:, edges[index] : edges[index + 1]] for index in range(7)]
    return (
        result.astype(jnp.bfloat16),
        residual_gradient,
        pieces[0],
        pieces[6].reshape(-1),
        pieces[1],
        pieces[2],
        pieces[3],
        pieces[4],
        pieces[5],
        down_share,
    )


def solution(mesh):
    placed = (
        P(("wide", "narrow"), None),
        P(("wide", "narrow")),
        P(("wide", "narrow")),
        P(("wide", "narrow")),
        P(("wide", "narrow")),
        P(("wide", "narrow"), None),
        P(("wide", "narrow")),
        P(("wide", "narrow"), None),
        P(("wide", "narrow"), None),
        P(("wide", "narrow"), None),
        P(("wide", "narrow"), None),
        P(("wide", "narrow"), None),
        P(("wide", "narrow"), None),
        P(("wide", "narrow"), None),
    )
    return jax.shard_map(
        on_device,
        mesh=mesh,
        in_specs=placed,
        out_specs=(
            P(("wide", "narrow"), None),
            P(("wide", "narrow"), None),
            P(("wide", "narrow"), None),
            P(("wide", "narrow")),
            P(("wide", "narrow"), None),
            P(("wide", "narrow"), None),
            P(("wide", "narrow"), None),
            P(("wide", "narrow"), None),
            P(("wide", "narrow"), None),
            P(("wide", "narrow"), None),
        ),
        check_vma=False,
    )
```

profile of v0, /device:TPU:0, one launch (start us, length us, event | category | flops | bytes accessed | tf_op | source)
XLA Modules:
  0.0 1572.0 jit_solution(12347525134263095765)
XLA Ops:
  15.9 42.7 %all-reduce = bf16[6912]{0:T(1024)(128)(2,1)S(1)} all-reduce(bf16[6912]{0:T(1024)(128)(2,1)S(1)} %dynamic-update-slice), channel_id=1, replica_groups=mesh['wide'=16,'narrow'=2] {'wide','narrow'}, use_global_device_ids=true, to_apply=%add | all-reduce | flops 6912 | bytes 27648
  58.7 42.2 %all-gather.8.cloned.1.call-done = bf16[768,6912]{1,0:T(8,128)(2,1)} async-done(((bf16[24,6912]{1,0:T(8,128)(2,1)}), bf16[768,6912]{1,0:T(8,128)(2,1)}) %all-gather.8.cloned.1.call-update) | async-done | bytes 10616848 | tf_op jit(solution)/shard_map/all_gather | solution.py:150
  101.0 5.5 convolution_add_fusion
  106.5 2.6 fusion.141
  110.5 51.9 %all-gather.10.cloned.1.call-done = bf16[768,2304]{1,0:T(8,128)(2,1)} async-done(((bf16[24,2304]{1,0:T(8,128)(2,1)}), bf16[768,2304]{1,0:T(8,128)(2,1)}) %all-gather.10.cloned.1.call-update) | async-done | bytes 3538960 | tf_op jit(solution)/shard_map/all_gather | solution.py:152
  162.4 4.1 convolution_convert_fusion.1
  166.5 2.4 copy.50
  175.5 27.0 %while.52 = (s32[]{:T(128)}, bf16[12,256,64]{1,2,0:T(8,128)(2,1)S(1)}, bf16[12,256,64]{2,1,0:T(8,128)(2,1)}, bf16[12,256,64]{2,1,0:T(8,128)(2,1)}, bf16[12,256,6...) while((s32[]{:T(128)}, bf16[12,256,64]{1,2,0:T(8,128)(2,1)S(1)}, ...), condition=%wide.region_5.6_spmd.clone, body=%wide.region_2.5_spmd.clone.sunk | while | flops 17497600 | bytes 1059933 | solution.py:105
  202.5 15.7 all-gather.12.cloned.1.call-done
  218.2 2.9 fusion.173
  223.0 57.0 %all-gather.14.cloned.1.call-done = bf16[768,2304]{1,0:T(8,128)(2,1)} async-done(((bf16[24,2304]{1,0:T(8,128)(2,1)}), bf16[768,2304]{1,0:T(8,128)(2,1)}) %all-gather.14.cloned.1.call-update) | async-done | bytes 3538960 | tf_op jit(solution)/shard_map/all_gather | solution.py:154
  280.0 4.3 convolution_convert_fusion
  296.2 34.4 %while.53 = (s32[]{:T(128)}, bf16[12,256,64]{1,2,0:T(8,128)(2,1)}, bf16[12,256,64]{2,1,0:T(8,128)(2,1)}, bf16[12,256,64]{2,1,0:T(8,128)(2,1)}, bf16[12,256,64]{2...) while((s32[]{:T(128)}, bf16[12,256,64]{1,2,0:T(8,128)(2,1)}, ...), condition=%wide.region_11.12_spmd.clone, body=%wide.region_8.11_spmd.clone.sunk | while | flops 17497600 | bytes 1059933 | solution.py:105
  330.6 5.0 all-gather.16.cloned.1.call-done
  335.6 3.0 fusion.172
  343.2 57.7 %all-gather.18.cloned.1.call-done = bf16[768,3072]{1,0:T(8,128)(2,1)} async-done(((bf16[24,3072]{1,0:T(8,128)(2,1)}), bf16[768,3072]{1,0:T(8,128)(2,1)}) %all-gather.18.cloned.1.call-update) | async-done | bytes 4718608 | tf_op jit(solution)/shard_map/all_gather | solution.py:156
  400.9 5.5 fusion.180
  406.4 59.9 %all-gather.20.cloned.1.call-done = bf16[3072,768]{1,0:T(8,128)(2,1)} async-done(((bf16[96,768]{1,0:T(8,128)(2,1)}), bf16[3072,768]{1,0:T(8,128)(2,1)}) %all-gather.20.cloned.1.call-update) | async-done | bytes 4718608 | tf_op jit(solution)/shard_map/all_gather | solution.py:157
  466.3 6.4 fusion.100
  477.3 3.5 fusion.171
  489.2 86.5 %while.54 = (s32[]{:T(128)}, bf16[12,256,64]{1,2,0:T(8,128)(2,1)}, bf16[12,256,64]{1,2,0:T(8,128)(2,1)}, bf16[12,256,64]{1,2,0:T(8,128)(2,1)}, bf16[12,256,64]{2...) while((s32[]{:T(128)}, bf16[12,256,64]{1,2,0:T(8,128)(2,1)}, ...), condition=%wide.region_20.21_spmd.clone, body=%wide.region_16.20_spmd.clone.sunk | while | flops 43285760 | bytes 2838645 | solution.py:119
  577.1 4.0 fusion.167
  581.3 2.9 fusion.170
  588.3 78.8 %while.55 = (s32[]{:T(128)}, bf16[12,256,64]{1,2,0:T(8,128)(2,1)}, bf16[12,256,64]{1,2,0:T(8,128)(2,1)}, bf16[12,256,64]{1,2,0:T(8,128)(2,1)S(1)}, bf16[12,256,6...) while((s32[]{:T(128)}, bf16[12,256,64]{1,2,0:T(8,128)(2,1)}, ...), condition=%wide.region_27.28_spmd.clone, body=%wide.region_23.27_spmd.clone.sunk | while | flops 43285760 | bytes 2838645 | solution.py:119
  668.4 3.8 fusion.168
  676.6 9.0 convolution_dynamic-update-slice_fusion
  685.9 4.0 convolution_dynamic-update-slice_fusion.3
  691.8 4.0 convolution_dynamic-update-slice_fusion.2
  697.7 5.0 convolution_dynamic-update-slice_fusion.1
  704.6 7.9 fusion.160
  712.5 710.3 %all-reduce.4.cloned.1.call-done = f32[768,16137]{1,0:T(8,128)} async-done(((f32[768,16137]{1,0:T(8,128)}), f32[768,16137]{1,0:T(8,128)}) %all-reduce.4.cloned.1.call-update) | async-done | bytes 49572880
  1431.8 133.2 %reduce-scatter.2.cloned.1.call-done = f32[96,768]{1,0:T(8,128)} async-done(((f32[3072,768]{1,0:T(8,128)}), f32[96,768]{1,0:T(8,128)}) %reduce-scatter.2.cloned.1.call-update) | async-done | bytes 294928 | tf_op jit(solution)/shard_map/reduce_scatter | solution.py:294
  (435 shorter events, 299.4 us)
Async XLA Ops:
  7.2 93.8 %all-gather.8.cloned.1.call-start = ((), (), s32[]{:S(2)}) async-start(), calls=%async_computation.1 | async-start | bytes 10948608 | tf_op jit(solution)/shard_map/all_gather | solution.py:150
  7.9 154.5 %all-gather.10.cloned.1.call-start = ((), (), s32[]{:S(2)}) async-start(), calls=%async_computation.2 | async-start | bytes 3649536 | tf_op jit(solution)/shard_map/all_gather | solution.py:152
  8.7 209.5 %all-gather.12.cloned.1.call-start = ((), (), s32[]{:S(2)}) async-start(), calls=%async_computation.3 | async-start | bytes 1216512 | tf_op jit(solution)/shard_map/all_gather | solution.py:153
  9.4 270.6 %all-gather.14.cloned.1.call-start = ((), (), s32[]{:S(2)}) async-start(), calls=%async_computation.4 | async-start | bytes 3649536 | tf_op jit(solution)/shard_map/all_gather | solution.py:154
  10.0 325.6 %all-gather.16.cloned.1.call-start = ((), (), s32[]{:S(2)}) async-start(), calls=%async_computation.5 | async-start | bytes 1216512 | tf_op jit(solution)/shard_map/all_gather | solution.py:155
  10.6 390.4 %all-gather.18.cloned.1.call-start = ((), (), s32[]{:S(2)}) async-start(), calls=%async_computation.6 | async-start | bytes 4866048 | tf_op jit(solution)/shard_map/all_gather | solution.py:156
  11.1 455.2 %all-gather.20.cloned.1.call-start = ((), (), s32[]{:S(2)}) async-start(), calls=%async_computation.7 | async-start | bytes 4866048 | tf_op jit(solution)/shard_map/all_gather | solution.py:157
  11.9 1411.0 %all-reduce.4.cloned.1.call-start = ((), (), s32[]{:S(2)}) async-start(), calls=%async_computation.9 | async-start | bytes 99876864
  15.0 95.2 %copy-start.40 = (f32[256]{0:T(256)}, f32[256]{0:T(256)S(1)}, u32[]{:S(2)}) copy-start(f32[256]{0:T(256)S(1)} %add_rsqrt_fusion.2) | copy-start | bytes 3076
  101.0 5.5 copy-start.37
  110.5 58.4 %copy-start.24 = (bf16[256,768]{1,0:T(8,128)(2,1)}, bf16[256,768]{1,0:T(8,128)(2,1)S(1)}, u32[]{:S(2)}) copy-start(bf16[256,768]{1,0:T(8,128)(2,1)S(1)} %fusion.126) | copy-start | bytes 1179652
  202.5 15.7 copy-start.15
  466.3 6.4 copy-start.3
  466.3 6.4 copy-start.5
  466.3 6.5 copy-start.43
  466.3 6.5 copy-start.47
  466.3 6.5 copy-start.49
  472.8 4.5 copy-start.48
  474.5 6.3 copy-start.50
  477.3 6.4 copy-start.10
  577.1 4.1 copy-start.11
  577.1 4.1 copy-start.20
  577.1 4.1 copy-start.22
  577.1 4.1 copy-start.45
  584.2 4.1 copy-start.39
  668.4 4.9 copy-start.32
  668.4 4.9 copy-start.33
  668.4 4.9 copy-start.52
  676.5 9.3 copy-start.14
  676.6 9.3 copy-start.25
  685.9 4.0 copy-start.16
  703.6 861.4 %reduce-scatter.2.cloned.1.call-start = ((), (), s32[]{:S(2)}) async-start(), calls=%async_computation.8 | async-start | bytes 9732096 | tf_op jit(solution)/shard_map/reduce_scatter | solution.py:294
  (32 other events, 79.7 us)
Sparse Core Ops, SparseCore 0:
  10.9 90.0 all-gather.7
  103.9 58.5 all-gather.9
  165.3 52.8 all-gather.11
  220.9 58.9 all-gather.13
  282.7 52.8 all-gather.15
  338.3 62.5 all-gather.17
  403.8 62.4 all-gather.19
  703.7 719.0 all-reduce.3
  1430.3 134.6 reduce-scatter.1
where the time goes:
time: 1590 us; the launch traced here: 1570 us
  waiting for transfers between devices  1140 us (72%)
  matrix products  309 us (19%)
  local copies, waits for them, and re-layouts  47.1 us (3%)
  blocking collectives  42.7 us (3%)
  other arithmetic  19.3 us (1%)
    unnamed x10, waiting for transfers between devices  715 us
    reduce_scatter x1, waiting for transfers between devices, on_device(): lax.psum_scatter(contract_rows(hidden, grad_branch_c), ('wide', 'narrow')...  133 us
    dot_general x55, matrix products, contract_rows(): lax.dot_general(left, right, (((0,), (0,)), ((), ())), preferred_element_...  104 us
    dot_general x78, matrix products, contract_cols(): lax.dot_general(left, right, (((1,), (1,)), ((), ())), preferred_element_...  96 us
    all_gather x1, waiting for transfers between devices, on_device(): lax.all_gather(w_down, ('wide', 'narrow'), axis=0, tiled=True)  59.9 us
    all_gather x1, waiting for transfers between devices, on_device(): lax.all_gather(w_up, ('wide', 'narrow'), axis=0, tiled=True)  57.7 us
    all_gather x1, waiting for transfers between devices, on_device(): lax.all_gather(w_qkv_temporal, ('wide', 'narrow'), axis=0, tiled=True)  57 us
    all_gather x1, waiting for transfers between devices, on_device(): lax.all_gather(w_qkv_spatial, ('wide', 'narrow'), axis=0, tiled=True)  51.9 us
  transfers between devices with their start and end apart: 9, of which 9 were waited for; matrix products, arithmetic and copies ran while one was open for 9% of the time, Pallas kernels for 0%

commit v1 on v0

--- a/solution.py
+++ b/solution.py
@@ -146,24 +146,32 @@
     w_down,
     cotangent,
 ):
+    axes = ("wide", "narrow")
     gathered = (
-        lax.all_gather(w_ada, ("wide", "narrow"), axis=0, tiled=True),
-        lax.all_gather(b_ada, ("wide", "narrow"), axis=0, tiled=True),
-        lax.all_gather(w_qkv_spatial, ("wide", "narrow"), axis=0, tiled=True),
-        lax.all_gather(w_out_spatial, ("wide", "narrow"), axis=0, tiled=True),
-        lax.all_gather(w_qkv_temporal, ("wide", "narrow"), axis=0, tiled=True),
-        lax.all_gather(w_out_temporal, ("wide", "narrow"), axis=0, tiled=True),
-        lax.all_gather(w_up, ("wide", "narrow"), axis=0, tiled=True),
-        lax.all_gather(w_down, ("wide", "narrow"), axis=0, tiled=True),
+        None,
+        None,
+        lax.all_gather(w_qkv_spatial, axes, axis=0, tiled=True),
+        lax.all_gather(w_out_spatial, axes, axis=0, tiled=True),
+        lax.all_gather(w_qkv_temporal, axes, axis=0, tiled=True),
+        lax.all_gather(w_out_temporal, axes, axis=0, tiled=True),
+        lax.all_gather(w_up, axes, axis=0, tiled=True),
+        lax.all_gather(w_down, axes, axis=0, tiled=True),
     )
     width = tokens.shape[1]
-    ff_width = w_down.shape[1] * 0 + gathered[7].shape[0]
     head_count = HEADS
     clip_count = timesteps.shape[0]
-    cond_low = jax.nn.silu(time_embed(timesteps, width)).astype(jnp.bfloat16)
-    modulation = jnp.dot(cond_low, gathered[0], preferred_element_type=jnp.float32) + gathered[
-        1
-    ].astype(jnp.float32)
+    row_count = w_ada.shape[0]
+    place = lax.axis_index(axes)
+    all_steps = lax.all_gather(timesteps, axes, axis=0, tiled=True)
+    cond_all = jax.nn.silu(time_embed(all_steps, width)).astype(jnp.bfloat16)
+    cond_rows = lax.dynamic_slice_in_dim(cond_all, place * row_count, row_count, axis=1)
+    all_bias = lax.all_gather(b_ada, axes, axis=0, tiled=True)
+    modulation = lax.psum_scatter(
+        jnp.dot(cond_rows, w_ada, preferred_element_type=jnp.float32),
+        axes,
+        scatter_dimension=0,
+        tiled=True,
+    ) + all_bias.astype(jnp.float32)
     one_hot = (seg_ids[:, None] == jnp.arange(clip_count, dtype=jnp.int32)[None, :]).astype(
         jnp.float32
     )
@@ -199,16 +207,7 @@
     hidden = act_out.astype(jnp.bfloat16)
     branch_c = jnp.dot(hidden, gathered[7], preferred_element_type=jnp.float32)
     result = residual_third + gate_c * branch_c
-    back_weights = (
-        lax.all_gather(w_ada, ("wide", "narrow"), axis=0, tiled=True),
-        lax.all_gather(b_ada, ("wide", "narrow"), axis=0, tiled=True),
-        lax.all_gather(w_qkv_spatial, ("wide", "narrow"), axis=0, tiled=True),
-        lax.all_gather(w_out_spatial, ("wide", "narrow"), axis=0, tiled=True),
-        lax.all_gather(w_qkv_temporal, ("wide", "narrow"), axis=0, tiled=True),
-        lax.all_gather(w_out_temporal, ("wide", "narrow"), axis=0, tiled=True),
-        lax.all_gather(w_up, ("wide", "narrow"), axis=0, tiled=True),
-        lax.all_gather(w_down, ("wide", "narrow"), axis=0, tiled=True),
-    )
+    back_weights = gathered
     output_gradient = cotangent.astype(jnp.float32)
     gate_gradient_third = output_gradient * branch_c
     grad_branch_c = (gate_c * output_gradient).astype(jnp.bfloat16)
@@ -273,49 +272,30 @@
         axis=1,
     )
     grad_mod_low = grad_mod.astype(jnp.bfloat16)
-    bias_rows = jnp.sum(grad_mod, axis=0).reshape(width, 9)
-    row_share = lax.psum_scatter(
-        jnp.concatenate(
-            [
-                contract_rows(cond_low, grad_mod_low),
-                contract_rows(normalized_first, grad_qkv_s),
-                contract_rows(merged_a, grad_branch_a),
-                contract_rows(normalized_second, grad_qkv_t),
-                contract_rows(merged_b, grad_branch_b),
-                contract_rows(normalized_third, grad_pre),
-                bias_rows,
-            ],
-            axis=1,
-        ),
-        ("wide", "narrow"),
-        scatter_dimension=0,
-        tiled=True,
-    )
-    down_share = lax.psum_scatter(
-        contract_rows(hidden, grad_branch_c), ("wide", "narrow"), scatter_dimension=0, tiled=True
-    )
-    edges = [
-        0,
-        9 * width,
-        12 * width,
-        13 * width,
-        16 * width,
-        17 * width,
-        17 * width + ff_width,
-        17 * width + ff_width + 9,
-    ]
-    pieces = [row_share[:, edges[index] : edges[index + 1]] for index in range(7)]
+    all_grad_mod = lax.all_gather(grad_mod_low, axes, axis=0, tiled=True)
+    bias_share = lax.psum_scatter(
+        jnp.sum(grad_mod, axis=0), axes, scatter_dimension=0, tiled=True
+    )
+
+    def share(left, right):
+        return lax.psum_scatter(
+            contract_rows(left, right).astype(jnp.bfloat16),
+            axes,
+            scatter_dimension=0,
+            tiled=True,
+        ).astype(jnp.float32)
+
     return (
         result.astype(jnp.bfloat16),
         residual_gradient,
-        pieces[0],
-        pieces[6].reshape(-1),
-        pieces[1],
-        pieces[2],
-        pieces[3],
-        pieces[4],
-        pieces[5],
-        down_share,
+        contract_rows(cond_rows, all_grad_mod),
+        bias_share,
+        share(normalized_first, grad_qkv_s),
+        share(merged_a, grad_branch_a),
+        share(normalized_second, grad_qkv_t),
+        share(merged_b, grad_branch_b),
+        share(normalized_third, grad_pre),
+        share(hidden, grad_branch_c),
     )
 
 

time: 1590 us -> 1330 us (0.84)
  waiting for transfers between devices: 1140 us -> 777 us
  blocking collectives: 42.7 us -> 162 us
  matrix products: 309 us -> 289 us
    unnamed x10 -> x14, waiting for transfers between devices: 715 us -> 90.8 us
    reduce_scatter x1 -> x6, waiting for transfers between devices: 133 us -> 432 us  [share(): lax.psum_scatter(contract_rows(left, right).astype(jnp.bfloat16), axes, s...]
    unnamed x1 -> x3, blocking collectives: 42.7 us -> 120 us
    all_gather x0 -> x1, blocking collectives: none -> 42.2 us  [on_device(): all_grad_mod = lax.all_gather(grad_mod_low, axes, axis=0, tiled=True)]
    all_gather x7 -> x6, waiting for transfers between devices: 289 us -> 254 us  [the longest x1 60.3 us: on_device(): lax.all_gather(w_up, axes, axis=0, tiled=True)]
  transfers between devices with their start and end apart: 9 -> 13, of which waited for: 9 -> 11; matrix products, arithmetic and copies ran while one was open for 9% -> 17% of each run, Pallas kernels for 0% -> 0%
where the time goes in v1:
time: 1330 us; the launch traced here: 1310 us
  waiting for transfers between devices  777 us (58%)
  matrix products  289 us (22%)
  blocking collectives  162 us (12%)
  local copies, waits for them, and re-layouts  43.4 us (3%)
  other arithmetic  26.4 us (2%)
  between operations  14.9 us (1%)
    reduce_scatter x6, waiting for transfers between devices, share(): lax.psum_scatter(contract_rows(left, right).astype(jnp.bfloat16), axes, s...  432 us
    unnamed x3, blocking collectives  120 us
    dot_general x78, matrix products, contract_cols(): lax.dot_general(left, right, (((1,), (1,)), ((), ())), preferred_element_...  97.1 us
    dot_general x55, matrix products, contract_rows(): lax.dot_general(left, right, (((0,), (0,)), ((), ())), preferred_element_...  93 us
    unnamed x14, waiting for transfers between devices  90.8 us
    all_gather x1, waiting for transfers between devices, on_device(): lax.all_gather(w_up, axes, axis=0, tiled=True)  60.3 us
    all_gather x1, waiting for transfers between devices, on_device(): lax.all_gather(w_down, axes, axis=0, tiled=True)  59.9 us
    all_gather x1, waiting for transfers between devices, on_device(): lax.all_gather(w_qkv_temporal, axes, axis=0, tiled=True)  57.5 us
  transfers between devices with their start and end apart: 13, of which 11 were waited for; matrix products, arithmetic and copies ran while one was open for 17% of the time, Pallas kernels for 0%

profile of v1, /device:TPU:0, one launch (start us, length us, event | category | flops | bytes accessed | tf_op | source)
XLA Modules:
  0.0 1314.6 jit_solution(7511616641751393173)
XLA Ops:
  8.1 42.0 %all-reduce = s32[64]{0:T(128)S(1)} all-reduce(s32[64]{0:T(128)S(1)} %dynamic-update-slice), channel_id=1, replica_groups=mesh['wide'=16,'narrow'=2] {'wide','narrow'}, use_global_device_ids=true, to_apply=%add | all-reduce | flops 64 | bytes 512
  57.2 40.6 %all-reduce.1 = bf16[6912]{0:T(1024)(128)(2,1)S(1)} all-reduce(bf16[6912]{0:T(1024)(128)(2,1)S(1)} %dynamic-update-slice.1), channel_id=1, replica_groups=mesh['wide'=16,'narrow'=2] {'wide','narrow'}, use_global_device_ids=true, to_apply=%add.1 | all-reduce | flops 6912 | bytes 27648
  98.3 87.0 %all-reduce.6.cloned.1.call-done = f32[64,6912]{1,0:T(8,128)} async-done(((f32[64,6912]{1,0:T(8,128)}), f32[64,6912]{1,0:T(8,128)}) %all-reduce.6.cloned.1.call-update) | async-done | bytes 1769488
  192.9 54.9 %all-gather.8.cloned.1.call-done = bf16[768,2304]{1,0:T(8,128)(2,1)} async-done(((bf16[24,2304]{1,0:T(8,128)(2,1)}), bf16[768,2304]{1,0:T(8,128)(2,1)}) %all-gather.8.cloned.1.call-update) | async-done | bytes 3538960 | tf_op jit(solution)/shard_map/all_gather | solution.py:153
  247.7 4.1 convolution_convert_fusion.5
  260.8 26.9 %while.52 = (s32[]{:T(128)}, bf16[12,256,64]{1,2,0:T(8,128)(2,1)S(1)}, bf16[12,256,64]{2,1,0:T(8,128)(2,1)}, bf16[12,256,64]{2,1,0:T(8,128)(2,1)}, bf16[12,256,6...) while((s32[]{:T(128)}, bf16[12,256,64]{1,2,0:T(8,128)(2,1)S(1)}, ...), condition=%wide.region_6.7_spmd.clone, body=%wide.region_3.6_spmd.clone.sunk | while | flops 17497600 | bytes 1059933 | solution.py:105
  287.8 15.9 %all-gather.10.cloned.1.call-done = bf16[768,768]{1,0:T(8,128)(2,1)} async-done(((bf16[24,768]{1,0:T(8,128)(2,1)}), bf16[768,768]{1,0:T(8,128)(2,1)}) %all-gather.10.cloned.1.call-update) | async-done | bytes 1179664 | tf_op jit(solution)/shard_map/all_gather | solution.py:154
  303.7 3.0 fusion.171
  308.0 57.5 %all-gather.12.cloned.1.call-done = bf16[768,2304]{1,0:T(8,128)(2,1)} async-done(((bf16[24,2304]{1,0:T(8,128)(2,1)}), bf16[768,2304]{1,0:T(8,128)(2,1)}) %all-gather.12.cloned.1.call-update) | async-done | bytes 3538960 | tf_op jit(solution)/shard_map/all_gather | solution.py:155
  365.5 4.2 convolution_convert_fusion.4
  381.7 34.2 %while.53 = (s32[]{:T(128)}, bf16[12,256,64]{1,2,0:T(8,128)(2,1)}, bf16[12,256,64]{2,1,0:T(8,128)(2,1)}, bf16[12,256,64]{2,1,0:T(8,128)(2,1)}, bf16[12,256,64]{2...) while((s32[]{:T(128)}, bf16[12,256,64]{1,2,0:T(8,128)(2,1)}, ...), condition=%wide.region_12.13_spmd.clone, body=%wide.region_9.12_spmd.clone.sunk | while | flops 17497600 | bytes 1059933 | solution.py:105
  415.8 5.4 all-gather.14.cloned.1.call-done
  421.2 3.2 fusion.170
  426.3 60.3 %all-gather.16.cloned.1.call-done = bf16[768,3072]{1,0:T(8,128)(2,1)} async-done(((bf16[24,3072]{1,0:T(8,128)(2,1)}), bf16[768,3072]{1,0:T(8,128)(2,1)}) %all-gather.16.cloned.1.call-update) | async-done | bytes 4718608 | tf_op jit(solution)/shard_map/all_gather | solution.py:157
  486.5 5.5 fusion.176
  492.1 59.9 %all-gather.18.cloned.1.call-done = bf16[3072,768]{1,0:T(8,128)(2,1)} async-done(((bf16[96,768]{1,0:T(8,128)(2,1)}), bf16[3072,768]{1,0:T(8,128)(2,1)}) %all-gather.18.cloned.1.call-update) | async-done | bytes 4718608 | tf_op jit(solution)/shard_map/all_gather | solution.py:158
  551.9 6.4 fusion.100
  562.9 3.5 fusion.169
  574.9 86.3 %while.54 = (s32[]{:T(128)}, bf16[12,256,64]{1,2,0:T(8,128)(2,1)}, bf16[12,256,64]{1,2,0:T(8,128)(2,1)}, bf16[12,256,64]{1,2,0:T(8,128)(2,1)}, bf16[12,256,64]{2...) while((s32[]{:T(128)}, bf16[12,256,64]{1,2,0:T(8,128)(2,1)}, ...), condition=%wide.region_21.22_spmd.clone, body=%wide.region_17.21_spmd.clone.sunk | while | flops 43285760 | bytes 2838645 | solution.py:119
  663.2 3.5 fusion.165
  678.9 72.0 %while.55 = (s32[]{:T(128)}, bf16[12,256,64]{1,2,0:T(8,128)(2,1)S(1)}, bf16[12,256,64]{1,2,0:T(8,128)(2,1)S(1)}, bf16[12,256,64]{1,2,0:T(8,128)(2,1)}, bf16[12,2...) while((s32[]{:T(128)}, ...), condition=%wide.region_28.29_spmd.clone, body=%wide.region_24.28_spmd.clone.sunk | while | flops 43285760 | bytes 2838645 | solution.py:119
  753.1 2.9 convolution_convert_fusion.3
  757.0 4.2 convolution_convert_fusion.2
  762.2 5.0 convolution_convert_fusion.1
  768.2 6.6 convolution_convert_fusion
  775.7 3.9 fusion.166
  784.5 42.2 %all-gather = bf16[32,2,6912]{2,1,0:T(2,128)(2,1)S(1)} all-gather(bf16[1,2,6912]{2,1,0:T(2,128)(2,1)S(1)} %convert_bitcast_fusion.6), channel_id=1, replica_groups=mesh['wide'=16,'narrow'=2] {'wide','narrow'}, dimensions={0}, use_global_device_ids=true | all-gather | bytes 912384 | tf_op jit(solution)/shard_map/all_gather | solution.py:275
  827.1 37.4 %all-reduce.3 = f32[6912]{0:T(1024)S(1)} all-reduce(f32[6912]{0:T(1024)S(1)} %fusion.156), channel_id=3, replica_groups=mesh['wide'=16,'narrow'=2] {'wide','narrow'}, use_global_device_ids=true, to_apply=%region_32.33.clone | all-reduce | flops 6912 | bytes 55296
  869.2 105.7 %reduce-scatter.7.cloned.1.call-done = bf16[24,2304]{1,0:T(8,128)(2,1)} async-done(((bf16[768,2304]{1,0:T(8,128)(2,1)}), bf16[24,2304]{1,0:T(8,128)(2,1)}) %reduce-scatter.7.cloned.1.call-update) | async-done | bytes 110608 | tf_op jit(solution)/shard_map/reduce_scatter | solution.py:281
  976.5 105.8 %reduce-scatter.11.cloned.1.call-done = bf16[24,2304]{1,0:T(8,128)(2,1)} async-done(((bf16[768,2304]{1,0:T(8,128)(2,1)}), bf16[24,2304]{1,0:T(8,128)(2,1)}) %reduce-scatter.11.cloned.1.call-update) | async-done | bytes 110608 | tf_op jit(solution)/shard_map/reduce_scatter | solution.py:281
  1083.9 109.7 %reduce-scatter.15.cloned.1.call-done = bf16[24,3072]{1,0:T(8,128)(2,1)} async-done(((bf16[768,3072]{1,0:T(8,128)(2,1)}), bf16[24,3072]{1,0:T(8,128)(2,1)}) %reduce-scatter.15.cloned.1.call-update) | async-done | bytes 147472 | tf_op jit(solution)/shard_map/reduce_scatter | solution.py:281
  1195.2 110.8 %reduce-scatter.17.cloned.1.call-done = bf16[96,768]{1,0:T(8,128)(2,1)} async-done(((bf16[3072,768]{1,0:T(8,128)(2,1)}), bf16[96,768]{1,0:T(8,128)(2,1)}) %reduce-scatter.17.cloned.1.call-update) | async-done | bytes 147472 | tf_op jit(solution)/shard_map/reduce_scatter | solution.py:281
  (448 shorter events, 307.7 us)
Async XLA Ops:
  7.2 44.1 %copy-start = (bf16[24,6912]{1,0:T(8,128)(2,1)S(1)}, bf16[24,6912]{1,0:T(8,128)(2,1)}, u32[]{:S(2)}) copy-start(bf16[24,6912]{1,0:T(8,128)(2,1)} %param.27) | copy-start | bytes 995332
  7.2 178.1 %all-reduce.6.cloned.1.call-start = ((), (), s32[]{:S(2)}) async-start(), calls=%async_computation.18 | async-start | bytes 3538944
  50.6 6.4 copy-start.45
  51.2 46.6 %copy-start.4 = (bf16[256,768]{1,0:T(8,128)(2,1)S(1)}, bf16[256,768]{1,0:T(8,128)(2,1)}, u32[]{:S(2)}) copy-start(bf16[256,768]{1,0:T(8,128)(2,1)} %param.22) | copy-start | bytes 1179652
  51.2 135.0 %copy-start.38 = (s32[256]{0:T(256)S(1)}, s32[256]{0:T(256)}, u32[]{:S(2)}) copy-start(s32[256]{0:T(256)} %param.23) | copy-start | bytes 3076
  52.9 194.8 %all-gather.8.cloned.1.call-start = ((), (), s32[]{:S(2)}) async-start(), calls=%async_computation.6 | async-start | bytes 3649536 | tf_op jit(solution)/shard_map/all_gather | solution.py:153
  53.7 250.0 %all-gather.10.cloned.1.call-start = ((), (), s32[]{:S(2)}) async-start(), calls=%async_computation.7 | async-start | bytes 1216512 | tf_op jit(solution)/shard_map/all_gather | solution.py:154
  54.4 311.0 %all-gather.12.cloned.1.call-start = ((), (), s32[]{:S(2)}) async-start(), calls=%async_computation.8 | async-start | bytes 3649536 | tf_op jit(solution)/shard_map/all_gather | solution.py:155
  55.0 366.2 %all-gather.14.cloned.1.call-start = ((), (), s32[]{:S(2)}) async-start(), calls=%async_computation.9 | async-start | bytes 1216512 | tf_op jit(solution)/shard_map/all_gather | solution.py:156
  55.6 431.0 %all-gather.16.cloned.1.call-start = ((), (), s32[]{:S(2)}) async-start(), calls=%async_computation.10 | async-start | bytes 4866048 | tf_op jit(solution)/shard_map/all_gather | solution.py:157
  56.2 495.8 %all-gather.18.cloned.1.call-start = ((), (), s32[]{:S(2)}) async-start(), calls=%async_computation.11 | async-start | bytes 4866048 | tf_op jit(solution)/shard_map/all_gather | solution.py:158
  56.9 809.5 %reduce-scatter.9.cloned.1.call-start = ((), (), s32[]{:S(2)}) async-start(), calls=%async_computation.13 | async-start | bytes 1216512 | tf_op jit(solution)/shard_map/reduce_scatter | solution.py:281
  192.9 59.0 %copy-start.25 = (bf16[256,768]{1,0:T(8,128)(2,1)}, bf16[256,768]{1,0:T(8,128)(2,1)S(1)}, u32[]{:S(2)}) copy-start(bf16[256,768]{1,0:T(8,128)(2,1)S(1)} %fusion.126) | copy-start | bytes 1179652
  256.3 4.5 copy-start.44
  287.7 15.9 %copy-start.15 = (bf16[12,256,64]{1,2,0:T(8,128)(2,1)}, bf16[12,256,64]{1,2,0:T(8,128)(2,1)S(1)}, u32[]{:S(2)}) copy-start(bf16[12,256,64]{1,2,0:T(8,128)(2,1)S(1)} %get-tuple-element.172) | copy-start | bytes 1179652
  374.4 7.3 copy-start.43
  551.9 6.4 copy-start.7
  551.9 6.4 copy-start.11
  551.9 6.4 copy-start.40
  558.4 4.5 copy-start.46
  560.1 6.3 copy-start.47
  562.9 6.5 copy-start.12
  671.6 4.9 copy-start.17
  671.6 4.9 copy-start.19
  671.6 196.2 %reduce-scatter.13.cloned.1.call-start = ((), (), s32[]{:S(2)}) async-start(), calls=%async_computation.15 | async-start | bytes 1216512 | tf_op jit(solution)/shard_map/reduce_scatter | solution.py:281
  678.0 296.9 %reduce-scatter.7.cloned.1.call-start = ((), (), s32[]{:S(2)}) async-start(), calls=%async_computation.12 | async-start | bytes 3649536 | tf_op jit(solution)/shard_map/reduce_scatter | solution.py:281
  756.0 326.2 %reduce-scatter.11.cloned.1.call-start = ((), (), s32[]{:S(2)}) async-start(), calls=%async_computation.14 | async-start | bytes 3649536 | tf_op jit(solution)/shard_map/reduce_scatter | solution.py:281
  761.2 432.4 %reduce-scatter.15.cloned.1.call-start = ((), (), s32[]{:S(2)}) async-start(), calls=%async_computation.16 | async-start | bytes 4866048 | tf_op jit(solution)/shard_map/reduce_scatter | solution.py:281
  767.2 538.9 %reduce-scatter.17.cloned.1.call-start = ((), (), s32[]{:S(2)}) async-start(), calls=%async_computation.17 | async-start | bytes 4866048 | tf_op jit(solution)/shard_map/reduce_scatter | solution.py:281
  783.5 81.7 %copy-start.30 = (f32[64,384]{1,0:T(8,128)S(1)}, f32[64,384]{1,0:T(8,128)}, u32[]{:S(2)}) copy-start(f32[64,384]{1,0:T(8,128)} %copy-done.29) | copy-start | bytes 294916
  783.5 81.7 %copy-start.32 = (f32[64,384]{1,0:T(8,128)S(1)}, f32[64,384]{1,0:T(8,128)}, u32[]{:S(2)}) copy-start(f32[64,384]{1,0:T(8,128)} %copy-done.31) | copy-start | bytes 294916
  784.5 523.2 %copy-start.1 = (bf16[24,6912]{1,0:T(8,128)(2,1)S(1)}, bf16[24,6912]{1,0:T(8,128)(2,1)}, u32[]{:S(2)}) copy-start(bf16[24,6912]{1,0:T(8,128)(2,1)} %param.27) | copy-start | bytes 995332
  (33 other events, 68.1 us)
Sparse Core Ops, SparseCore 0:
  53.0 132.2 all-reduce.5
  188.2 59.4 all-gather.7
  250.6 53.0 all-gather.9
  306.4 58.9 all-gather.11
  368.2 52.9 all-gather.13
  423.9 62.5 all-gather.15
  489.4 62.4 all-gather.17
  671.7 95.1 reduce-scatter.8
  772.0 95.3 reduce-scatter.12
  872.7 102.1 reduce-scatter.6
  980.3 101.9 reduce-scatter.10
  1087.6 105.9 reduce-scatter.14
  1200.0 106.0 reduce-scatter.16

commit v2 on v1

--- a/solution.py
+++ b/solution.py
@@ -4,6 +4,8 @@
 import jax
 import jax.numpy as jnp
 from jax import lax
+from jax.experimental import pallas as pl
+from jax.experimental.pallas import tpu as pltpu
 from jax.sharding import PartitionSpec as P
 
 HEADS = 12
@@ -128,6 +130,255 @@
     )
     normalized_gradient = contract_cols(grad_qkv, w_qkv)
     return (normalized_gradient, grad_qkv)
+
+
+MESH = pl.DeviceIdType.MESH
+
+
+class Spot:
+    def __init__(self):
+        chip = lax.axis_index("wide")
+        core = lax.axis_index("narrow")
+        z, y, x = lax.div(chip, 4), lax.rem(lax.div(chip, 2), 2), lax.rem(chip, 2)
+        half = lax.div(z, 2)
+        toward = 1 - 2 * half
+        self.chip, self.core, self.z, self.y, self.x = chip, core, z, y, x
+        self.half = half
+        self.middle = z + half * (3 - 2 * z)
+        self.is_middle = self.middle == 1
+        self.is_end = self.middle == 0
+        self.plane = 2 * y + x
+        self.inner = ((z + toward) * 4 + self.plane, core)
+        self.outer = ((z - toward) * 4 + self.plane, core)
+        self.first_plane = 2 * lax.rem(y + core, 2) + lax.rem(x + 1 - core, 2)
+        self.second_plane = 2 * lax.rem(y + 1 - core, 2) + lax.rem(x + core, 2)
+        self.far_plane = 3 - self.plane
+        self.first = (z * 4 + self.first_plane, core)
+        self.second = (z * 4 + self.second_plane, core)
+        self.twin = (chip, 1 - core)
+
+    def layer(self, mirrored):
+        return mirrored + self.half * (3 - 2 * mirrored)
+
+    def arrival(self, k):
+        return (self.z, self.layer(1 - self.middle), self.layer(2), self.layer(3))[k]
+
+
+def greet(spot):
+    barrier = pltpu.get_barrier_semaphore()
+    for device in (spot.twin, spot.inner, spot.first, spot.second):
+        pl.semaphore_signal(barrier, inc=1, device_id=device, device_id_type=MESH)
+
+    @pl.when(spot.is_middle)
+    def _():
+        pl.semaphore_signal(barrier, inc=1, device_id=spot.outer, device_id_type=MESH)
+        pl.semaphore_wait(barrier, 5)
+
+    @pl.when(spot.is_end)
+    def _():
+        pl.semaphore_wait(barrier, 4)
+
+
+class Gather:
+    def __init__(self, spot, shard, held, stage, apart, stage_sems, send, recv):
+        self.spot, self.shard, self.held = spot, shard, held
+        self.stage, self.apart, self.stage_sems = stage, apart, stage_sems
+        self.send, self.recv = send, recv
+        self.rows = held.shape[1] // 16
+        self.width = held.shape[2]
+
+    def block(self, z, plane):
+        start = pl.multiple_of((z * 4 + plane) * self.rows, 16)
+        return self.held.at[self.spot.core, pl.ds(start, self.rows), :]
+
+    def layer_rows(self, half, z):
+        start = pl.multiple_of(z * 4 * self.rows, 16)
+        return self.held.at[half, pl.ds(start, 4 * self.rows), :]
+
+    def copy(self, ref, send, recv, device):
+        return pltpu.make_async_remote_copy(
+            src_ref=ref,
+            dst_ref=ref,
+            send_sem=self.send.at[send],
+            recv_sem=self.recv.at[recv],
+            device_id=device,
+            device_id_type=MESH,
+        )
+
+    def swap(self):
+        rows = self.rows // 2
+        core = self.spot.core
+        start = pl.multiple_of(core * rows, 8)
+        return pltpu.make_async_remote_copy(
+            src_ref=self.apart,
+            dst_ref=self.stage.at[pl.ds(start, rows), :],
+            send_sem=self.stage_sems.at[0],
+            recv_sem=self.stage_sems.at[1],
+            device_id=self.spot.twin,
+            device_id_type=MESH,
+        )
+
+    def open(self):
+        rows, core = self.rows // 2, self.spot.core
+        theirs = pl.multiple_of((1 - core) * self.width, 128)
+        ours = pl.multiple_of(core * self.width, 128)
+        self.apart[...] = self.shard[:, pl.ds(theirs, self.width)].astype(jnp.float32)
+        self.swap().start()
+        self.stage[pl.ds(pl.multiple_of(core * rows, 8), rows), :] = self.shard[
+            :, pl.ds(ours, self.width)
+        ].astype(jnp.float32)
+
+    def own(self):
+        self.swap().wait_recv()
+        start = pl.multiple_of(self.spot.chip * self.rows, 16)
+        self.held[self.spot.core, pl.ds(start, self.rows), :] = self.stage[...].astype(jnp.bfloat16)
+        self.z_own(True).start()
+        pl.when(self.spot.is_middle)(lambda: self.z_own(False).start())
+        self.first_copy(0).start()
+        self.second_copy(0).start()
+
+    def z_own(self, inward):
+        spot = self.spot
+        return self.copy(
+            self.block(spot.z, spot.plane),
+            0 if inward else 1,
+            spot.z,
+            spot.inner if inward else spot.outer,
+        )
+
+    def z_pass(self, k):
+        spot = self.spot
+        z = spot.arrival(k)
+        return self.copy(
+            self.block(z, spot.plane), 1 + k, z, spot.inner if k == 1 else spot.outer
+        )
+
+    def first_copy(self, k):
+        z = self.spot.arrival(k)
+        return self.copy(self.block(z, self.spot.plane), 5 + k, 4 + z, self.spot.first)
+
+    def second_copy(self, k):
+        z = self.spot.arrival(k)
+        return self.copy(self.block(z, self.spot.plane), 9 + k, 8 + z, self.spot.second)
+
+    def second_pass(self, k):
+        z = self.spot.arrival(k)
+        return self.copy(self.block(z, self.spot.first_plane), 13 + k, 12 + z, self.spot.second)
+
+    def twin_copy(self, k):
+        z = self.spot.arrival(k)
+        return self.copy(self.layer_rows(self.spot.core, z), 17 + k, 16 + z, self.spot.twin)
+
+    def along_z(self, k):
+        spot = self.spot
+        z = spot.arrival(k)
+        self.copy(self.block(z, spot.plane), 0, z, spot.inner).wait_recv()
+        pl.when(spot.is_middle)(lambda: self.z_pass(k).start())
+        self.first_copy(k).start()
+        self.second_copy(k).start()
+
+    def along_first(self, k):
+        spot = self.spot
+        z = spot.arrival(k)
+        self.copy(self.block(z, spot.first_plane), 0, 4 + z, spot.first).wait_recv()
+        self.second_pass(k).start()
+
+    def along_second(self, k):
+        spot = self.spot
+        z = spot.arrival(k)
+        self.copy(self.block(z, spot.second_plane), 0, 8 + z, spot.second).wait_recv()
+        self.copy(self.block(z, spot.far_plane), 0, 12 + z, spot.second).wait_recv()
+        self.twin_copy(k).start()
+
+    def from_twin(self, k):
+        z = self.spot.arrival(k)
+        self.copy(self.layer_rows(1 - self.spot.core, z), 0, 16 + z, self.spot.twin).wait_recv()
+
+    def events(self):
+        return [
+            (0.0, self.own),
+            (2.5, lambda: self.along_first(0)),
+            (2.6, lambda: self.along_z(1)),
+            (4.0, lambda: self.along_z(2)),
+            (5.0, lambda: self.along_first(1)),
+            (5.5, lambda: self.along_z(3)),
+            (6.0, lambda: self.along_second(0)),
+            (7.0, lambda: self.along_first(2)),
+            (8.0, lambda: self.along_second(1)),
+            (9.0, lambda: self.along_first(3)),
+            (10.5, lambda: self.along_second(2)),
+            (13.0, lambda: self.along_second(3)),
+        ]
+
+    def landed(self):
+        for k in range(4):
+            self.from_twin(k)
+
+    def drain(self):
+        spot = self.spot
+        self.swap().wait_send()
+        self.z_own(True).wait_send()
+
+        @pl.when(spot.is_middle)
+        def _():
+            self.z_own(False).wait_send()
+            for k in (1, 2, 3):
+                self.z_pass(k).wait_send()
+
+        for k in range(4):
+            self.first_copy(k).wait_send()
+            self.second_copy(k).wait_send()
+            self.second_pass(k).wait_send()
+            self.twin_copy(k).wait_send()
+
+
+def gather_kernel(*refs):
+    shards, held = refs[:6], refs[6:12]
+    stage, apart = refs[12:18], refs[18:24]
+    stage_sems, send, recv = refs[24:]
+    spot = Spot()
+    gathers = [
+        Gather(spot, shards[i], held[i], stage[i], apart[i], stage_sems.at[i], send.at[i], recv.at[i])
+        for i in range(6)
+    ]
+    greet(spot)
+    events = []
+    start = 0.0
+    for i, gather in enumerate(gathers):
+        unit = gather.rows * gather.width / (48 * 1152)
+        for place, (at, action) in enumerate(gather.events()):
+            when = start + at * unit if place else start - 10
+            events.append((when, i, place, action))
+        start += 12 * unit
+    events.sort(key=lambda e: e[:3])
+    for gather in gathers:
+        gather.open()
+    for _, _, _, action in events:
+        action()
+    for gather in gathers:
+        gather.landed()
+    for gather in gathers:
+        gather.drain()
+
+
+def gather_weights(shards):
+    dims = [(16 * 2 * s.shape[0], s.shape[1] // 2) for s in shards]
+    return pl.pallas_call(
+        gather_kernel,
+        out_shape=[jax.ShapeDtypeStruct((2, r, n), jnp.bfloat16) for r, n in dims],
+        in_specs=[pl.BlockSpec(memory_space=pltpu.VMEM)] * 6,
+        out_specs=[pl.BlockSpec(memory_space=pltpu.VMEM)] * 6,
+        scratch_shapes=[pltpu.VMEM((r // 16, n), jnp.float32) for r, n in dims]
+        + [pltpu.VMEM((r // 32, n), jnp.float32) for r, n in dims]
+        + [
+            pltpu.SemaphoreType.DMA((6, 2)),
+            pltpu.SemaphoreType.DMA((6, 21)),
+            pltpu.SemaphoreType.DMA((6, 20)),
+        ],
+        compiler_params=pltpu.CompilerParams(
+            collective_id=0, has_side_effects=True, vmem_limit_bytes=60 * 2**20
+        ),
+    )(*shards)
 
 
 def on_device(
@@ -145,18 +396,17 @@
     w_up,
     w_down,
     cotangent,
+    on_grid,
 ):
     axes = ("wide", "narrow")
-    gathered = (
-        None,
-        None,
-        lax.all_gather(w_qkv_spatial, axes, axis=0, tiled=True),
-        lax.all_gather(w_out_spatial, axes, axis=0, tiled=True),
-        lax.all_gather(w_qkv_temporal, axes, axis=0, tiled=True),
-        lax.all_gather(w_out_temporal, axes, axis=0, tiled=True),
-        lax.all_gather(w_up, axes, axis=0, tiled=True),
-        lax.all_gather(w_down, axes, axis=0, tiled=True),
-    )
+    shards = (w_qkv_spatial, w_out_spatial, w_qkv_temporal, w_out_temporal, w_up, w_down)
+    if on_grid:
+        halves = gather_weights(shards)
+        gathered = (None, None) + tuple(jnp.concatenate([h[0], h[1]], axis=1) for h in halves)
+    else:
+        gathered = (None, None) + tuple(
+            lax.all_gather(s, axes, axis=0, tiled=True) for s in shards
+        )
     width = tokens.shape[1]
     head_count = HEADS
     clip_count = timesteps.shape[0]
@@ -316,8 +566,9 @@
         P(("wide", "narrow"), None),
         P(("wide", "narrow"), None),
     )
+    on_grid = dict(mesh.shape) == {"wide": 16, "narrow": 2}
     return jax.shard_map(
-        on_device,
+        partial(on_device, on_grid=on_grid),
         mesh=mesh,
         in_specs=placed,
         out_specs=(

time: 1330 us -> 1100 us (0.83)
  waiting for transfers between devices: 777 us -> 433 us
  Pallas kernels: 0 us -> 114 us
  local copies, waits for them, and re-layouts: 43.4 us -> 61.4 us
    all_gather x6 -> x0, waiting for transfers between devices: 254 us -> none  [the longest x1 60.3 us: on_device(): lax.all_gather(w_up, axes, axis=0, tiled=True)]
    pallas_call x0 -> x1, Pallas kernels: none -> 114 us  [gather_weights(): pl.pallas_call(gather_kernel, out_shape=[jax.ShapeDtypeStruct((2, r, n),...]
    unnamed x14 -> x8, waiting for transfers between devices: 90.8 us -> 0.12 us
    squeeze x0 -> x4, local copies, waits for them, and re-layouts: none -> 14.9 us  [on_device(): h[0]]
    unnamed x116 -> x134, local copies, waits for them, and re-layouts: 26.4 us -> 29.6 us
  transfers between devices with their start and end apart: 13 -> 7, of which waited for: 11 -> 5; matrix products, arithmetic and copies ran while one was open for 17% -> 12% of each run, Pallas kernels for 0% -> 11%
where the time goes in v2:
time: 1100 us; the launch traced here: 1090 us
  waiting for transfers between devices  433 us (39%)
  matrix products  277 us (25%)
  blocking collectives  161 us (15%)
  Pallas kernels  114 us (10%)
  local copies, waits for them, and re-layouts  61.4 us (6%)
  other arithmetic  24.8 us (2%)
  between operations  15.2 us (1%)
    reduce_scatter x6, waiting for transfers between devices, share(): lax.psum_scatter(contract_rows(left, right).astype(jnp.bfloat16), axes, s...  433 us
    unnamed x3, blocking collectives  117 us
    pallas_call x1, Pallas kernels, gather_weights(): pl.pallas_call(gather_kernel, out_shape=[jax.ShapeDtypeStruct((2, r, n),...  114 us
    dot_general x78, matrix products, contract_cols(): lax.dot_general(left, right, (((1,), (1,)), ((), ())), preferred_element_...  94.1 us
    dot_general x55, matrix products, contract_rows(): lax.dot_general(left, right, (((0,), (0,)), ((), ())), preferred_element_...  92.9 us
    all_gather x1, blocking collectives, on_device(): all_grad_mod = lax.all_gather(grad_mod_low, axes, axis=0, tiled=True)  43.7 us
    dot_general x24, matrix products, head_backward(): jnp.dot(score_low, key_vecs, preferred_element_type=jnp.float32) * scale  32.6 us
    dot_general x24, matrix products, head_forward(): jnp.dot(attn_prob.astype(jnp.bfloat16), val_vecs, preferred_element_type=...  32.2 us
  transfers between devices with their start and end apart: 7, of which 5 were waited for; matrix products, arithmetic and copies ran while one was open for 12% of the time, Pallas kernels for 11%

profile of v2, /device:TPU:0, one launch (start us, length us, event | category | flops | bytes accessed | tf_op | source)
XLA Modules:
  0.0 1088.3 jit_solution(11262678187034344792)
XLA Ops:
  8.2 42.0 %all-reduce = s32[64]{0:T(128)S(1)} all-reduce(s32[64]{0:T(128)S(1)} %dynamic-update-slice), channel_id=1, replica_groups=mesh['wide'=16,'narrow'=2] {'wide','narrow'}, use_global_device_ids=true, to_apply=%add | all-reduce | flops 64 | bytes 512
  53.5 114.4 %shard_map.213 = (bf16[2,768,1152]{2,1,0:T(8,128)(2,1)}, bf16[2,768,384]{2,1,0:T(8,128)(2,1)}, bf16[2,768,1152]{2,1,0:T(8,128)(2,1)}, bf16[2,768,384]{2,1,0:T(8,...) custom-call(bf16[24,2304]{1,0:T(8,128)(2,1)} %refs_0_.1, bf16[24,768]{1,0:T(8,128)(2,1)} %refs_1_.1, ...), custom_call_target="tpu_custom_call" | custom-call | tf_op jit(solution)/shard_map/pallas_call | solution.py:366
  167.9 5.2 slice_bitcast_fusion.3
  174.1 3.2 slice_bitcast_fusion.5
  178.9 37.7 %all-reduce.1 = bf16[6912]{0:T(1024)(128)(2,1)S(1)} all-reduce(bf16[6912]{0:T(1024)(128)(2,1)S(1)} %dynamic-update-slice.1), channel_id=1, replica_groups=mesh['wide'=16,'narrow'=2] {'wide','narrow'}, use_global_device_ids=true, to_apply=%add.1 | all-reduce | flops 6912 | bytes 27648
  216.7 5.0 slice_bitcast_fusion.1
  223.8 2.5 fusion.149
  226.4 2.5 fusion.148
  232.1 2.4 copy.46
  241.1 26.9 %while.52 = (s32[]{:T(128)}, bf16[12,256,64]{1,2,0:T(8,128)(2,1)S(1)}, bf16[12,256,64]{2,1,0:T(8,128)(2,1)}, bf16[12,256,64]{2,1,0:T(8,128)(2,1)}, bf16[12,256,6...) while((s32[]{:T(128)}, bf16[12,256,64]{1,2,0:T(8,128)(2,1)S(1)}, ...), condition=%wide.region_6.7_spmd.clone, body=%wide.region_3.6_spmd.clone.sunk | while | flops 17497600 | bytes 1059933 | solution.py:107
  268.7 3.0 fusion.187
  276.1 2.4 copy.50
  278.4 2.3 slice_bitcast_fusion.12
  288.0 33.9 %while.53 = (s32[]{:T(128)}, bf16[12,256,64]{1,2,0:T(8,128)(2,1)}, bf16[12,256,64]{2,1,0:T(8,128)(2,1)}, bf16[12,256,64]{2,1,0:T(8,128)(2,1)}, bf16[12,256,64]{2...) while((s32[]{:T(128)}, bf16[12,256,64]{1,2,0:T(8,128)(2,1)}, ...), condition=%wide.region_12.13_spmd.clone, body=%wide.region_9.12_spmd.clone.sunk | while | flops 17497600 | bytes 1059933 | solution.py:107
  321.9 2.4 fusion.186
  328.9 3.4 fusion.100
  334.0 3.7 fusion.185
  346.2 86.2 %while.54 = (s32[]{:T(128)}, bf16[12,256,64]{1,2,0:T(8,128)(2,1)}, bf16[12,256,64]{1,2,0:T(8,128)(2,1)}, bf16[12,256,64]{1,2,0:T(8,128)(2,1)}, bf16[12,256,64]{2...) while((s32[]{:T(128)}, bf16[12,256,64]{1,2,0:T(8,128)(2,1)}, ...), condition=%wide.region_21.22_spmd.clone, body=%wide.region_17.21_spmd.clone.sunk | while | flops 43285760 | bytes 2838645 | solution.py:121
  434.4 3.5 fusion.182
  442.8 2.7 convolution_convert_fusion.8
  449.8 72.0 %while.55 = (s32[]{:T(128)}, bf16[12,256,64]{1,2,0:T(8,128)(2,1)S(1)}, bf16[12,256,64]{1,2,0:T(8,128)(2,1)S(1)}, bf16[12,256,64]{1,2,0:T(8,128)(2,1)}, bf16[12,2...) while((s32[]{:T(128)}, ...), condition=%wide.region_28.29_spmd.clone, body=%wide.region_24.28_spmd.clone.sunk | while | flops 43285760 | bytes 2838645 | solution.py:121
  524.0 2.9 convolution_convert_fusion.3
  528.0 4.2 convolution_convert_fusion.2
  533.1 5.0 convolution_convert_fusion.1
  539.1 6.6 convolution_convert_fusion
  546.7 3.9 fusion.183
  555.4 43.7 %all-gather = bf16[32,2,6912]{2,1,0:T(2,128)(2,1)S(1)} all-gather(bf16[1,2,6912]{2,1,0:T(2,128)(2,1)S(1)} %convert_bitcast_fusion.6), channel_id=1, replica_groups=mesh['wide'=16,'narrow'=2] {'wide','narrow'}, dimensions={0}, use_global_device_ids=true | all-gather | bytes 912384 | tf_op jit(solution)/shard_map/all_gather | solution.py:525
  599.5 37.3 %all-reduce.3 = f32[6912]{0:T(1024)S(1)} all-reduce(f32[6912]{0:T(1024)S(1)} %fusion.176), channel_id=3, replica_groups=mesh['wide'=16,'narrow'=2] {'wide','narrow'}, use_global_device_ids=true, to_apply=%region_32.33.clone | all-reduce | flops 6912 | bytes 55296
  642.2 106.1 %reduce-scatter.7.cloned.1.call-done = bf16[24,2304]{1,0:T(8,128)(2,1)} async-done(((bf16[768,2304]{1,0:T(8,128)(2,1)}), bf16[24,2304]{1,0:T(8,128)(2,1)}) %reduce-scatter.7.cloned.1.call-update) | async-done | bytes 110608 | tf_op jit(solution)/shard_map/reduce_scatter | solution.py:531
  749.9 105.8 %reduce-scatter.11.cloned.1.call-done = bf16[24,2304]{1,0:T(8,128)(2,1)} async-done(((bf16[768,2304]{1,0:T(8,128)(2,1)}), bf16[24,2304]{1,0:T(8,128)(2,1)}) %reduce-scatter.11.cloned.1.call-update) | async-done | bytes 110608 | tf_op jit(solution)/shard_map/reduce_scatter | solution.py:531
  857.3 109.6 %reduce-scatter.15.cloned.1.call-done = bf16[24,3072]{1,0:T(8,128)(2,1)} async-done(((bf16[768,3072]{1,0:T(8,128)(2,1)}), bf16[24,3072]{1,0:T(8,128)(2,1)}) %reduce-scatter.15.cloned.1.call-update) | async-done | bytes 147472 | tf_op jit(solution)/shard_map/reduce_scatter | solution.py:531
  968.6 110.8 %reduce-scatter.17.cloned.1.call-done = bf16[96,768]{1,0:T(8,128)(2,1)} async-done(((bf16[3072,768]{1,0:T(8,128)(2,1)}), bf16[96,768]{1,0:T(8,128)(2,1)}) %reduce-scatter.17.cloned.1.call-update) | async-done | bytes 147472 | tf_op jit(solution)/shard_map/reduce_scatter | solution.py:531
  (454 shorter events, 298.2 us)
Async XLA Ops:
  7.2 44.1 %copy-start = (bf16[24,6912]{1,0:T(8,128)(2,1)S(1)}, bf16[24,6912]{1,0:T(8,128)(2,1)}, u32[]{:S(2)}) copy-start(bf16[24,6912]{1,0:T(8,128)(2,1)} %param.27) | copy-start | bytes 995332
  7.2 45.9 %copy-start.4 = (bf16[256,768]{1,0:T(8,128)(2,1)S(1)}, bf16[256,768]{1,0:T(8,128)(2,1)}, u32[]{:S(2)}) copy-start(bf16[256,768]{1,0:T(8,128)(2,1)} %param.22) | copy-start | bytes 1179652
  7.2 214.5 %all-reduce.6.cloned.1.call-start = ((), (), s32[]{:S(2)}) async-start(), calls=%async_computation.12 | async-start | bytes 3538944
  53.0 585.7 %reduce-scatter.9.cloned.1.call-start = ((), (), s32[]{:S(2)}) async-start(), calls=%async_computation.7 | async-start | bytes 1216512 | tf_op jit(solution)/shard_map/reduce_scatter | solution.py:531
  167.9 5.2 copy-start.11
  167.9 6.2 copy-start.12
  216.7 6.0 copy-start.49
  226.4 3.6 copy-start.31
  226.4 3.6 copy-start.32
  236.5 4.6 copy-start.53
  268.7 3.3 copy-start.2
  280.7 7.3 copy-start.52
  327.6 6.4 copy-start.60
  334.0 3.8 copy-start.55
  334.0 6.6 copy-start.23
  334.0 6.6 copy-start.24
  433.9 4.0 copy-start.9
  434.4 3.5 copy-start.16
  434.4 3.6 copy-start.18
  442.7 4.7 copy-start.15
  442.7 4.7 copy-start.37
  442.7 198.1 %reduce-scatter.13.cloned.1.call-start = ((), (), s32[]{:S(2)}) async-start(), calls=%async_computation.9 | async-start | bytes 1216512 | tf_op jit(solution)/shard_map/reduce_scatter | solution.py:531
  448.9 299.4 %reduce-scatter.7.cloned.1.call-start = ((), (), s32[]{:S(2)}) async-start(), calls=%async_computation.6 | async-start | bytes 3649536 | tf_op jit(solution)/shard_map/reduce_scatter | solution.py:531
  527.0 328.7 %reduce-scatter.11.cloned.1.call-start = ((), (), s32[]{:S(2)}) async-start(), calls=%async_computation.8 | async-start | bytes 3649536 | tf_op jit(solution)/shard_map/reduce_scatter | solution.py:531
  532.2 434.8 %reduce-scatter.15.cloned.1.call-start = ((), (), s32[]{:S(2)}) async-start(), calls=%async_computation.10 | async-start | bytes 4866048 | tf_op jit(solution)/shard_map/reduce_scatter | solution.py:531
  538.1 541.3 %reduce-scatter.17.cloned.1.call-start = ((), (), s32[]{:S(2)}) async-start(), calls=%async_computation.11 | async-start | bytes 4866048 | tf_op jit(solution)/shard_map/reduce_scatter | solution.py:531
  546.7 3.9 copy-start.56
  546.7 3.9 copy-start.58
  546.7 3.9 copy-start.59
  554.4 83.1 %copy-start.42 = (f32[64,384]{1,0:T(8,128)S(1)}, f32[64,384]{1,0:T(8,128)}, u32[]{:S(2)}) copy-start(f32[64,384]{1,0:T(8,128)} %copy-done.41) | copy-start | bytes 294916
  554.4 83.1 %copy-start.44 = (f32[64,384]{1,0:T(8,128)S(1)}, f32[64,384]{1,0:T(8,128)}, u32[]{:S(2)}) copy-start(f32[64,384]{1,0:T(8,128)} %copy-done.43) | copy-start | bytes 294916
  555.4 525.7 %copy-start.1 = (bf16[24,6912]{1,0:T(8,128)(2,1)S(1)}, bf16[24,6912]{1,0:T(8,128)(2,1)}, u32[]{:S(2)}) copy-start(bf16[24,6912]{1,0:T(8,128)(2,1)} %param.27) | copy-start | bytes 995332
  (36 other events, 59.2 us)
Sparse Core Ops, SparseCore 0:
  53.2 134.2 all-reduce.5
  442.8 97.3 reduce-scatter.8
  545.4 95.4 reduce-scatter.12
  646.1 102.1 reduce-scatter.6
  753.6 102.0 reduce-scatter.10
  861.0 105.8 reduce-scatter.14
  973.3 106.0 reduce-scatter.16

commit v3 on v2

--- a/solution.py
+++ b/solution.py
@@ -179,61 +179,59 @@
         pl.semaphore_wait(barrier, 4)
 
 
+def remote(src, dst, send, recv, device):
+    return pltpu.make_async_remote_copy(
+        src_ref=src,
+        dst_ref=dst,
+        send_sem=send,
+        recv_sem=recv,
+        device_id=device,
+        device_id_type=MESH,
+    )
+
+
 class Gather:
-    def __init__(self, spot, shard, held, stage, apart, stage_sems, send, recv):
-        self.spot, self.shard, self.held = spot, shard, held
-        self.stage, self.apart, self.stage_sems = stage, apart, stage_sems
+    def __init__(self, spot, held, stage, apart, swap_sems, send, recv):
+        self.spot, self.held = spot, held
+        self.stage, self.apart, self.swap_sems = stage, apart, swap_sems
         self.send, self.recv = send, recv
-        self.rows = held.shape[1] // 16
-        self.width = held.shape[2]
+        self.whole = apart.shape[1] == 48
 
     def block(self, z, plane):
-        start = pl.multiple_of((z * 4 + plane) * self.rows, 16)
-        return self.held.at[self.spot.core, pl.ds(start, self.rows), :]
-
-    def layer_rows(self, half, z):
-        start = pl.multiple_of(z * 4 * self.rows, 16)
-        return self.held.at[half, pl.ds(start, 4 * self.rows), :]
+        return self.held.at[self.spot.core, z * 4 + plane]
+
+    def layer_blocks(self, half, z):
+        return self.held.at[half, pl.ds(z * 4, 4)]
 
     def copy(self, ref, send, recv, device):
-        return pltpu.make_async_remote_copy(
-            src_ref=ref,
-            dst_ref=ref,
-            send_sem=self.send.at[send],
-            recv_sem=self.recv.at[recv],
-            device_id=device,
-            device_id_type=MESH,
+        return remote(ref, ref, self.send.at[send], self.recv.at[recv], device)
+
+    def mine(self):
+        core = self.spot.core
+        if self.whole:
+            return self.stage.at[pl.ds(2 * core, 2)]
+        return self.stage.at[:, pl.ds(pl.multiple_of(core * 24, 8), 24), :]
+
+    def swap(self):
+        return remote(
+            self.apart, self.mine(), self.swap_sems.at[0], self.swap_sems.at[1], self.spot.twin
         )
 
-    def swap(self):
-        rows = self.rows // 2
+    def open(self, piece):
         core = self.spot.core
-        start = pl.multiple_of(core * rows, 8)
-        return pltpu.make_async_remote_copy(
-            src_ref=self.apart,
-            dst_ref=self.stage.at[pl.ds(start, rows), :],
-            send_sem=self.stage_sems.at[0],
-            recv_sem=self.stage_sems.at[1],
-            device_id=self.spot.twin,
-            device_id_type=MESH,
-        )
-
-    def open(self):
-        rows, core = self.rows // 2, self.spot.core
-        theirs = pl.multiple_of((1 - core) * self.width, 128)
-        ours = pl.multiple_of(core * self.width, 128)
-        self.apart[...] = self.shard[:, pl.ds(theirs, self.width)].astype(jnp.float32)
+        for chunk in range(self.apart.shape[0]):
+            self.apart[chunk] = piece(1 - core, chunk).astype(jnp.float32)
         self.swap().start()
-        self.stage[pl.ds(pl.multiple_of(core * rows, 8), rows), :] = self.shard[
-            :, pl.ds(ours, self.width)
-        ].astype(jnp.float32)
+        place = self.mine()
+        for chunk in range(self.apart.shape[0]):
+            place[chunk] = piece(core, chunk).astype(jnp.float32)
 
     def own(self):
+        spot = self.spot
         self.swap().wait_recv()
-        start = pl.multiple_of(self.spot.chip * self.rows, 16)
-        self.held[self.spot.core, pl.ds(start, self.rows), :] = self.stage[...].astype(jnp.bfloat16)
+        self.held[spot.core, spot.chip] = self.stage[...].astype(jnp.bfloat16)
         self.z_own(True).start()
-        pl.when(self.spot.is_middle)(lambda: self.z_own(False).start())
+        pl.when(spot.is_middle)(lambda: self.z_own(False).start())
         self.first_copy(0).start()
         self.second_copy(0).start()
 
@@ -267,7 +265,7 @@
 
     def twin_copy(self, k):
         z = self.spot.arrival(k)
-        return self.copy(self.layer_rows(self.spot.core, z), 17 + k, 16 + z, self.spot.twin)
+        return self.copy(self.layer_blocks(self.spot.core, z), 17 + k, 16 + z, self.spot.twin)
 
     def along_z(self, k):
         spot = self.spot
@@ -292,23 +290,7 @@
 
     def from_twin(self, k):
         z = self.spot.arrival(k)
-        self.copy(self.layer_rows(1 - self.spot.core, z), 0, 16 + z, self.spot.twin).wait_recv()
-
-    def events(self):
-        return [
-            (0.0, self.own),
-            (2.5, lambda: self.along_first(0)),
-            (2.6, lambda: self.along_z(1)),
-            (4.0, lambda: self.along_z(2)),
-            (5.0, lambda: self.along_first(1)),
-            (5.5, lambda: self.along_z(3)),
-            (6.0, lambda: self.along_second(0)),
-            (7.0, lambda: self.along_first(2)),
-            (8.0, lambda: self.along_second(1)),
-            (9.0, lambda: self.along_first(3)),
-            (10.5, lambda: self.along_second(2)),
-            (13.0, lambda: self.along_second(3)),
-        ]
+        self.copy(self.layer_blocks(1 - self.spot.core, z), 0, 16 + z, self.spot.twin).wait_recv()
 
     def landed(self):
         for k in range(4):
@@ -316,7 +298,6 @@
 
     def drain(self):
         spot = self.spot
-        self.swap().wait_send()
         self.z_own(True).wait_send()
 
         @pl.when(spot.is_middle)
@@ -332,53 +313,1151 @@
             self.twin_copy(k).wait_send()
 
 
-def gather_kernel(*refs):
-    shards, held = refs[:6], refs[6:12]
-    stage, apart = refs[12:18], refs[18:24]
-    stage_sems, send, recv = refs[24:]
+class LineSum:
+    def __init__(self, spot, part, slot, send, recv):
+        self.spot, self.part, self.slot = spot, part, slot
+        self.send, self.recv = send, recv
+
+    def layer(self, k):
+        spot = self.spot
+        return (spot.layer(3), spot.layer(2), spot.layer(1 - spot.middle), spot.z)[k]
+
+    def copy(self, k, slot, device):
+        return remote(
+            self.part(self.layer(k)), self.slot(slot), self.send.at[k], self.recv.at[slot], device
+        )
+
+    def from_end(self, k):
+        return self.copy(k, k, self.spot.inner)
+
+    def from_middle(self, k):
+        return self.copy(k, 3 + k, self.spot.inner) if k < 2 else self.copy(2, 3, self.spot.outer)
+
+    def arrived(self, slot):
+        self.copy(0, slot, self.spot.inner).wait_recv()
+        return self.slot(slot)
+
+    def step(self, k):
+        spot = self.spot
+
+        @pl.when(spot.is_end)
+        def _():
+            self.from_end(k).start()
+
+        @pl.when(spot.is_middle)
+        def _():
+            source, part = self.arrived((0, 1, 3)[k]), self.part(self.layer(k))
+            for i in range(part.shape[0]):
+                part[i] += source[i]
+            self.from_middle(k).start()
+
+    def total(self, put):
+        def add(*slots):
+            sources = [self.arrived(slot) for slot in slots]
+            part = self.part(self.spot.z)
+            for i in range(part.shape[0]):
+                value = part[i].astype(jnp.float32)
+                for source in sources:
+                    value += source[i].astype(jnp.float32)
+                put(i, value)
+
+        pl.when(self.spot.is_end)(lambda: add(3))
+        pl.when(self.spot.is_middle)(lambda: add(2, 4))
+
+    def drain(self):
+        for k in range(3):
+            self.from_end(k).wait_send()
+
+
+class LineGather:
+    def __init__(self, spot, part, send, recv):
+        self.spot, self.part = spot, part
+        self.send, self.recv = send, recv
+
+    def copy(self, z, send, device):
+        ref = self.part(z)
+        return remote(ref, ref, self.send.at[send], self.recv.at[z], device)
+
+    def own(self, inward):
+        spot = self.spot
+        return self.copy(spot.z, 0 if inward else 1, spot.inner if inward else spot.outer)
+
+    def onward(self, k):
+        spot = self.spot
+        return self.copy(spot.arrival(k), 1 + k, spot.inner if k == 1 else spot.outer)
+
+    def open(self):
+        self.own(True).start()
+        pl.when(self.spot.is_middle)(lambda: self.own(False).start())
+
+    def step(self, k):
+        self.copy(self.spot.arrival(k), 0, self.spot.inner).wait_recv()
+        pl.when(self.spot.is_middle)(lambda: self.onward(k).start())
+
+    def drain(self):
+        self.own(True).wait_send()
+
+        @pl.when(self.spot.is_middle)
+        def _():
+            self.own(False).wait_send()
+            for k in (1, 2, 3):
+                self.onward(k).wait_send()
+
+
+class Scatter:
+    def __init__(
+        self, spot, sums, from_second, from_first, from_z, final, theirs, send, recv, credit, owed
+    ):
+        self.spot, self.sums = spot, sums
+        self.from_second, self.from_first = from_second, from_first
+        self.final, self.theirs = final, theirs
+        self.send, self.recv, self.credit = send, recv, credit
+        self.owed, self.whole = owed, theirs.shape[1] == 48
+        self.line = LineSum(
+            spot,
+            lambda z: sums.at[pl.ds(16 * z, 4)],
+            lambda i: from_z.at[i],
+            send.at[pl.ds(8, 3)],
+            recv.at[pl.ds(8, 5)],
+        )
+
+    def place(self, chip):
+        spot = self.spot
+        z, y, x = chip // 4, (chip // 2) % 2, chip % 2
+        other_y, other_x = lax.rem(spot.y + y, 2), lax.rem(spot.x + x, 2)
+        second = other_y * (1 - spot.core) + other_x * spot.core
+        first = other_x * (1 - spot.core) + other_y * spot.core
+        return 16 * z + 8 * second + 4 * first
+
+    def second_copy(self, k):
+        z = self.line.layer(k)
+        return remote(
+            self.sums.at[pl.ds(16 * z + 8, 8)],
+            self.from_second.at[z],
+            self.send.at[k],
+            self.recv.at[z],
+            self.spot.second,
+        )
+
+    def first_copy(self, k):
+        z = self.line.layer(k)
+        return remote(
+            self.sums.at[pl.ds(16 * z + 4, 4)],
+            self.from_first.at[z],
+            self.send.at[4 + k],
+            self.recv.at[4 + z],
+            self.spot.first,
+        )
+
+    def swap(self):
+        core = self.spot.core
+        if self.whole:
+            src = self.final.at[pl.ds(2 * (1 - core), 2)]
+        else:
+            src = self.final.at[:, pl.ds(pl.multiple_of((1 - core) * 24, 8), 24), :]
+        return remote(src, self.theirs, self.send.at[11], self.recv.at[13], self.spot.twin)
+
+    def start(self):
+        spot = self.spot
+        if self.owed:
+            for kind in range(3):
+                pl.semaphore_wait(self.credit.at[kind], 1)
+            pl.when(spot.is_middle)(lambda: pl.semaphore_wait(self.credit.at[3], 1))
+        for k in range(4):
+            self.second_copy(k).start()
+
+    def add_second(self, k):
+        z = self.line.layer(k)
+        self.second_copy(k).wait_recv()
+        for i in (4, 5, 6, 7, 0, 1, 2, 3):
+            self.sums[16 * z + i] += self.from_second[z, i]
+            if i == 7:
+                self.first_copy(k).start()
+
+    def add_first(self, k):
+        z = self.line.layer(k)
+        self.first_copy(k).wait_recv()
+        for i in range(4):
+            self.sums[16 * z + i] += self.from_first[z, i]
+        if k < 3:
+            self.line.step(k)
+
+    def finish(self):
+        def put(i, value):
+            self.final[i] = value
+
+        self.line.total(put)
+        self.swap().start()
+
+    def store(self, put):
+        core = self.spot.core
+        for chunk in range(self.theirs.shape[0]):
+            if self.whole:
+                mine = self.final[2 * core + chunk]
+            else:
+                mine = self.final[chunk, pl.ds(pl.multiple_of(core * 24, 8), 24), :]
+            put(core, chunk, mine)
+        self.swap().wait_recv()
+        for chunk in range(self.theirs.shape[0]):
+            put(1 - core, chunk, self.theirs[chunk])
+
+    def drain(self):
+        for k in range(4):
+            self.second_copy(k).wait_send()
+            self.first_copy(k).wait_send()
+        self.line.drain()
+
+    def release(self):
+        spot, credit = self.spot, self.credit
+
+        def tell(kind, device):
+            pl.semaphore_signal(credit.at[kind], inc=1, device_id=device, device_id_type=MESH)
+
+        tell(0, spot.second)
+        tell(1, spot.first)
+
+        @pl.when(spot.is_end)
+        def _():
+            tell(3, spot.inner)
+
+        @pl.when(spot.is_middle)
+        def _():
+            tell(2, spot.inner)
+            tell(2, spot.outer)
+
+
+class Plan:
+    def __init__(self):
+        self.clock, self.waiting, self.count = 0.0, [], 0
+
+    def at(self, time, action):
+        self.waiting.append((time, self.count, action))
+        self.count += 1
+
+    def flush(self):
+        while self.waiting:
+            first = min(self.waiting, key=lambda entry: entry[:2])
+            if first[0] > self.clock:
+                return
+            self.waiting.remove(first)
+            first[2]()
+
+    def run(self, cost, action):
+        self.flush()
+        action()
+        self.clock += cost
+
+    def until(self, time):
+        while self.waiting and min(entry[0] for entry in self.waiting) <= time:
+            self.clock = max(self.clock, min(entry[0] for entry in self.waiting))
+            self.flush()
+        self.clock = max(self.clock, time)
+
+
+def dot(left, right):
+    return jnp.dot(left, right, preferred_element_type=jnp.float32)
+
+
+GATHER_STEPS = (
+    (2.5, "first", 0),
+    (2.6, "z", 1),
+    (4.0, "z", 2),
+    (5.0, "first", 1),
+    (5.5, "z", 3),
+    (6.0, "second", 0),
+    (7.0, "first", 2),
+    (8.0, "second", 1),
+    (9.0, "first", 3),
+    (10.5, "second", 2),
+    (13.0, "second", 3),
+)
+SCATTER_STEPS = (
+    (2.0, "second", 0),
+    (4.0, "second", 1),
+    (5.5, "first", 0),
+    (6.0, "second", 2),
+    (7.5, "first", 1),
+    (8.0, "second", 3),
+    (9.5, "first", 2),
+    (11.0, "first", 3),
+    (13.0, "finish", 0),
+)
+UNIT = 1.6
+GROUPS = ("spatial", "temporal", "up", "down")
+
+
+def layer_kernel(
+    tokens,
+    cotangent,
+    ids_row,
+    ids_col,
+    steps,
+    bias,
+    w_ada,
+    w_qkv_s,
+    w_out_s,
+    w_qkv_t,
+    w_out_t,
+    w_up,
+    w_down,
+    o_layer,
+    o_tokens,
+    o_ada,
+    o_bias,
+    o_qkv_s,
+    o_out_s,
+    o_qkv_t,
+    o_out_t,
+    o_up,
+    o_down,
+    held,
+    stage,
+    apart,
+    apart_down,
+    sums,
+    from_second,
+    from_first,
+    from_z,
+    all_steps,
+    cond,
+    mod_half,
+    mod,
+    tally,
+    rows_mod,
+    all_rows_mod,
+    xhat,
+    deviation,
+    normed,
+    attended,
+    turned,
+    hidden_turned,
+    qkv,
+    probs,
+    branch,
+    stream,
+    grad,
+    hidden,
+    slope,
+    grad_pre_twin,
+    gated,
+    gated_twin,
+    grad_attended,
+    grad_qkv_twin,
+    disallowed,
+    swap_sems,
+    gather_send,
+    gather_recv,
+    scatter_send,
+    scatter_recv,
+    credit,
+    twin_send,
+    twin_recv,
+    step_send,
+    step_recv,
+    mod_send,
+    mod_recv,
+    row_send,
+    row_recv,
+):
+    width, tok = tokens.shape[1], tokens.shape[0]
+    f32, bf16 = jnp.float32, jnp.bfloat16
     spot = Spot()
+    core = spot.core
+    grad_qkv, grad_normed = hidden, stream
+    greet(spot)
+
+    def attention_piece(w_qkv, w_out):
+        def piece(half, chunk):
+            if chunk < 3:
+                return w_qkv[:, pl.ds(pl.multiple_of(half * 1152 + chunk * 384, 128), 384)]
+            return w_out[:, pl.ds(pl.multiple_of(half * 384, 128), 384)]
+
+        return piece
+
+    def up_piece(half, chunk):
+        return w_up[:, pl.ds(pl.multiple_of(half * 1536 + chunk * 384, 128), 384)]
+
+    def down_piece(half, chunk):
+        return w_down[chunk * 48 : chunk * 48 + 48, pl.ds(pl.multiple_of(half * 384, 128), 384)]
+
+    pieces = (
+        attention_piece(w_qkv_s, w_out_s),
+        attention_piece(w_qkv_t, w_out_t),
+        up_piece,
+        down_piece,
+    )
     gathers = [
-        Gather(spot, shards[i], held[i], stage[i], apart[i], stage_sems.at[i], send.at[i], recv.at[i])
-        for i in range(6)
+        Gather(
+            spot,
+            held.at[g],
+            stage.at[g],
+            apart.at[g] if g < 3 else apart_down,
+            swap_sems.at[g],
+            gather_send.at[g],
+            gather_recv.at[g],
+        )
+        for g in range(4)
     ]
-    greet(spot)
-    events = []
-    start = 0.0
-    for i, gather in enumerate(gathers):
-        unit = gather.rows * gather.width / (48 * 1152)
-        for place, (at, action) in enumerate(gather.events()):
-            when = start + at * unit if place else start - 10
-            events.append((when, i, place, action))
-        start += 12 * unit
-    events.sort(key=lambda e: e[:3])
+    scatters = [
+        Scatter(
+            spot,
+            sums.at[n % 2],
+            from_second.at[n % 2],
+            from_first.at[n % 2],
+            from_z.at[n % 2],
+            stage.at[3 - n],
+            apart_down if n == 0 else apart.at[3 - n],
+            scatter_send.at[n],
+            scatter_recv.at[n],
+            credit.at[n % 2],
+            n >= 2,
+        )
+        for n in range(4)
+    ]
+
+    def put_attention(o_qkv, o_out):
+        def put(half, chunk, rows):
+            if chunk < 3:
+                o_qkv[:, pl.ds(pl.multiple_of(half * 1152 + chunk * 384, 128), 384)] = rows
+            else:
+                o_out[:, pl.ds(pl.multiple_of(half * 384, 128), 384)] = rows
+
+        return put
+
+    def put_up(half, chunk, rows):
+        o_up[:, pl.ds(pl.multiple_of(half * 1536 + chunk * 384, 128), 384)] = rows
+
+    def put_down(half, chunk, rows):
+        o_down[chunk * 48 : chunk * 48 + 48, pl.ds(pl.multiple_of(half * 384, 128), 384)] = rows
+
+    puts = (put_down, put_up, put_attention(o_qkv_t, o_out_t), put_attention(o_qkv_s, o_out_s))
+
+    def to_twin(index, src, dst):
+        return remote(src, dst, twin_send.at[index], twin_recv.at[index], spot.twin)
+
+    def turned_copy(i):
+        return to_twin(i, turned.at[i, 0], turned.at[i, 1])
+
+    def hidden_copy():
+        return to_twin(5, hidden_turned.at[0], hidden_turned.at[1])
+
+    def gated_copy(j):
+        theirs = pl.multiple_of((1 - core) * 384, 128)
+        return to_twin(6 + j, gated.at[j, :, pl.ds(theirs, 384)], gated_twin.at[j])
+
+    def grad_pre_copy():
+        theirs = pl.multiple_of((1 - core) * 1536, 128)
+        return to_twin(9, slope.at[:, pl.ds(theirs, 1536)], grad_pre_twin)
+
+    def grad_qkv_copy(j):
+        theirs = pl.multiple_of((1 - core) * 1152, 128)
+        return to_twin(10 + j, grad_qkv.at[:, pl.ds(theirs, 1152)], grad_qkv_twin.at[j])
+
+    def step_copy(index, ref, device):
+        return remote(ref, ref, step_send.at[index], step_recv.at[index], device)
+
+    def step_pair(plane):
+        return all_steps.at[spot.z, plane]
+
+    step_line = LineGather(
+        spot, lambda z: all_steps.at[z], step_send.at[pl.ds(4, 5)], step_recv.at[pl.ds(4, 4)]
+    )
+
+    def steps_open():
+        all_steps[spot.z, spot.plane, core] = steps[...]
+        step_copy(0, all_steps.at[spot.z, spot.plane, core], spot.twin).start()
+
+    def steps_first():
+        step_copy(0, all_steps.at[spot.z, spot.plane, 1 - core], spot.twin).wait_recv()
+        step_copy(1, step_pair(spot.plane), spot.first).start()
+        step_copy(2, step_pair(spot.plane), spot.second).start()
+
+    def steps_second():
+        step_copy(1, step_pair(spot.first_plane), spot.first).wait_recv()
+        step_copy(3, step_pair(spot.first_plane), spot.second).start()
+
+    def steps_z():
+        step_copy(2, step_pair(spot.second_plane), spot.second).wait_recv()
+        step_copy(3, step_pair(spot.far_plane), spot.second).wait_recv()
+        step_line.open()
+
+    def steps_drain():
+        step_copy(0, all_steps.at[spot.z, spot.plane, core], spot.twin).wait_send()
+        for index in (1, 2, 3):
+            step_copy(index, step_pair(spot.plane), spot.first).wait_send()
+        step_line.drain()
+
+    def make_cond():
+        flat = all_steps[...].reshape(256, 128)
+        clip = lax.broadcasted_iota(jnp.int32, (64, 256), 0)
+        column = lax.broadcasted_iota(jnp.int32, (64, 256), 1)
+        wanted = 8 * lax.shift_right_logical(clip, 1) + (clip & 1)
+        times = jnp.dot(
+            (column == wanted).astype(f32),
+            flat,
+            precision=lax.Precision.HIGHEST,
+            preferred_element_type=f32,
+        )
+        first = (spot.chip * 2 + core) * 24
+        half_width = width // 2
+        feature = first + lax.broadcasted_iota(jnp.int32, (64, 128), 1)
+        place = jnp.where(feature < half_width, feature, feature - half_width).astype(f32)
+        angle = times * jnp.exp(-math.log(FREQ_BASE) * place / half_width)
+        value = jnp.where(feature < half_width, jnp.cos(angle), jnp.sin(angle))
+        cond[...] = (value / (1.0 + jnp.exp(-value))).astype(bf16)
+
+    spare = sums.at[1]
+    mod_out, mod_in, mod_sum = (spare.at[pl.ds(i, 12)] for i in (0, 12, 24))
+    mod_first, mod_second, mod_one, mod_two = (spare.at[pl.ds(i, 3)] for i in (51, 54, 57, 60))
+    mod_line = LineSum(
+        spot,
+        lambda z: spare.at[pl.ds(24 + 3 * z, 3)],
+        lambda i: spare.at[pl.ds(36 + 3 * i, 3)],
+        mod_send.at[pl.ds(0, 3)],
+        mod_recv.at[pl.ds(0, 5)],
+    )
+
+    def mod_copy(index):
+        src, dst, device = (
+            (mod_out, mod_in, spot.twin),
+            (mod_one, mod_first, spot.first),
+            (mod_two, mod_second, spot.second),
+            (mod_half.at[core], mod_half.at[core], spot.twin),
+        )[index]
+        return remote(src, dst, mod_send.at[3 + index], mod_recv.at[5 + index], device)
+
+    def mod_partial(half, chunk):
+        columns = pl.ds(pl.multiple_of(half * 3456 + chunk * 384, 128), 384)
+        return dot(cond[:, :24], w_ada[:, columns]) + bias[:, columns]
+
+    def mod_twin():
+        for chunk in range(9):
+            value = mod_partial(1 - core, chunk).astype(bf16)
+            for z in range(4):
+                mod_out[3 * z + chunk // 3, 16 * (chunk % 3) : 16 * (chunk % 3) + 16] = value[
+                    16 * z : 16 * z + 16
+                ]
+        mod_copy(0).start()
+
+    def mod_own():
+        mod_copy(0).wait_recv()
+        for chunk in range(9):
+            value = mod_partial(core, chunk)
+            rows = slice(16 * (chunk % 3), 16 * (chunk % 3) + 16)
+            for z in range(4):
+                at = 3 * z + chunk // 3
+                mod_sum[at, rows] = (
+                    value[16 * z : 16 * z + 16] + mod_in[at, rows].astype(f32)
+                ).astype(bf16)
+
+    def mod_along_first():
+        def put(i, value):
+            mod_one[i] = value.astype(bf16)
+
+        mod_line.total(put)
+        mod_copy(1).start()
+
+    def mod_along_second():
+        mod_copy(1).wait_recv()
+        for i in range(3):
+            mod_two[i] = mod_one[i] + mod_first[i]
+        mod_copy(2).start()
+
+    def mod_to_twin():
+        mod_copy(2).wait_recv()
+        for chunk in range(9):
+            at, rows = chunk // 3, slice(16 * (chunk % 3), 16 * (chunk % 3) + 16)
+            mod_half[core, :, 384 * chunk : 384 * chunk + 384] = mod_two[at, rows].astype(
+                f32
+            ) + mod_second[at, rows].astype(f32)
+        mod_copy(3).start()
+
+    def mod_rows():
+        remote(
+            mod_half.at[1 - core], mod_half.at[1 - core], mod_send.at[6], mod_recv.at[8], spot.twin
+        ).wait_recv()
+        row = lax.broadcasted_iota(jnp.int32, (16, 384), 0)
+        for clip in range(2):
+            chosen = row == 4 * spot.plane + 2 * core + clip
+            for chunk in range(18):
+                at = 384 * (chunk % 9)
+                value = mod_half[chunk // 9, :, at : at + 384]
+                mod[clip : clip + 1, 384 * chunk : 384 * chunk + 384] = jnp.sum(
+                    jnp.where(chosen, value, 0.0), axis=0, keepdims=True
+                )
+
+    def mod_drain():
+        mod_line.drain()
+        for index in range(4):
+            mod_copy(index).wait_send()
+
+    row_line = LineGather(
+        spot,
+        lambda z: all_rows_mod.at[core, z],
+        row_send.at[pl.ds(4, 5)],
+        row_recv.at[pl.ds(4, 4)],
+    )
+
+    def row_copy(index):
+        src, dst, device = (
+            (rows_mod.at[1], rows_mod.at[2], spot.twin),
+            (rows_mod.at[0], rows_mod.at[3], spot.first),
+            (rows_mod.at[5], rows_mod.at[4], spot.second),
+            (all_rows_mod.at[core], all_rows_mod.at[core], spot.twin),
+        )[index]
+        return remote(src, dst, row_send.at[index], row_recv.at[index], device)
+
+    def row_value(half):
+        columns = pl.ds(pl.multiple_of(half * 3456, 128), 3456)
+        row = lax.broadcasted_iota(jnp.int32, (16, 3456), 0)
+        mine = 4 * spot.plane + 2 * core
+        value = jnp.where(row == mine, tally[0:1, columns], 0.0)
+        return jnp.where(row == mine + 1, tally[1:2, columns], value).astype(bf16)
+
+    def rows_open():
+        rows_mod[1] = row_value(1 - core)
+        row_copy(0).start()
+
+    def rows_first():
+        row_copy(0).wait_recv()
+        rows_mod[0] = row_value(core) + rows_mod[2]
+        row_copy(1).start()
+
+    def rows_second():
+        row_copy(1).wait_recv()
+        rows_mod[5] = rows_mod[0] + rows_mod[3]
+        row_copy(2).start()
+
+    def rows_z():
+        row_copy(2).wait_recv()
+        all_rows_mod[core, spot.z] = rows_mod[5] + rows_mod[4]
+        row_line.open()
+
+    def rows_twin():
+        row_copy(3).start()
+
+    def ada_half(half):
+        for chunk in range(9):
+            value = all_rows_mod[half, :, :, 384 * chunk : 384 * chunk + 384].reshape(64, 384)
+            columns = pl.ds(pl.multiple_of(half * 3456 + 384 * chunk, 128), 384)
+            o_ada[:, columns] = contract_rows(cond[...], value)[:24]
+            o_bias[:, columns] = jnp.sum(value.astype(f32), axis=0, keepdims=True)
+
+    def rows_last():
+        remote(
+            all_rows_mod.at[1 - core],
+            all_rows_mod.at[1 - core],
+            row_send.at[3],
+            row_recv.at[3],
+            spot.twin,
+        ).wait_recv()
+        ada_half(1 - core)
+
+    def rows_drain():
+        for index in range(4):
+            row_copy(index).wait_send()
+        row_line.drain()
+
+    def by_rows(action):
+        @pl.loop(0, tok // 64)
+        def _(i):
+            action(pl.ds(pl.multiple_of(i * 64, 64), 64))
+
+    def mod_part(j, component, rows):
+        at = (3 * j + component) * width
+        second = ids_col[rows, 2:3] == 1
+        return jnp.where(second, mod[1:2, at : at + width], mod[0:1, at : at + width])
+
+    def count(j, component, rows, value):
+        at = (3 * j + component) * width
+        second = ids_col[rows, 2:3] == 1
+        tally[0:1, at : at + width] += jnp.sum(jnp.where(second, 0.0, value), axis=0, keepdims=True)
+        tally[1:2, at : at + width] += jnp.sum(jnp.where(second, value, 0.0), axis=0, keepdims=True)
+
+    def masks():
+        for j in range(2):
+            same = ids_col[:, j : j + 1] == ids_row[j : j + 1, :]
+            disallowed[j] = jnp.where(same, 0.0, MASKED)
+        tally[...] = jnp.zeros_like(tally)
+
+    def standardize(j):
+        def action(rows):
+            if j == 0:
+                stream[rows] = tokens[rows].astype(f32)
+            value = stream[rows]
+            center = value - jnp.mean(value, axis=-1, keepdims=True)
+            inverse = lax.rsqrt(jnp.mean(center * center, axis=-1, keepdims=True) + EPSILON)
+            xhat[j, rows] = (center * inverse).astype(bf16)
+            deviation[rows, j : j + 1] = inverse
+
+        by_rows(action)
+
+    def modulate(j):
+        def action(rows):
+            normed[rows] = (
+                xhat[j, rows].astype(f32) * (1.0 + mod_part(j, 1, rows)) + mod_part(j, 0, rows)
+            ).astype(bf16)
+
+        by_rows(action)
+
+    def turn(i, source):
+        for at in range(0, tok, 128):
+            turned[i, 0, :, at : at + 128] = source[at : at + 128, :].T
+        turned_copy(i).start()
+
+    def weight(g, half, chunk):
+        return held[g, half, :, chunk].reshape(width, 384)
+
+    def project(j):
+        @pl.loop(0, 6)
+        def _(i):
+            half, chunk = lax.div(i, 3), lax.rem(i, 3)
+            columns = pl.ds(pl.multiple_of(i * 384, 128), 384)
+            qkv[j, :, columns] = dot(normed[...], weight(j, half, chunk)).astype(bf16)
+
+    def head_lanes():
+        lane = lax.broadcasted_iota(jnp.int32, (1, 128), 1)
+        return lane < 64, lane >= 64
+
+    def head_columns(pair):
+        return [pl.ds(pl.multiple_of(part * 768 + pair * 128, 128), 128) for part in range(3)]
+
+    def attend(j, first, last):
+        @pl.loop(first, last)
+        def _(pair):
+            at_q, at_k, at_v = head_columns(pair)
+            queries, keys, values = qkv[j, :, at_q], qkv[j, :, at_k], qkv[j, :, at_v]
+            results = []
+            for head, lanes in enumerate(head_lanes()):
+                scaled = jnp.where(lanes, queries, 0.0) * bf16(0.125)
+                scores = contract_cols(scaled, keys) + disallowed[j]
+                scores = jnp.exp(scores - jnp.max(scores, axis=-1, keepdims=True))
+                low = (scores * (1.0 / jnp.sum(scores, axis=-1, keepdims=True))).astype(bf16)
+                probs[j, 2 * pair + head] = low
+                results.append(dot(low, values))
+            attended[:, at_q] = jnp.where(head_lanes()[0], results[0], results[1]).astype(bf16)
+
+    def join(j):
+        @pl.loop(0, 2)
+        def _(half):
+            columns = pl.ds(pl.multiple_of(half * 384, 128), 384)
+            branch[j, :, columns] = dot(attended[...], weight(j, half, 3)).astype(bf16)
+
+    def add_branch(j):
+        def action(rows):
+            stream[rows] += mod_part(j, 2, rows) * branch[j, rows].astype(f32)
+
+        by_rows(action)
+
+    def expand(first, last):
+        @pl.loop(first, last)
+        def _(i):
+            columns = pl.ds(pl.multiple_of(i * 384, 128), 384)
+            matrix = weight(2, lax.div(i, 4), lax.rem(i, 4))
+            for at in range(0, tok, 128):
+                rows = slice(at, at + 128)
+                pre = dot(normed[rows], matrix)
+                square = pre * pre
+                root = math.sqrt(2.0 / math.pi)
+                bent = jnp.tanh(root * (pre + 0.044715 * (square * pre)))
+                value = (0.5 * pre * (1.0 + bent)).astype(bf16)
+                hidden[rows, columns] = value
+                hidden_turned[0, columns, rows] = value.T
+                slope[rows, columns] = (
+                    0.5 * (1.0 + bent)
+                    + 0.5 * pre * (1.0 - bent * bent) * (root * (1.0 + 3 * 0.044715 * square))
+                ).astype(bf16)
+
+    def gate(j):
+        def action(rows):
+            value = cotangent[rows].astype(f32) if j == 2 else grad[rows]
+            if j == 2:
+                grad[rows] = value
+            else:
+                count(j, 2, rows, value * branch[j, rows].astype(f32))
+            gated[j, rows] = (mod_part(j, 2, rows) * value).astype(bf16)
+
+        by_rows(action)
+        gated_copy(j).start()
+
+    def own_columns(first, width_of_half):
+        return pl.ds(pl.multiple_of(core * width_of_half + first, 128), 384)
+
+    def down_terms(first, last):
+        scatter = scatters[0]
+        for z in range(first, last):
+            rows = slice(768 * z, 768 * z + 768)
+            value = dot(hidden_turned[0, rows], gated[2, :, own_columns(0, 384)]) + dot(
+                hidden_turned[1, rows], gated_twin[2]
+            )
+            value = value.astype(bf16).reshape(4, 4, 48, 384)
+            for plane in range(4):
+                sums[0, pl.ds(scatter.place(4 * z + plane), 4)] = value[plane]
+
+    def column_terms(n, chunk, left, right, right_twin):
+        value = dot(turned[left, 0], right) + dot(turned[left, 1], right_twin)
+        value = value.astype(bf16).reshape(16, 48, 384)
+        for chip in range(16):
+            sums[n % 2, scatters[n].place(chip) + chunk] = value[chip]
+
+    def up_terms(chunk):
+        column_terms(
+            1,
+            chunk,
+            4,
+            slope[:, own_columns(384 * chunk, 1536)],
+            grad_pre_twin[:, 384 * chunk : 384 * chunk + 384],
+        )
+
+    def out_terms(j):
+        column_terms(3 - j, 3, 2 * j + 1, gated[j, :, own_columns(0, 384)], gated_twin[j])
+
+    def qkv_terms(j, chunk):
+        column_terms(
+            3 - j,
+            chunk,
+            2 * j,
+            grad_qkv[:, own_columns(384 * chunk, 1152)],
+            grad_qkv_twin[j, :, 384 * chunk : 384 * chunk + 384],
+        )
+
+    def contract():
+        @pl.loop(0, 2)
+        def _(half):
+            columns = pl.ds(pl.multiple_of(half * 384, 128), 384)
+            matrix = held[3, half].reshape(3072, 384)
+            normed[:, columns] = dot(hidden[...], matrix).astype(bf16)
+
+    def close():
+        def action(rows):
+            value = normed[rows].astype(f32)
+            o_layer[rows] = (stream[rows] + mod_part(2, 2, rows) * value).astype(bf16)
+            count(2, 2, rows, cotangent[rows].astype(f32) * value)
+
+        by_rows(action)
+
+    def grad_hidden(first, last):
+        @pl.loop(first, last)
+        def _(i):
+            columns = pl.ds(pl.multiple_of(i * 384, 128), 384)
+            value = sum(
+                contract_cols(
+                    gated[2, :, 384 * half : 384 * half + 384],
+                    held[3, half, pl.ds(2 * i, 2)].reshape(384, 384),
+                )
+                for half in range(2)
+            )
+            slope[:, columns] = (slope[:, columns].astype(f32) * value).astype(bf16)
+
+    def back_project(g, chunks, source, first, last):
+        @pl.loop(first, last)
+        def _(i):
+            columns = pl.ds(pl.multiple_of(i * 384, 128), 384)
+            value = contract_cols(
+                source[:, columns], weight(g, lax.div(i, chunks), lax.rem(i, chunks))
+            )
+
+            @pl.when(i == 0)
+            def _():
+                grad_normed[...] = value
+
+            @pl.when(i > 0)
+            def _():
+                grad_normed[...] += value
+
+    def norm_back(j):
+        def action(rows):
+            value, unit = grad_normed[rows], xhat[j, rows].astype(f32)
+            count(j, 0, rows, value)
+            count(j, 1, rows, value * unit)
+            scaled = value * (1.0 + mod_part(j, 1, rows))
+            inner = jnp.mean(scaled * unit, axis=-1, keepdims=True)
+            scaled = scaled - jnp.mean(scaled, axis=-1, keepdims=True)
+            total = grad[rows] + deviation[rows, j : j + 1] * (scaled - unit * inner)
+            if j == 0:
+                o_tokens[rows] = total
+            else:
+                grad[rows] = total
+
+        by_rows(action)
+
+    def split(j):
+        value = sum(
+            contract_cols(gated[j, :, 384 * half : 384 * half + 384], weight(j, half, 3))
+            for half in range(2)
+        )
+        grad_attended[...] = value.astype(bf16)
+
+    def attend_back(j, first, last):
+        @pl.loop(first, last)
+        def _(pair):
+            at_q, at_k, at_v = head_columns(pair)
+            queries, keys, values = qkv[j, :, at_q], qkv[j, :, at_k], qkv[j, :, at_v]
+            given = grad_attended[:, at_q]
+            grad_q, grad_k, grad_v = [], 0.0, 0.0
+            for head, lanes in enumerate(head_lanes()):
+                part = jnp.where(lanes, given, 0.0).astype(bf16)
+                low = probs[j, 2 * pair + head]
+                product = low.astype(f32) * contract_cols(part, values)
+                total = jnp.sum(product, axis=-1, keepdims=True)
+                scores = ((product - low.astype(f32) * total) * 0.125).astype(bf16)
+                grad_v += contract_rows(low, part)
+                grad_k += contract_rows(scores, jnp.where(lanes, queries, 0.0).astype(bf16))
+                grad_q.append(dot(scores, keys))
+            grad_qkv[:, at_q] = jnp.where(head_lanes()[0], grad_q[0], grad_q[1]).astype(bf16)
+            grad_qkv[:, at_k] = grad_k.astype(bf16)
+            grad_qkv[:, at_v] = grad_v.astype(bf16)
+
+    plan = Plan()
+    run = plan.run
+    for g, gather in enumerate(gathers):
+        gather.open(pieces[g])
+        begin = 1.0 + 12 * UNIT * g
+        plan.at(begin - (2 * UNIT if g else 0.5), gather.own)
+        kinds = {"z": gather.along_z, "first": gather.along_first, "second": gather.along_second}
+        for at, kind, k in GATHER_STEPS:
+            plan.at(begin + at * UNIT, partial(kinds[kind], k))
+
+    def landed(g):
+        plan.until(2.0 + UNIT * (12 * g + 14.5))
+        gathers[g].landed()
+
+    steps_open()
+    plan.at(2.0, steps_first)
+    plan.at(4.0, steps_second)
+    plan.at(6.0, steps_z)
+    for k in (1, 2, 3):
+        plan.at(6.0 + 2 * k, partial(step_line.step, k))
+    plan.at(12.1, make_cond)
+    plan.at(12.5, mod_twin)
+    plan.at(14.5, mod_own)
+    plan.at(15.5, lambda: mod_line.step(0))
+    plan.at(16.5, lambda: mod_line.step(1))
+    plan.at(20.0, lambda: mod_line.step(2))
+    plan.at(25.0, mod_along_first)
+    plan.at(28.5, mod_along_second)
+    plan.at(32.0, mod_to_twin)
+
+    run(1.0, masks)
+    run(1.0, lambda: standardize(0))
+    plan.until(34.0)
+    mod_rows()
+    landed(0)
+    for j in range(2):
+        if j:
+            run(1.0, lambda: standardize(1))
+            landed(1)
+        run(1.0, lambda: modulate(j))
+        run(2.0, lambda: project(j))
+        run(0.5, lambda: turn(2 * j, normed))
+        for pair in range(0, 6, 2):
+            run(1.5, lambda: attend(j, pair, pair + 2))
+        run(0.7, lambda: join(j))
+        run(0.5, lambda: add_branch(j))
+        run(0.5, lambda: turn(2 * j + 1, attended))
+    run(1.0, lambda: standardize(2))
+    run(1.0, lambda: modulate(2))
+    run(0.5, lambda: turn(4, normed))
+    run(1.0, lambda: gate(2))
+    landed(2)
+    for i in range(0, 8, 2):
+        run(1.2, lambda: expand(i, i + 2))
+    steps_drain()
+    mod_drain()
     for gather in gathers:
-        gather.open()
-    for _, _, _, action in events:
-        action()
-    for gather in gathers:
-        gather.landed()
+        gather.swap().wait_send()
+    run(0.0, lambda: hidden_copy().start())
+
+    link = [0.0]
+
+    def begin_scatter(n):
+        scatters[n].start()
+        begin = max(plan.clock, link[0])
+        link[0] = begin + 12 * UNIT
+        kinds = {"second": scatters[n].add_second, "first": scatters[n].add_first}
+        for at, kind, k in SCATTER_STEPS:
+            action = scatters[n].finish if kind == "finish" else partial(kinds[kind], k)
+            plan.at(begin + at * UNIT, action)
+        return begin + 13 * UNIT + 0.1
+
+    plan.until(plan.clock + 2.0)
+    gated_copy(2).wait_recv()
+    hidden_copy().wait_recv()
+    for z in range(4):
+        run(0.7, lambda: down_terms(z, z + 1))
+    ends = [begin_scatter(0)]
+    landed(3)
+    for i in range(0, 8, 2):
+        run(0.6, lambda: grad_hidden(i, i + 2))
+    run(0.0, lambda: grad_pre_copy().start())
+    run(2.0, contract)
+    run(1.0, close)
+    plan.flush()
+    grad_pre_copy().wait_recv()
+    turned_copy(4).wait_recv()
+    for chunk in range(4):
+        run(0.7, lambda: up_terms(chunk))
+    ends.append(begin_scatter(1))
+    for i in range(0, 8, 2):
+        run(0.7, lambda: back_project(2, 4, slope, i, i + 2))
+    run(1.5, lambda: norm_back(2))
+
+    def retire(n):
+        scatters[n].drain()
+        scatters[n].store(puts[n])
+        scatters[n].swap().wait_send()
+        if n < 2:
+            scatters[n].release()
+
+    for j in (1, 0):
+        n = 3 - j
+        run(1.0, lambda: gate(j))
+        run(1.0, lambda: split(j))
+        for pair in range(0, 6, 2):
+            run(2.5, lambda: attend_back(j, pair, pair + 2))
+        run(0.0, lambda: grad_qkv_copy(j).start())
+        plan.until(ends[n - 2])
+        retire(n - 2)
+        turned_copy(2 * j + 1).wait_recv()
+        gated_copy(j).wait_recv()
+        run(0.7, lambda: out_terms(j))
+        turned_copy(2 * j).wait_recv()
+        grad_qkv_copy(j).wait_recv()
+        for chunk in range(3):
+            run(0.7, lambda: qkv_terms(j, chunk))
+        ends.append(begin_scatter(n))
+        for i in range(0, 6, 2):
+            run(0.7, lambda: back_project(j, 3, grad_qkv, i, i + 2))
+        run(1.5, lambda: norm_back(j))
+        grad_qkv_copy(j).wait_send()
+    now = plan.clock
+    plan.at(now, rows_open)
+    plan.at(now + 2.0, rows_first)
+    plan.at(now + 5.0, rows_second)
+    plan.at(now + 8.0, rows_z)
+    plan.at(now + 11.0, lambda: row_line.step(1))
+    plan.at(now + 14.0, lambda: row_line.step(2))
+    plan.at(now + 17.0, lambda: row_line.step(3))
+    plan.at(now + 17.1, rows_twin)
+    plan.at(now + 17.2, lambda: ada_half(core))
+    plan.at(now + 18.5, rows_last)
+    plan.at(ends[2], lambda: retire(2))
+    plan.until(1e6)
+    retire(3)
+    rows_drain()
     for gather in gathers:
         gather.drain()
-
-
-def gather_weights(shards):
-    dims = [(16 * 2 * s.shape[0], s.shape[1] // 2) for s in shards]
+    for i in range(5):
+        turned_copy(i).wait_send()
+    hidden_copy().wait_send()
+    for j in range(3):
+        gated_copy(j).wait_send()
+    grad_pre_copy().wait_send()
+
+
+def layer(tokens, cotangent, ids_row, ids_col, steps, bias, w_ada, *shards):
+    f32, bf16 = jnp.float32, jnp.bfloat16
+    tok, width = tokens.shape
+    block = (4, 48, 384)
+    dma, vmem = pltpu.SemaphoreType.DMA, pltpu.VMEM
     return pl.pallas_call(
-        gather_kernel,
-        out_shape=[jax.ShapeDtypeStruct((2, r, n), jnp.bfloat16) for r, n in dims],
-        in_specs=[pl.BlockSpec(memory_space=pltpu.VMEM)] * 6,
-        out_specs=[pl.BlockSpec(memory_space=pltpu.VMEM)] * 6,
-        scratch_shapes=[pltpu.VMEM((r // 16, n), jnp.float32) for r, n in dims]
-        + [pltpu.VMEM((r // 32, n), jnp.float32) for r, n in dims]
-        + [
-            pltpu.SemaphoreType.DMA((6, 2)),
-            pltpu.SemaphoreType.DMA((6, 21)),
-            pltpu.SemaphoreType.DMA((6, 20)),
+        layer_kernel,
+        out_shape=[
+            jax.ShapeDtypeStruct((tok, width), bf16),
+            jax.ShapeDtypeStruct((tok, width), f32),
+            jax.ShapeDtypeStruct(w_ada.shape, f32),
+            jax.ShapeDtypeStruct((1, w_ada.shape[1]), f32),
+        ]
+        + [jax.ShapeDtypeStruct(shard.shape, f32) for shard in shards],
+        in_specs=[pl.BlockSpec(memory_space=vmem)] * 13,
+        out_specs=[pl.BlockSpec(memory_space=vmem)] * 10,
+        scratch_shapes=[
+            vmem((4, 2, 16) + block, bf16),
+            vmem((4,) + block, f32),
+            vmem((3, 4, 24, 384), f32),
+            vmem((2, 48, 384), f32),
+            vmem((2, 64, 48, 384), bf16),
+            vmem((2, 4, 8, 48, 384), bf16),
+            vmem((2, 4) + block, bf16),
+            vmem((2, 5) + block, bf16),
+            vmem((4, 4, 2, 8, 128), f32),
+            vmem((64, 128), bf16),
+            vmem((2, 16, 3456), f32),
+            vmem((8, 6912), f32),
+            vmem((8, 6912), f32),
+            vmem((6, 16, 3456), bf16),
+            vmem((2, 4, 16, 3456), bf16),
+            vmem((3, tok, width), bf16),
+            vmem((tok, 128), f32),
+            vmem((tok, width), bf16),
+            vmem((tok, width), bf16),
+            vmem((5, 2, width, tok), bf16),
+            vmem((2, 4 * width, tok), bf16),
+            vmem((2, tok, 3 * width), bf16),
+            vmem((2, HEADS, tok, tok), bf16),
+            vmem((2, tok, width), bf16),
+            vmem((tok, width), f32),
+            vmem((tok, width), f32),
+            vmem((tok, 4 * width), bf16),
+            vmem((tok, 4 * width), bf16),
+            vmem((tok, 2 * width), bf16),
+            vmem((3, tok, width), bf16),
+            vmem((3, tok, width // 2), bf16),
+            vmem((tok, width), bf16),
+            vmem((2, tok, 3 * width // 2), bf16),
+            vmem((2, tok, tok), f32),
+            dma((4, 2)),
+            dma((4, 21)),
+            dma((4, 20)),
+            dma((4, 12)),
+            dma((4, 14)),
+            pltpu.SemaphoreType.REGULAR((2, 4)),
+            dma((12,)),
+            dma((12,)),
+            dma((9,)),
+            dma((8,)),
+            dma((7,)),
+            dma((9,)),
+            dma((9,)),
+            dma((8,)),
         ],
         compiler_params=pltpu.CompilerParams(
-            collective_id=0, has_side_effects=True, vmem_limit_bytes=60 * 2**20
+            collective_id=0, has_side_effects=True, vmem_limit_bytes=64 * 2**20
         ),
-    )(*shards)
+    )(tokens, cotangent, ids_row, ids_col, steps, bias, w_ada, *shards)
+
+
+def on_grid(
+    tokens,
+    seg_ids,
+    frame_ids,
+    patch_ids,
+    timesteps,
+    w_ada,
+    b_ada,
+    w_qkv_spatial,
+    w_out_spatial,
+    w_qkv_temporal,
+    w_out_temporal,
+    w_up,
+    w_down,
+    cotangent,
+):
+    place = lax.axis_index(("wide", "narrow"))
+    share = b_ada.shape[0]
+    ids = jnp.stack([seg_ids * 16 + frame_ids, seg_ids * 16 + patch_ids, seg_ids])
+    steps = jnp.broadcast_to(
+        jnp.pad(timesteps.astype(jnp.float32), (0, 6))[:, None], (8, 128)
+    )
+    bias = lax.dynamic_update_slice(
+        jnp.zeros((1, w_ada.shape[1]), jnp.float32),
+        b_ada.astype(jnp.float32)[None],
+        (0, place * share),
+    )
+    shards = (w_qkv_spatial, w_out_spatial, w_qkv_temporal, w_out_temporal, w_up, w_down)
+    outs = layer(tokens, cotangent, ids, ids.T, steps, bias, w_ada, *shards)
+    bias_share = lax.dynamic_slice(outs[3][0], (place * share,), (share,))
+    return (*outs[:3], bias_share, *outs[4:])
 
 
 def on_device(
@@ -396,17 +1475,18 @@
     w_up,
     w_down,
     cotangent,
-    on_grid,
 ):
     axes = ("wide", "narrow")
-    shards = (w_qkv_spatial, w_out_spatial, w_qkv_temporal, w_out_temporal, w_up, w_down)
-    if on_grid:
-        halves = gather_weights(shards)
-        gathered = (None, None) + tuple(jnp.concatenate([h[0], h[1]], axis=1) for h in halves)
-    else:
-        gathered = (None, None) + tuple(
-            lax.all_gather(s, axes, axis=0, tiled=True) for s in shards
-        )
+    gathered = (
+        None,
+        None,
+        lax.all_gather(w_qkv_spatial, axes, axis=0, tiled=True),
+        lax.all_gather(w_out_spatial, axes, axis=0, tiled=True),
+        lax.all_gather(w_qkv_temporal, axes, axis=0, tiled=True),
+        lax.all_gather(w_out_temporal, axes, axis=0, tiled=True),
+        lax.all_gather(w_up, axes, axis=0, tiled=True),
+        lax.all_gather(w_down, axes, axis=0, tiled=True),
+    )
     width = tokens.shape[1]
     head_count = HEADS
     clip_count = timesteps.shape[0]
@@ -566,9 +1646,9 @@
         P(("wide", "narrow"), None),
         P(("wide", "narrow"), None),
     )
-    on_grid = dict(mesh.shape) == {"wide": 16, "narrow": 2}
+    grid = dict(mesh.shape) == {"wide": 16, "narrow": 2}
     return jax.shard_map(
-        partial(on_device, on_grid=on_grid),
+        on_grid if grid else on_device,
         mesh=mesh,
         in_specs=placed,
         out_specs=(

time: 1100 us -> 249 us (0.23)
  waiting for transfers between devices: 433 us -> 0 us
  matrix products: 277 us -> 0 us
  blocking collectives: 161 us -> 0 us
  Pallas kernels: 114 us -> 231 us
  local copies, waits for them, and re-layouts: 61.4 us -> 14.2 us
  other arithmetic: 24.8 us -> 0.02 us
  between operations: 15.2 us -> 0.73 us
    reduce_scatter x6 -> x0, waiting for transfers between devices: 433 us -> none  [share(): lax.psum_scatter(contract_rows(left, right).astype(jnp.bfloat16), axes, s...]
    dot_general x194 -> x0, matrix products: 277 us -> none  [the longest x78 94.1 us: contract_cols(): lax.dot_general(left, right, (((1,), (1,)), ((), ())), preferred_element_...]
    unnamed x3 -> x0, blocking collectives: 117 us -> none
    pallas_call x1, Pallas kernels: 114 us -> 231 us  [layer(): pl.pallas_call(layer_kernel, out_shape=[jax.ShapeDtypeStruct((tok, width)...]
    all_gather x1 -> x0, blocking collectives: 43.7 us -> none  [on_device(): all_grad_mod = lax.all_gather(grad_mod_low, axes, axis=0, tiled=True)]
    squeeze x6 -> x0, local copies, waits for them, and re-layouts: 19.2 us -> none  [the longest x4 14.9 us: on_device(): h[0]]
    unnamed x134 -> x39, local copies, waits for them, and re-layouts: 29.6 us -> 11.2 us
    convert_element_type x37 -> x1, other arithmetic: 13.5 us -> 0.01 us  [on_grid(): timesteps.astype(jnp.float32)]
  transfers between devices with their start and end apart: 7 -> 0, of which waited for: 5 -> 0; matrix products, arithmetic and copies ran while one was open for 12% -> 0% of each run, Pallas kernels for 11% -> 0%
where the time goes in v3:
time: 249 us; the launch traced here: 246 us
  Pallas kernels  231 us (93%)
  local copies, waits for them, and re-layouts  14.2 us (6%)
    pallas_call x1, Pallas kernels, layer(): pl.pallas_call(layer_kernel, out_shape=[jax.ShapeDtypeStruct((tok, width)...  231 us
    unnamed x39, local copies, waits for them, and re-layouts  11.2 us

profile of v3, /device:TPU:0, one launch (start us, length us, event | category | flops | bytes accessed | tf_op | source)
XLA Modules:
  0.0 245.8 jit_solution(4211085992879696597)
XLA Ops:
  0.6 0.0 copy-start.13
  0.7 0.6 copy-done.13
  1.3 0.6 copy-done.14
  2.0 0.7 copy-done.11
  2.6 0.0 copy-done.12
  2.7 0.0 copy-done.10
  2.7 0.7 broadcast_in_dim.15.steps
  3.4 0.2 dynamic_update_slice.3.bias
  3.6 0.0 copy-done.9
  3.6 0.0 copy-start.6
  3.6 0.8 copy.29
  4.4 0.0 copy-done.6
  4.4 230.8 %shard_map.213 = (bf16[256,768]{1,0:T(8,128)(2,1)}, f32[256,768]{1,0:T(8,128)}, f32[24,6912]{1,0:T(8,128)}, f32[1,6912]{1,0:T(1,128)}, f32[24,2304]{1,0:T(8,128)...) custom-call(bf16[256,768]{1,0:T(8,128)(2,1)} %tokens.1, ...), custom_call_target="tpu_custom_call" | custom-call | tf_op jit(solution)/shard_map/pallas_call | solution.py:1363
  235.2 0.0 copy-start
  235.2 1.4 constant_dynamic-slice_fusion
  236.6 1.8 copy.40
  238.4 0.0 copy-done
  238.4 0.9 copy.41
  239.3 0.5 copy-done.1
  239.8 0.8 copy.42
  240.6 0.3 copy-done.5
  240.9 0.7 copy.43
  241.6 0.2 copy-done.8
  241.8 0.6 copy.44
  242.4 0.0 copy-done.4
  242.4 0.7 copy.45
  243.1 0.2 copy-done.7
  243.4 0.6 copy.46
  244.0 0.0 copy-done.3
  244.0 0.7 copy.47
  244.7 0.4 copy-done.2
  245.1 0.7 copy.48
  (18 shorter events, 0.1 us)
Async XLA Ops:
  0.6 0.7 copy-start.13
  1.3 0.7 copy-start.14
  2.0 0.7 copy-start.11
  2.0 0.7 copy-start.12
  2.0 0.7 copy-start.10
  2.7 0.9 copy-start.9
  3.6 0.8 copy-start.6
  235.2 3.2 %copy-start = (f32[256,768]{1,0:T(8,128)S(1)}, f32[256,768]{1,0:T(8,128)}, u32[]{:S(2)}) copy-start(f32[256,768]{1,0:T(8,128)} %get-tuple-element.43) | copy-start | bytes 2359300
  238.4 1.4 copy-start.1
  239.8 1.1 copy-start.5
  240.9 0.9 copy-start.8
  240.9 1.5 copy-start.4
  242.4 0.9 copy-start.7
  242.4 1.5 copy-start.3
  244.0 1.1 copy-start.2

commit v4 on v3

--- a/solution.py
+++ b/solution.py
@@ -190,129 +190,6 @@
     )
 
 
-class Gather:
-    def __init__(self, spot, held, stage, apart, swap_sems, send, recv):
-        self.spot, self.held = spot, held
-        self.stage, self.apart, self.swap_sems = stage, apart, swap_sems
-        self.send, self.recv = send, recv
-        self.whole = apart.shape[1] == 48
-
-    def block(self, z, plane):
-        return self.held.at[self.spot.core, z * 4 + plane]
-
-    def layer_blocks(self, half, z):
-        return self.held.at[half, pl.ds(z * 4, 4)]
-
-    def copy(self, ref, send, recv, device):
-        return remote(ref, ref, self.send.at[send], self.recv.at[recv], device)
-
-    def mine(self):
-        core = self.spot.core
-        if self.whole:
-            return self.stage.at[pl.ds(2 * core, 2)]
-        return self.stage.at[:, pl.ds(pl.multiple_of(core * 24, 8), 24), :]
-
-    def swap(self):
-        return remote(
-            self.apart, self.mine(), self.swap_sems.at[0], self.swap_sems.at[1], self.spot.twin
-        )
-
-    def open(self, piece):
-        core = self.spot.core
-        for chunk in range(self.apart.shape[0]):
-            self.apart[chunk] = piece(1 - core, chunk).astype(jnp.float32)
-        self.swap().start()
-        place = self.mine()
-        for chunk in range(self.apart.shape[0]):
-            place[chunk] = piece(core, chunk).astype(jnp.float32)
-
-    def own(self):
-        spot = self.spot
-        self.swap().wait_recv()
-        self.held[spot.core, spot.chip] = self.stage[...].astype(jnp.bfloat16)
-        self.z_own(True).start()
-        pl.when(spot.is_middle)(lambda: self.z_own(False).start())
-        self.first_copy(0).start()
-        self.second_copy(0).start()
-
-    def z_own(self, inward):
-        spot = self.spot
-        return self.copy(
-            self.block(spot.z, spot.plane),
-            0 if inward else 1,
-            spot.z,
-            spot.inner if inward else spot.outer,
-        )
-
-    def z_pass(self, k):
-        spot = self.spot
-        z = spot.arrival(k)
-        return self.copy(
-            self.block(z, spot.plane), 1 + k, z, spot.inner if k == 1 else spot.outer
-        )
-
-    def first_copy(self, k):
-        z = self.spot.arrival(k)
-        return self.copy(self.block(z, self.spot.plane), 5 + k, 4 + z, self.spot.first)
-
-    def second_copy(self, k):
-        z = self.spot.arrival(k)
-        return self.copy(self.block(z, self.spot.plane), 9 + k, 8 + z, self.spot.second)
-
-    def second_pass(self, k):
-        z = self.spot.arrival(k)
-        return self.copy(self.block(z, self.spot.first_plane), 13 + k, 12 + z, self.spot.second)
-
-    def twin_copy(self, k):
-        z = self.spot.arrival(k)
-        return self.copy(self.layer_blocks(self.spot.core, z), 17 + k, 16 + z, self.spot.twin)
-
-    def along_z(self, k):
-        spot = self.spot
-        z = spot.arrival(k)
-        self.copy(self.block(z, spot.plane), 0, z, spot.inner).wait_recv()
-        pl.when(spot.is_middle)(lambda: self.z_pass(k).start())
-        self.first_copy(k).start()
-        self.second_copy(k).start()
-
-    def along_first(self, k):
-        spot = self.spot
-        z = spot.arrival(k)
-        self.copy(self.block(z, spot.first_plane), 0, 4 + z, spot.first).wait_recv()
-        self.second_pass(k).start()
-
-    def along_second(self, k):
-        spot = self.spot
-        z = spot.arrival(k)
-        self.copy(self.block(z, spot.second_plane), 0, 8 + z, spot.second).wait_recv()
-        self.copy(self.block(z, spot.far_plane), 0, 12 + z, spot.second).wait_recv()
-        self.twin_copy(k).start()
-
-    def from_twin(self, k):
-        z = self.spot.arrival(k)
-        self.copy(self.layer_blocks(1 - self.spot.core, z), 0, 16 + z, self.spot.twin).wait_recv()
-
-    def landed(self):
-        for k in range(4):
-            self.from_twin(k)
-
-    def drain(self):
-        spot = self.spot
-        self.z_own(True).wait_send()
-
-        @pl.when(spot.is_middle)
-        def _():
-            self.z_own(False).wait_send()
-            for k in (1, 2, 3):
-                self.z_pass(k).wait_send()
-
-        for k in range(4):
-            self.first_copy(k).wait_send()
-            self.second_copy(k).wait_send()
-            self.second_pass(k).wait_send()
-            self.twin_copy(k).wait_send()
-
-
 class LineSum:
     def __init__(self, spot, part, slot, send, recv):
         self.spot, self.part, self.slot = spot, part, slot
@@ -337,14 +214,11 @@
         self.copy(0, slot, self.spot.inner).wait_recv()
         return self.slot(slot)
 
-    def step(self, k):
-        spot = self.spot
-
-        @pl.when(spot.is_end)
-        def _():
-            self.from_end(k).start()
-
-        @pl.when(spot.is_middle)
+    def send_end(self, k):
+        pl.when(self.spot.is_end)(lambda: self.from_end(k).start())
+
+    def send_middle(self, k):
+        @pl.when(self.spot.is_middle)
         def _():
             source, part = self.arrived((0, 1, 3)[k]), self.part(self.layer(k))
             for i in range(part.shape[0]):
@@ -390,9 +264,17 @@
         self.own(True).start()
         pl.when(self.spot.is_middle)(lambda: self.own(False).start())
 
-    def step(self, k):
+    def get(self, k):
         self.copy(self.spot.arrival(k), 0, self.spot.inner).wait_recv()
-        pl.when(self.spot.is_middle)(lambda: self.onward(k).start())
+
+    def pass_on(self, k):
+        @pl.when(self.spot.is_middle)
+        def _():
+            self.get(k)
+            self.onward(k).start()
+
+    def take(self, k):
+        pl.when(self.spot.is_end)(lambda: self.get(k))
 
     def drain(self):
         self.own(True).wait_send()
@@ -404,35 +286,215 @@
                 self.onward(k).wait_send()
 
 
+class Gather:
+    def __init__(self, spot, held, stage, apart, swap_sems, send, recv):
+        self.spot, self.held = spot, held
+        self.stage, self.apart, self.swap_sems = stage, apart, swap_sems
+        self.send, self.recv = send, recv
+        self.whole = apart.shape[1] == 48
+        self.line = LineGather(
+            spot,
+            lambda z: held.at[spot.core, pl.ds(4 * z, 4), 3],
+            send.at[pl.ds(24, 5)],
+            recv.at[pl.ds(23, 4)],
+        )
+
+    def block(self, z, plane):
+        return self.held.at[self.spot.core, z * 4 + plane, 0:3]
+
+    def last(self, plane):
+        return self.held.at[self.spot.core, self.spot.z * 4 + plane, 3]
+
+    def copy(self, ref, send, recv, device):
+        return remote(ref, ref, self.send.at[send], self.recv.at[recv], device)
+
+    def mine(self):
+        core = self.spot.core
+        if self.whole:
+            return self.stage.at[pl.ds(2 * core, 2)]
+        return self.stage.at[:, pl.ds(pl.multiple_of(core * 24, 8), 24), :]
+
+    def swap(self):
+        return remote(
+            self.apart, self.mine(), self.swap_sems.at[0], self.swap_sems.at[1], self.spot.twin
+        )
+
+    def open(self, piece):
+        core = self.spot.core
+        for chunk in range(self.apart.shape[0]):
+            self.apart[chunk] = piece(1 - core, chunk).astype(jnp.float32)
+        self.swap().start()
+        place = self.mine()
+        for chunk in range(self.apart.shape[0]):
+            place[chunk] = piece(core, chunk).astype(jnp.float32)
+
+    def own(self):
+        spot = self.spot
+        self.swap().wait_recv()
+        self.held[spot.core, spot.chip] = self.stage[...].astype(jnp.bfloat16)
+        self.z_own(True).start()
+        pl.when(spot.is_middle)(lambda: self.z_own(False).start())
+        self.last_first().start()
+        self.last_second(False).start()
+
+    def z_own(self, inward):
+        spot = self.spot
+        return self.copy(
+            self.block(spot.z, spot.plane),
+            0 if inward else 1,
+            spot.z,
+            spot.inner if inward else spot.outer,
+        )
+
+    def z_pass(self, k):
+        spot = self.spot
+        z = spot.arrival(k)
+        return self.copy(
+            self.block(z, spot.plane), 1 + k, z, spot.inner if k == 1 else spot.outer
+        )
+
+    def first_copy(self, k):
+        z = self.spot.arrival(k)
+        return self.copy(self.block(z, self.spot.plane), 5 + k, 4 + z, self.spot.first)
+
+    def second_copy(self, k):
+        z = self.spot.arrival(k)
+        return self.copy(self.block(z, self.spot.plane), 9 + k, 8 + z, self.spot.second)
+
+    def second_pass(self, k):
+        z = self.spot.arrival(k)
+        return self.copy(self.block(z, self.spot.first_plane), 13 + k, 12 + z, self.spot.second)
+
+    def twin_copy(self, half, k):
+        z = self.spot.arrival(k)
+        ref = self.held.at[half, pl.ds(z * 4, 4), 0:3]
+        return self.copy(ref, 17 + k, 16 + z, self.spot.twin)
+
+    def last_first(self):
+        return self.copy(self.last(self.spot.plane), 21, 20, self.spot.first)
+
+    def last_second(self, onward):
+        spot = self.spot
+        plane = spot.first_plane if onward else spot.plane
+        return self.copy(self.last(plane), 23 if onward else 22, 22 if onward else 21, spot.second)
+
+    def last_twin(self, half, k):
+        z = self.spot.arrival(k)
+        ref = self.held.at[half, pl.ds(z * 4, 4), 3]
+        return self.copy(ref, 29 + k, 27 + z, self.spot.twin)
+
+    def get(self, k):
+        spot = self.spot
+        z = spot.arrival(k)
+        self.copy(self.block(z, spot.plane), 0, z, spot.inner).wait_recv()
+
+    def pass_on(self, k):
+        @pl.when(self.spot.is_middle)
+        def _():
+            self.get(k)
+            self.z_pass(k).start()
+
+    def spread(self, k):
+        if k:
+            pl.when(self.spot.is_end)(lambda: self.get(k))
+        self.first_copy(k).start()
+        self.second_copy(k).start()
+
+    def along_first(self, k):
+        spot = self.spot
+        z = spot.arrival(k)
+        self.copy(self.block(z, spot.first_plane), 0, 4 + z, spot.first).wait_recv()
+        self.second_pass(k).start()
+
+    def along_second(self, k):
+        spot = self.spot
+        z = spot.arrival(k)
+        self.copy(self.block(z, spot.second_plane), 0, 8 + z, spot.second).wait_recv()
+        self.copy(self.block(z, spot.far_plane), 0, 12 + z, spot.second).wait_recv()
+        self.twin_copy(spot.core, k).start()
+
+    def last_along_first(self):
+        spot = self.spot
+        self.copy(self.last(spot.first_plane), 0, 20, spot.first).wait_recv()
+        self.last_second(True).start()
+
+    def last_along_second(self):
+        spot = self.spot
+        self.copy(self.last(spot.second_plane), 0, 21, spot.second).wait_recv()
+        self.copy(self.last(spot.far_plane), 0, 22, spot.second).wait_recv()
+        self.line.open()
+        self.last_twin(spot.core, 0).start()
+
+    def last_along_z(self, k):
+        self.line.take(k)
+        self.last_twin(self.spot.core, k).start()
+
+    def landed(self):
+        for k in range(4):
+            self.twin_copy(1 - self.spot.core, k).wait_recv()
+            self.last_twin(1 - self.spot.core, k).wait_recv()
+
+    def drain(self):
+        spot = self.spot
+        self.z_own(True).wait_send()
+
+        @pl.when(spot.is_middle)
+        def _():
+            self.z_own(False).wait_send()
+            for k in (1, 2, 3):
+                self.z_pass(k).wait_send()
+
+        for k in range(4):
+            self.first_copy(k).wait_send()
+            self.second_copy(k).wait_send()
+            self.second_pass(k).wait_send()
+            self.twin_copy(spot.core, k).wait_send()
+            self.last_twin(spot.core, k).wait_send()
+        self.last_first().wait_send()
+        self.last_second(False).wait_send()
+        self.last_second(True).wait_send()
+        self.line.drain()
+
+
 class Scatter:
     def __init__(
-        self, spot, sums, from_second, from_first, from_z, final, theirs, send, recv, credit, owed
+        self, spot, sums, from_second, from_first, from_z, last_pair, last_one, last_z, final,
+        theirs, send, recv, credit, owed,
     ):
         self.spot, self.sums = spot, sums
         self.from_second, self.from_first = from_second, from_first
+        self.last_pair, self.last_one = last_pair, last_one
         self.final, self.theirs = final, theirs
         self.send, self.recv, self.credit = send, recv, credit
         self.owed, self.whole = owed, theirs.shape[1] == 48
         self.line = LineSum(
             spot,
-            lambda z: sums.at[pl.ds(16 * z, 4)],
+            lambda z: sums.at[pl.ds(12 * z, 3)],
             lambda i: from_z.at[i],
             send.at[pl.ds(8, 3)],
             recv.at[pl.ds(8, 5)],
         )
-
-    def place(self, chip):
+        self.last_line = LineSum(
+            spot,
+            lambda z: sums.at[pl.ds(48 + 4 * z, 4)],
+            lambda i: last_z.at[i],
+            send.at[pl.ds(12, 3)],
+            recv.at[pl.ds(14, 5)],
+        )
+
+    def place(self, chip, chunk):
         spot = self.spot
         z, y, x = chip // 4, (chip // 2) % 2, chip % 2
         other_y, other_x = lax.rem(spot.y + y, 2), lax.rem(spot.x + x, 2)
         second = other_y * (1 - spot.core) + other_x * spot.core
         first = other_x * (1 - spot.core) + other_y * spot.core
-        return 16 * z + 8 * second + 4 * first
+        block = 4 * z + 2 * second + first
+        return 48 + block if chunk == 3 else 3 * block + chunk
 
     def second_copy(self, k):
         z = self.line.layer(k)
         return remote(
-            self.sums.at[pl.ds(16 * z + 8, 8)],
+            self.sums.at[pl.ds(12 * z + 6, 6)],
             self.from_second.at[z],
             self.send.at[k],
             self.recv.at[z],
@@ -442,10 +504,28 @@
     def first_copy(self, k):
         z = self.line.layer(k)
         return remote(
-            self.sums.at[pl.ds(16 * z + 4, 4)],
+            self.sums.at[pl.ds(12 * z + 3, 3)],
             self.from_first.at[z],
             self.send.at[4 + k],
             self.recv.at[4 + z],
+            self.spot.first,
+        )
+
+    def last_second_copy(self):
+        return remote(
+            self.sums.at[pl.ds(48 + 4 * self.spot.z + 2, 2)],
+            self.last_pair,
+            self.send.at[15],
+            self.recv.at[19],
+            self.spot.second,
+        )
+
+    def last_first_copy(self):
+        return remote(
+            self.sums.at[48 + 4 * self.spot.z + 1],
+            self.last_one,
+            self.send.at[16],
+            self.recv.at[20],
             self.spot.first,
         )
 
@@ -457,37 +537,56 @@
             src = self.final.at[:, pl.ds(pl.multiple_of((1 - core) * 24, 8), 24), :]
         return remote(src, self.theirs, self.send.at[11], self.recv.at[13], self.spot.twin)
 
-    def start(self):
+    def wait_credit(self):
         spot = self.spot
         if self.owed:
             for kind in range(3):
                 pl.semaphore_wait(self.credit.at[kind], 1)
             pl.when(spot.is_middle)(lambda: pl.semaphore_wait(self.credit.at[3], 1))
-        for k in range(4):
-            self.second_copy(k).start()
 
     def add_second(self, k):
         z = self.line.layer(k)
         self.second_copy(k).wait_recv()
-        for i in (4, 5, 6, 7, 0, 1, 2, 3):
-            self.sums[16 * z + i] += self.from_second[z, i]
-            if i == 7:
+        for i in (3, 4, 5, 0, 1, 2):
+            self.sums[12 * z + i] += self.from_second[z, i]
+            if i == 5:
                 self.first_copy(k).start()
 
     def add_first(self, k):
         z = self.line.layer(k)
         self.first_copy(k).wait_recv()
-        for i in range(4):
-            self.sums[16 * z + i] += self.from_first[z, i]
+        for i in range(3):
+            self.sums[12 * z + i] += self.from_first[z, i]
         if k < 3:
-            self.line.step(k)
+            self.line.send_end(k)
 
     def finish(self):
         def put(i, value):
             self.final[i] = value
 
         self.line.total(put)
-        self.swap().start()
+
+    def last_total(self):
+        at = 48 + 4 * self.spot.z
+
+        def put(i, value):
+            self.sums[at + i] = value.astype(jnp.bfloat16)
+
+        self.last_line.total(put)
+        self.last_second_copy().start()
+
+    def last_add_second(self):
+        at = 48 + 4 * self.spot.z
+        self.last_second_copy().wait_recv()
+        self.sums[at + 1] += self.last_pair[1]
+        self.last_first_copy().start()
+        self.sums[at] += self.last_pair[0]
+
+    def last_finish(self):
+        self.last_first_copy().wait_recv()
+        self.final[3] = self.sums[48 + 4 * self.spot.z].astype(jnp.float32) + self.last_one[
+            ...
+        ].astype(jnp.float32)
 
     def store(self, put):
         core = self.spot.core
@@ -500,12 +599,16 @@
         self.swap().wait_recv()
         for chunk in range(self.theirs.shape[0]):
             put(1 - core, chunk, self.theirs[chunk])
+        self.swap().wait_send()
 
     def drain(self):
         for k in range(4):
             self.second_copy(k).wait_send()
             self.first_copy(k).wait_send()
         self.line.drain()
+        self.last_line.drain()
+        self.last_second_copy().wait_send()
+        self.last_first_copy().wait_send()
 
     def release(self):
         spot, credit = self.spot, self.credit
@@ -526,64 +629,55 @@
             tell(2, spot.outer)
 
 
-class Plan:
-    def __init__(self):
-        self.clock, self.waiting, self.count = 0.0, [], 0
-
-    def at(self, time, action):
-        self.waiting.append((time, self.count, action))
-        self.count += 1
-
-    def flush(self):
-        while self.waiting:
-            first = min(self.waiting, key=lambda entry: entry[:2])
-            if first[0] > self.clock:
-                return
-            self.waiting.remove(first)
-            first[2]()
-
-    def run(self, cost, action):
-        self.flush()
-        action()
-        self.clock += cost
-
-    def until(self, time):
-        while self.waiting and min(entry[0] for entry in self.waiting) <= time:
-            self.clock = max(self.clock, min(entry[0] for entry in self.waiting))
-            self.flush()
-        self.clock = max(self.clock, time)
+ORDER = (
+    ("masks",), ("standardize", 0), ("steps", 0), ("own", 0), ("gs", 0, 0), ("steps", 1), ("own", 1), ("lx", 0),
+    ("gs", 1, 0), ("gz", 0, 1), ("gz", 0, 2), ("steps", 2), ("gx", 0, 0), ("lx", 1), ("ly", 0), ("gz", 1, 1),
+    ("gz", 1, 2), ("gs", 0, 1), ("stepp", 1), ("gz", 0, 3), ("gx", 1, 0), ("stepp", 2), ("stepz", 1), ("gy", 0, 0),
+    ("gs", 0, 2), ("lp", 0, 1), ("lp", 0, 2), ("gx", 0, 1), ("lz", 0, 1), ("gy", 1, 0), ("gs", 1, 1), ("gz", 1, 3),
+    ("stepp", 3), ("gx", 0, 2), ("gy", 0, 1), ("gs", 1, 2), ("stepz", 2), ("lp", 0, 3), ("gx", 1, 1), ("gy", 0, 2),
+    ("gs", 0, 3), ("lz", 0, 2), ("ly", 1), ("gx", 1, 2), ("gy", 1, 1), ("stepz", 3), ("cond",), ("modpart", 0),
+    ("lp", 1, 2), ("gx", 0, 3), ("lp", 1, 1), ("gs", 1, 3), ("lz", 0, 3), ("gy", 1, 2), ("modpart", 1), ("mode", 0),
+    ("mode", 1), ("mode", 2), ("gy", 0, 3), ("gx", 1, 3), ("lz", 1, 1), ("lp", 1, 3), ("gy", 1, 3), ("lz", 1, 2),
+    ("modz", 0), ("own", 2), ("gs", 2, 0), ("lx", 2), ("modz", 1), ("lz", 1, 3), ("modz", 2), ("gx", 2, 0),
+    ("own", 3), ("gs", 3, 0), ("gz", 2, 2), ("gy", 2, 0), ("lx", 3), ("gz", 2, 1), ("gs", 2, 1), ("modfirst",),
+    ("ly", 2), ("gz", 3, 1), ("gx", 3, 0), ("gz", 3, 2), ("gx", 2, 1), ("lp", 2, 1), ("gs", 2, 2), ("gz", 2, 3),
+    ("modsecond",), ("gy", 3, 0), ("lz", 2, 1), ("gy", 2, 1), ("gs", 3, 1), ("lp", 2, 2), ("gx", 2, 2), ("gz", 3, 3),
+    ("modrows",), ("gs", 3, 2), ("modulate", 0), ("gate", 2), ("ly", 3), ("lp", 2, 3), ("landed", 0), ("project", 0),
+    ("gx", 3, 1), ("gy", 2, 2), ("lz", 2, 2), ("gx", 3, 2), ("turnn", 0), ("gs", 2, 3), ("attend", 0, 0),
+    ("lp", 3, 1), ("lp", 3, 2), ("attend", 0, 1), ("gy", 3, 1), ("gy", 3, 2), ("lz", 3, 1), ("gs", 3, 3),
+    ("attend", 0, 2), ("gx", 2, 3), ("join", 0), ("lp", 3, 3), ("gx", 3, 3), ("add", 0), ("lz", 2, 3), ("turna", 0),
+    ("standardize", 1), ("modulate", 1), ("gy", 2, 3), ("landed", 1), ("project", 1), ("lz", 3, 2), ("gy", 3, 3),
+    ("turnn", 1), ("attend", 1, 0), ("lz", 3, 3), ("attend", 1, 1), ("attend", 1, 2), ("join", 1), ("add", 1),
+    ("turna", 1), ("standardize", 2), ("modulate", 2), ("turnn", 2), ("landed", 2), ("expand", 0), ("expand", 1),
+    ("expand", 2), ("expand", 3), ("sendh",), ("needh",), ("cwait", 0), ("downt", 0), ("downt", 1), ("downt", 2),
+    ("downt", 3), ("te", 0, 0), ("ss", 0, 0), ("landed", 3), ("ghid", 0), ("te", 0, 1), ("ss", 0, 1), ("ghid", 1),
+    ("ghid", 2), ("ghid", 3), ("te", 0, 2), ("ss", 0, 2), ("sendp",), ("sy", 0, 0), ("tz", 0, 0), ("sy", 0, 1),
+    ("needp",), ("cwait", 1), ("upt", 3), ("te", 1, 0), ("upt", 0), ("tz", 0, 1), ("ss", 0, 3), ("upt", 1),
+    ("sy", 0, 2), ("upt", 2), ("tz", 0, 2), ("contract",), ("sx", 0, 0), ("sx", 0, 1), ("ss", 1, 0), ("close",),
+    ("back2", 0), ("back2", 1), ("sy", 0, 3), ("ttot", 0), ("tz", 1, 0), ("sx", 0, 2), ("back2", 2), ("ss", 1, 1),
+    ("back2", 3), ("sz", 0, 0), ("normb", 2), ("sy", 1, 0), ("te", 1, 1), ("sx", 0, 3), ("gate", 1), ("ty", 0),
+    ("sz", 0, 1), ("split", 1), ("te", 1, 2), ("ss", 1, 2), ("attb", 1, 0), ("sy", 1, 1), ("sz", 0, 2),
+    ("attb", 1, 1), ("tx", 0), ("sx", 1, 0), ("tz", 1, 1), ("tz", 1, 2), ("ss", 1, 3), ("attb", 1, 2), ("sy", 1, 2),
+    ("sfin", 0), ("swap", 0), ("sx", 1, 1), ("sendq", 1), ("retire", 0), ("ttot", 1), ("sy", 1, 3), ("sz", 1, 0),
+    ("sx", 1, 2), ("cwait", 2), ("needq", 1), ("outt", 1), ("te", 2, 0), ("qkvt", 1, 0), ("ty", 1), ("qkvt", 1, 1),
+    ("sz", 1, 1), ("sx", 1, 3), ("qkvt", 1, 2), ("te", 2, 1), ("ss", 2, 0), ("back", 1, 0), ("tx", 1), ("sz", 1, 2),
+    ("ss", 2, 1), ("back", 1, 1), ("back", 1, 2), ("ss", 2, 2), ("normb", 1), ("te", 2, 2), ("sy", 2, 0),
+    ("tz", 2, 0), ("sentq", 1), ("gate", 0), ("sfin", 1), ("swap", 1), ("split", 0), ("sy", 2, 1), ("attb", 0, 0),
+    ("tz", 2, 1), ("ss", 2, 3), ("attb", 0, 1), ("sy", 2, 2), ("tz", 2, 2), ("sx", 2, 0), ("attb", 0, 2),
+    ("sx", 2, 1), ("sendq", 0), ("retire", 1), ("sy", 2, 3), ("sx", 2, 2), ("sz", 2, 0), ("cwait", 3), ("needq", 0),
+    ("outt", 0), ("ttot", 2), ("te", 3, 0), ("qkvt", 0, 0), ("sx", 2, 3), ("qkvt", 0, 1), ("sz", 2, 1),
+    ("qkvt", 0, 2), ("ty", 2), ("te", 3, 1), ("ss", 3, 0), ("back", 0, 0), ("sz", 2, 2), ("ss", 3, 1), ("back", 0, 1),
+    ("tx", 2), ("back", 0, 2), ("te", 3, 2), ("normb", 0), ("rows", 0), ("tz", 3, 0), ("sy", 3, 0), ("sfin", 2),
+    ("swap", 2), ("ss", 3, 2), ("sentq", 0), ("sy", 3, 1), ("tz", 3, 1), ("retire", 2), ("rows", 1), ("sx", 3, 0),
+    ("tz", 3, 2), ("ss", 3, 3), ("sy", 3, 2), ("sx", 3, 1), ("sz", 3, 0), ("rows", 2), ("ttot", 3), ("sy", 3, 3),
+    ("sz", 3, 1), ("sx", 3, 2), ("sz", 3, 2), ("ty", 3), ("rowp", 1), ("rowz", 1), ("rowp", 2), ("sx", 3, 3),
+    ("tx", 3), ("sfin", 3), ("swap", 3), ("retire", 3), ("rowz", 2), ("rowp", 3), ("rowz", 3), ("rowt",), ("ada", 0),
+    ("ada", 1),
+)
 
 
 def dot(left, right):
     return jnp.dot(left, right, preferred_element_type=jnp.float32)
-
-
-GATHER_STEPS = (
-    (2.5, "first", 0),
-    (2.6, "z", 1),
-    (4.0, "z", 2),
-    (5.0, "first", 1),
-    (5.5, "z", 3),
-    (6.0, "second", 0),
-    (7.0, "first", 2),
-    (8.0, "second", 1),
-    (9.0, "first", 3),
-    (10.5, "second", 2),
-    (13.0, "second", 3),
-)
-SCATTER_STEPS = (
-    (2.0, "second", 0),
-    (4.0, "second", 1),
-    (5.5, "first", 0),
-    (6.0, "second", 2),
-    (7.5, "first", 1),
-    (8.0, "second", 3),
-    (9.5, "first", 2),
-    (11.0, "first", 3),
-    (13.0, "finish", 0),
-)
-UNIT = 1.6
-GROUPS = ("spatial", "temporal", "up", "down")
 
 
 def layer_kernel(
@@ -618,9 +712,11 @@
     from_second,
     from_first,
     from_z,
+    last_pair,
+    last_one,
+    last_z,
     all_steps,
     cond,
-    mod_half,
     mod,
     tally,
     rows_mod,
@@ -705,6 +801,9 @@
             from_second.at[n % 2],
             from_first.at[n % 2],
             from_z.at[n % 2],
+            last_pair.at[n % 2],
+            last_one.at[n % 2],
+            last_z.at[n % 2],
             stage.at[3 - n],
             apart_down if n == 0 else apart.at[3 - n],
             scatter_send.at[n],
@@ -791,7 +890,7 @@
         flat = all_steps[...].reshape(256, 128)
         clip = lax.broadcasted_iota(jnp.int32, (64, 256), 0)
         column = lax.broadcasted_iota(jnp.int32, (64, 256), 1)
-        wanted = 8 * lax.shift_right_logical(clip, 1) + (clip & 1)
+        wanted = 64 * ((clip >> 3) & 3) + 16 * ((clip >> 1) & 3) + 8 * (clip >> 5) + (clip & 1)
         times = jnp.dot(
             (column == wanted).astype(f32),
             flat,
@@ -822,33 +921,32 @@
             (mod_out, mod_in, spot.twin),
             (mod_one, mod_first, spot.first),
             (mod_two, mod_second, spot.second),
-            (mod_half.at[core], mod_half.at[core], spot.twin),
         )[index]
         return remote(src, dst, mod_send.at[3 + index], mod_recv.at[5 + index], device)
 
-    def mod_partial(half, chunk):
-        columns = pl.ds(pl.multiple_of(half * 3456 + chunk * 384, 128), 384)
-        return dot(cond[:, :24], w_ada[:, columns]) + bias[:, columns]
+    def mod_partial(owner, chunk):
+        rows = cond[pl.ds(pl.multiple_of(32 * owner, 32), 32), :24]
+        left, right = (
+            dot(rows, w_ada[:, at : at + 384]) + bias[:, at : at + 384]
+            for at in (384 * chunk, 3456 + 384 * chunk)
+        )
+        for z in range(4):
+            part = slice(8 * z, 8 * z + 8)
+            yield 3 * z + chunk // 3, jnp.concatenate([left[part], right[part]], axis=0)
 
     def mod_twin():
         for chunk in range(9):
-            value = mod_partial(1 - core, chunk).astype(bf16)
-            for z in range(4):
-                mod_out[3 * z + chunk // 3, 16 * (chunk % 3) : 16 * (chunk % 3) + 16] = value[
-                    16 * z : 16 * z + 16
-                ]
+            rows = slice(16 * (chunk % 3), 16 * (chunk % 3) + 16)
+            for at, value in mod_partial(1 - core, chunk):
+                mod_out[at, rows] = value.astype(bf16)
         mod_copy(0).start()
 
     def mod_own():
         mod_copy(0).wait_recv()
         for chunk in range(9):
-            value = mod_partial(core, chunk)
             rows = slice(16 * (chunk % 3), 16 * (chunk % 3) + 16)
-            for z in range(4):
-                at = 3 * z + chunk // 3
-                mod_sum[at, rows] = (
-                    value[16 * z : 16 * z + 16] + mod_in[at, rows].astype(f32)
-                ).astype(bf16)
+            for at, value in mod_partial(core, chunk):
+                mod_sum[at, rows] = (value + mod_in[at, rows].astype(f32)).astype(bf16)
 
     def mod_along_first():
         def put(i, value):
@@ -863,32 +961,23 @@
             mod_two[i] = mod_one[i] + mod_first[i]
         mod_copy(2).start()
 
-    def mod_to_twin():
+    def mod_rows():
         mod_copy(2).wait_recv()
+        row = lax.broadcasted_iota(jnp.int32, (16, 384), 0)
         for chunk in range(9):
             at, rows = chunk // 3, slice(16 * (chunk % 3), 16 * (chunk % 3) + 16)
-            mod_half[core, :, 384 * chunk : 384 * chunk + 384] = mod_two[at, rows].astype(
-                f32
-            ) + mod_second[at, rows].astype(f32)
-        mod_copy(3).start()
-
-    def mod_rows():
-        remote(
-            mod_half.at[1 - core], mod_half.at[1 - core], mod_send.at[6], mod_recv.at[8], spot.twin
-        ).wait_recv()
-        row = lax.broadcasted_iota(jnp.int32, (16, 384), 0)
-        for clip in range(2):
-            chosen = row == 4 * spot.plane + 2 * core + clip
-            for chunk in range(18):
-                at = 384 * (chunk % 9)
-                value = mod_half[chunk // 9, :, at : at + 384]
-                mod[clip : clip + 1, 384 * chunk : 384 * chunk + 384] = jnp.sum(
-                    jnp.where(chosen, value, 0.0), axis=0, keepdims=True
-                )
+            value = mod_two[at, rows].astype(f32) + mod_second[at, rows].astype(f32)
+            for clip in range(2):
+                for half in range(2):
+                    chosen = row == 8 * half + 2 * spot.plane + clip
+                    column = 3456 * half + 384 * chunk
+                    mod[clip : clip + 1, column : column + 384] = jnp.sum(
+                        jnp.where(chosen, value, 0.0), axis=0, keepdims=True
+                    )
 
     def mod_drain():
         mod_line.drain()
-        for index in range(4):
+        for index in range(3):
             mod_copy(index).wait_send()
 
     row_line = LineGather(
@@ -900,61 +989,62 @@
 
     def row_copy(index):
         src, dst, device = (
-            (rows_mod.at[1], rows_mod.at[2], spot.twin),
-            (rows_mod.at[0], rows_mod.at[3], spot.first),
-            (rows_mod.at[5], rows_mod.at[4], spot.second),
+            (rows_mod.at[0], rows_mod.at[1], spot.first),
+            (rows_mod.at[2], rows_mod.at[3], spot.second),
             (all_rows_mod.at[core], all_rows_mod.at[core], spot.twin),
         )[index]
         return remote(src, dst, row_send.at[index], row_recv.at[index], device)
 
-    def row_value(half):
-        columns = pl.ds(pl.multiple_of(half * 3456, 128), 3456)
-        row = lax.broadcasted_iota(jnp.int32, (16, 3456), 0)
-        mine = 4 * spot.plane + 2 * core
-        value = jnp.where(row == mine, tally[0:1, columns], 0.0)
-        return jnp.where(row == mine + 1, tally[1:2, columns], value).astype(bf16)
-
-    def rows_open():
-        rows_mod[1] = row_value(1 - core)
+    def rows_first():
+        row = lax.broadcasted_iota(jnp.int32, (16, 384), 0)
+        for chunk in range(9):
+            value = 0.0
+            for clip in range(2):
+                for half in range(2):
+                    chosen = row == 8 * half + 2 * spot.plane + clip
+                    column = 3456 * half + 384 * chunk
+                    value += jnp.where(chosen, tally[clip : clip + 1, column : column + 384], 0.0)
+            rows_mod[0, :, 384 * chunk : 384 * chunk + 384] = value.astype(bf16)
         row_copy(0).start()
 
-    def rows_first():
+    def rows_second():
         row_copy(0).wait_recv()
-        rows_mod[0] = row_value(core) + rows_mod[2]
+        rows_mod[2] = rows_mod[0] + rows_mod[1]
         row_copy(1).start()
 
-    def rows_second():
+    def rows_z():
         row_copy(1).wait_recv()
-        rows_mod[5] = rows_mod[0] + rows_mod[3]
+        all_rows_mod[core, spot.z] = rows_mod[2] + rows_mod[3]
+        row_line.open()
+
+    def rows_twin():
         row_copy(2).start()
 
-    def rows_z():
-        row_copy(2).wait_recv()
-        all_rows_mod[core, spot.z] = rows_mod[5] + rows_mod[4]
-        row_line.open()
-
-    def rows_twin():
-        row_copy(3).start()
-
-    def ada_half(half):
+    def ada(owner):
+        rows = cond[pl.ds(pl.multiple_of(32 * owner, 32), 32), :]
         for chunk in range(9):
-            value = all_rows_mod[half, :, :, 384 * chunk : 384 * chunk + 384].reshape(64, 384)
-            columns = pl.ds(pl.multiple_of(half * 3456 + 384 * chunk, 128), 384)
-            o_ada[:, columns] = contract_rows(cond[...], value)[:24]
-            o_bias[:, columns] = jnp.sum(value.astype(f32), axis=0, keepdims=True)
-
-    def rows_last():
-        remote(
-            all_rows_mod.at[1 - core],
-            all_rows_mod.at[1 - core],
-            row_send.at[3],
-            row_recv.at[3],
-            spot.twin,
-        ).wait_recv()
-        ada_half(1 - core)
+            value = all_rows_mod[owner, :, :, 384 * chunk : 384 * chunk + 384].astype(f32)
+            for half in range(2):
+                part = value[:, 8 * half : 8 * half + 8].reshape(32, 384)
+                columns = slice(3456 * half + 384 * chunk, 3456 * half + 384 * chunk + 384)
+                product = contract_rows(rows, part.astype(bf16))[:24]
+                total = jnp.sum(part, axis=0, keepdims=True)
+                yield columns, product, total
+
+    def ada_own():
+        for columns, product, total in ada(core):
+            o_ada[:, columns] = product
+            o_bias[:, columns] = total
+
+    def ada_twin():
+        theirs = all_rows_mod.at[1 - core]
+        remote(theirs, theirs, row_send.at[2], row_recv.at[2], spot.twin).wait_recv()
+        for columns, product, total in ada(1 - core):
+            o_ada[:, columns] += product
+            o_bias[:, columns] += total
 
     def rows_drain():
-        for index in range(4):
+        for index in range(3):
             row_copy(index).wait_send()
         row_line.drain()
 
@@ -1083,22 +1173,22 @@
     def own_columns(first, width_of_half):
         return pl.ds(pl.multiple_of(core * width_of_half + first, 128), 384)
 
-    def down_terms(first, last):
+    def down_terms(z):
         scatter = scatters[0]
-        for z in range(first, last):
-            rows = slice(768 * z, 768 * z + 768)
-            value = dot(hidden_turned[0, rows], gated[2, :, own_columns(0, 384)]) + dot(
-                hidden_turned[1, rows], gated_twin[2]
-            )
-            value = value.astype(bf16).reshape(4, 4, 48, 384)
-            for plane in range(4):
-                sums[0, pl.ds(scatter.place(4 * z + plane), 4)] = value[plane]
+        rows = slice(768 * z, 768 * z + 768)
+        value = dot(hidden_turned[0, rows], gated[2, :, own_columns(0, 384)]) + dot(
+            hidden_turned[1, rows], gated_twin[2]
+        )
+        value = value.astype(bf16).reshape(4, 4, 48, 384)
+        for plane in range(4):
+            sums[0, pl.ds(scatter.place(4 * z + plane, 0), 3)] = value[plane, :3]
+            sums[0, scatter.place(4 * z + plane, 3)] = value[plane, 3]
 
     def column_terms(n, chunk, left, right, right_twin):
         value = dot(turned[left, 0], right) + dot(turned[left, 1], right_twin)
         value = value.astype(bf16).reshape(16, 48, 384)
         for chip in range(16):
-            sums[n % 2, scatters[n].place(chip) + chunk] = value[chip]
+            sums[n % 2, scatters[n].place(chip, chunk)] = value[chip]
 
     def up_terms(chunk):
         column_terms(
@@ -1208,151 +1298,125 @@
             grad_qkv[:, at_k] = grad_k.astype(bf16)
             grad_qkv[:, at_v] = grad_v.astype(bf16)
 
-    plan = Plan()
-    run = plan.run
+    def each_twin_copy():
+        for i in range(5):
+            yield turned_copy(i)
+        yield hidden_copy()
+        for j in range(3):
+            yield gated_copy(j)
+        yield grad_pre_copy()
+
+    def forward_drain():
+        steps_drain()
+        mod_drain()
+        for gather in gathers:
+            gather.swap().wait_send()
+
+    def send_hidden():
+        forward_drain()
+        hidden_copy().start()
+
+    def retire(n):
+        scatters[n].store(puts[n])
+        scatters[n].drain()
+        if n < 2:
+            scatters[n].release()
+
+    def swap(n):
+        scatters[n].swap().start()
+
+    def need(copy, *indices):
+        copy(*indices).wait_recv()
+
+    steps_of = {
+        "steps": (steps_first, steps_second, steps_z),
+        "stepp": step_line.pass_on,
+        "stepz": step_line.take,
+        "cond": make_cond,
+        "modpart": (mod_twin, mod_own),
+        "mode": mod_line.send_end,
+        "modz": mod_line.send_middle,
+        "modfirst": mod_along_first,
+        "modsecond": mod_along_second,
+        "modrows": mod_rows,
+        "own": lambda g: gathers[g].own(),
+        "gz": lambda g, k: gathers[g].pass_on(k),
+        "gs": lambda g, k: gathers[g].spread(k),
+        "gx": lambda g, k: gathers[g].along_first(k),
+        "gy": lambda g, k: gathers[g].along_second(k),
+        "lx": lambda g: gathers[g].last_along_first(),
+        "ly": lambda g: gathers[g].last_along_second(),
+        "lp": lambda g, k: gathers[g].line.pass_on(k),
+        "lz": lambda g, k: gathers[g].last_along_z(k),
+        "landed": lambda g: gathers[g].landed(),
+        "cwait": lambda n: scatters[n].wait_credit(),
+        "ss": lambda n, k: scatters[n].second_copy(k).start(),
+        "sy": lambda n, k: scatters[n].add_second(k),
+        "sx": lambda n, k: scatters[n].add_first(k),
+        "sz": lambda n, k: scatters[n].line.send_middle(k),
+        "sfin": lambda n: scatters[n].finish(),
+        "te": lambda n, k: scatters[n].last_line.send_end(k),
+        "tz": lambda n, k: scatters[n].last_line.send_middle(k),
+        "ttot": lambda n: scatters[n].last_total(),
+        "ty": lambda n: scatters[n].last_add_second(),
+        "tx": lambda n: scatters[n].last_finish(),
+        "swap": swap,
+        "retire": retire,
+        "rows": (rows_first, rows_second, rows_z),
+        "rowp": row_line.pass_on,
+        "rowz": row_line.take,
+        "rowt": rows_twin,
+        "ada": (ada_own, ada_twin),
+        "masks": masks,
+        "standardize": standardize,
+        "modulate": modulate,
+        "project": project,
+        "turnn": lambda j: turn(2 * j, normed),
+        "turna": lambda j: turn(2 * j + 1, attended),
+        "attend": lambda j, i: attend(j, 2 * i, 2 * i + 2),
+        "join": join,
+        "add": add_branch,
+        "gate": gate,
+        "expand": lambda i: expand(2 * i, 2 * i + 2),
+        "sendh": send_hidden,
+        "needh": lambda: (need(gated_copy, 2), need(hidden_copy)),
+        "downt": down_terms,
+        "ghid": lambda i: grad_hidden(2 * i, 2 * i + 2),
+        "sendp": lambda: grad_pre_copy().start(),
+        "contract": contract,
+        "close": close,
+        "needp": lambda: (need(grad_pre_copy), need(turned_copy, 4)),
+        "upt": up_terms,
+        "back2": lambda i: back_project(2, 4, slope, 2 * i, 2 * i + 2),
+        "normb": norm_back,
+        "split": split,
+        "attb": lambda j, i: attend_back(j, 2 * i, 2 * i + 2),
+        "sendq": lambda j: grad_qkv_copy(j).start(),
+        "needq": lambda j: (
+            need(turned_copy, 2 * j + 1),
+            need(gated_copy, j),
+            need(turned_copy, 2 * j),
+            need(grad_qkv_copy, j),
+        ),
+        "outt": out_terms,
+        "qkvt": qkv_terms,
+        "back": lambda j, i: back_project(j, 3, grad_qkv, 2 * i, 2 * i + 2),
+        "sentq": lambda j: grad_qkv_copy(j).wait_send(),
+    }
     for g, gather in enumerate(gathers):
         gather.open(pieces[g])
-        begin = 1.0 + 12 * UNIT * g
-        plan.at(begin - (2 * UNIT if g else 0.5), gather.own)
-        kinds = {"z": gather.along_z, "first": gather.along_first, "second": gather.along_second}
-        for at, kind, k in GATHER_STEPS:
-            plan.at(begin + at * UNIT, partial(kinds[kind], k))
-
-    def landed(g):
-        plan.until(2.0 + UNIT * (12 * g + 14.5))
-        gathers[g].landed()
-
     steps_open()
-    plan.at(2.0, steps_first)
-    plan.at(4.0, steps_second)
-    plan.at(6.0, steps_z)
-    for k in (1, 2, 3):
-        plan.at(6.0 + 2 * k, partial(step_line.step, k))
-    plan.at(12.1, make_cond)
-    plan.at(12.5, mod_twin)
-    plan.at(14.5, mod_own)
-    plan.at(15.5, lambda: mod_line.step(0))
-    plan.at(16.5, lambda: mod_line.step(1))
-    plan.at(20.0, lambda: mod_line.step(2))
-    plan.at(25.0, mod_along_first)
-    plan.at(28.5, mod_along_second)
-    plan.at(32.0, mod_to_twin)
-
-    run(1.0, masks)
-    run(1.0, lambda: standardize(0))
-    plan.until(34.0)
-    mod_rows()
-    landed(0)
-    for j in range(2):
-        if j:
-            run(1.0, lambda: standardize(1))
-            landed(1)
-        run(1.0, lambda: modulate(j))
-        run(2.0, lambda: project(j))
-        run(0.5, lambda: turn(2 * j, normed))
-        for pair in range(0, 6, 2):
-            run(1.5, lambda: attend(j, pair, pair + 2))
-        run(0.7, lambda: join(j))
-        run(0.5, lambda: add_branch(j))
-        run(0.5, lambda: turn(2 * j + 1, attended))
-    run(1.0, lambda: standardize(2))
-    run(1.0, lambda: modulate(2))
-    run(0.5, lambda: turn(4, normed))
-    run(1.0, lambda: gate(2))
-    landed(2)
-    for i in range(0, 8, 2):
-        run(1.2, lambda: expand(i, i + 2))
-    steps_drain()
-    mod_drain()
-    for gather in gathers:
-        gather.swap().wait_send()
-    run(0.0, lambda: hidden_copy().start())
-
-    link = [0.0]
-
-    def begin_scatter(n):
-        scatters[n].start()
-        begin = max(plan.clock, link[0])
-        link[0] = begin + 12 * UNIT
-        kinds = {"second": scatters[n].add_second, "first": scatters[n].add_first}
-        for at, kind, k in SCATTER_STEPS:
-            action = scatters[n].finish if kind == "finish" else partial(kinds[kind], k)
-            plan.at(begin + at * UNIT, action)
-        return begin + 13 * UNIT + 0.1
-
-    plan.until(plan.clock + 2.0)
-    gated_copy(2).wait_recv()
-    hidden_copy().wait_recv()
-    for z in range(4):
-        run(0.7, lambda: down_terms(z, z + 1))
-    ends = [begin_scatter(0)]
-    landed(3)
-    for i in range(0, 8, 2):
-        run(0.6, lambda: grad_hidden(i, i + 2))
-    run(0.0, lambda: grad_pre_copy().start())
-    run(2.0, contract)
-    run(1.0, close)
-    plan.flush()
-    grad_pre_copy().wait_recv()
-    turned_copy(4).wait_recv()
-    for chunk in range(4):
-        run(0.7, lambda: up_terms(chunk))
-    ends.append(begin_scatter(1))
-    for i in range(0, 8, 2):
-        run(0.7, lambda: back_project(2, 4, slope, i, i + 2))
-    run(1.5, lambda: norm_back(2))
-
-    def retire(n):
-        scatters[n].drain()
-        scatters[n].store(puts[n])
-        scatters[n].swap().wait_send()
-        if n < 2:
-            scatters[n].release()
-
-    for j in (1, 0):
-        n = 3 - j
-        run(1.0, lambda: gate(j))
-        run(1.0, lambda: split(j))
-        for pair in range(0, 6, 2):
-            run(2.5, lambda: attend_back(j, pair, pair + 2))
-        run(0.0, lambda: grad_qkv_copy(j).start())
-        plan.until(ends[n - 2])
-        retire(n - 2)
-        turned_copy(2 * j + 1).wait_recv()
-        gated_copy(j).wait_recv()
-        run(0.7, lambda: out_terms(j))
-        turned_copy(2 * j).wait_recv()
-        grad_qkv_copy(j).wait_recv()
-        for chunk in range(3):
-            run(0.7, lambda: qkv_terms(j, chunk))
-        ends.append(begin_scatter(n))
-        for i in range(0, 6, 2):
-            run(0.7, lambda: back_project(j, 3, grad_qkv, i, i + 2))
-        run(1.5, lambda: norm_back(j))
-        grad_qkv_copy(j).wait_send()
-    now = plan.clock
-    plan.at(now, rows_open)
-    plan.at(now + 2.0, rows_first)
-    plan.at(now + 5.0, rows_second)
-    plan.at(now + 8.0, rows_z)
-    plan.at(now + 11.0, lambda: row_line.step(1))
-    plan.at(now + 14.0, lambda: row_line.step(2))
-    plan.at(now + 17.0, lambda: row_line.step(3))
-    plan.at(now + 17.1, rows_twin)
-    plan.at(now + 17.2, lambda: ada_half(core))
-    plan.at(now + 18.5, rows_last)
-    plan.at(ends[2], lambda: retire(2))
-    plan.until(1e6)
-    retire(3)
+    for name, *indices in ORDER:
+        step = steps_of[name]
+        if isinstance(step, tuple):
+            step[indices[0]]()
+        else:
+            step(*indices)
     rows_drain()
     for gather in gathers:
         gather.drain()
-    for i in range(5):
-        turned_copy(i).wait_send()
-    hidden_copy().wait_send()
-    for j in range(3):
-        gated_copy(j).wait_send()
-    grad_pre_copy().wait_send()
+    for copy in each_twin_copy():
+        copy.wait_send()
 
 
 def layer(tokens, cotangent, ids_row, ids_col, steps, bias, w_ada, *shards):
@@ -1377,15 +1441,17 @@
             vmem((3, 4, 24, 384), f32),
             vmem((2, 48, 384), f32),
             vmem((2, 64, 48, 384), bf16),
-            vmem((2, 4, 8, 48, 384), bf16),
-            vmem((2, 4) + block, bf16),
+            vmem((2, 4, 6, 48, 384), bf16),
+            vmem((2, 4, 3, 48, 384), bf16),
+            vmem((2, 5, 3, 48, 384), bf16),
+            vmem((2, 2, 48, 384), bf16),
+            vmem((2, 48, 384), bf16),
             vmem((2, 5) + block, bf16),
             vmem((4, 4, 2, 8, 128), f32),
             vmem((64, 128), bf16),
-            vmem((2, 16, 3456), f32),
             vmem((8, 6912), f32),
             vmem((8, 6912), f32),
-            vmem((6, 16, 3456), bf16),
+            vmem((4, 16, 3456), bf16),
             vmem((2, 4, 16, 3456), bf16),
             vmem((3, tok, width), bf16),
             vmem((tok, 128), f32),
@@ -1407,17 +1473,17 @@
             vmem((2, tok, 3 * width // 2), bf16),
             vmem((2, tok, tok), f32),
             dma((4, 2)),
+            dma((4, 33)),
+            dma((4, 31)),
+            dma((4, 17)),
             dma((4, 21)),
-            dma((4, 20)),
-            dma((4, 12)),
-            dma((4, 14)),
             pltpu.SemaphoreType.REGULAR((2, 4)),
             dma((12,)),
             dma((12,)),
             dma((9,)),
             dma((8,)),
-            dma((7,)),
-            dma((9,)),
+            dma((6,)),
+            dma((8,)),
             dma((9,)),
             dma((8,)),
         ],

time: 249 us -> 213 us (0.86); the launches traced: 246 us -> 212 us
  Pallas kernels: 231 us -> 197 us
    pallas_call x1, Pallas kernels: 231 us -> 197 us  [layer(): pl.pallas_call(layer_kernel, out_shape=[jax.ShapeDtypeStruct((tok, width)...]
where the time goes in v4:
time: 213 us; the launch traced here: 212 us
  Pallas kernels  197 us (92%)
  local copies, waits for them, and re-layouts  14.2 us (7%)
    pallas_call x1, Pallas kernels, layer(): pl.pallas_call(layer_kernel, out_shape=[jax.ShapeDtypeStruct((tok, width)...  197 us
    unnamed x39, local copies, waits for them, and re-layouts  11.2 us

profile of v4, /device:TPU:0, one launch (start us, length us, event | category | flops | bytes accessed | tf_op | source)
XLA Modules:
  0.0 212.4 jit_solution(12920231732705787608)
XLA Ops:
  0.6 0.0 copy-start.13
  0.7 0.6 copy-done.13
  1.3 0.6 copy-done.14
  2.0 0.7 copy-done.11
  2.6 0.0 copy-done.12
  2.7 0.0 copy-done.10
  2.7 0.7 broadcast_in_dim.15.steps
  3.4 0.2 dynamic_update_slice.3.bias
  3.6 0.0 copy-done.9
  3.6 0.0 copy-start.6
  3.6 0.8 copy.29
  4.4 0.0 copy-done.6
  4.4 197.5 %shard_map.213 = (bf16[256,768]{1,0:T(8,128)(2,1)}, f32[256,768]{1,0:T(8,128)}, f32[24,6912]{1,0:T(8,128)}, f32[1,6912]{1,0:T(1,128)}, f32[24,2304]{1,0:T(8,128)...) custom-call(bf16[256,768]{1,0:T(8,128)(2,1)} %tokens.1, ...), custom_call_target="tpu_custom_call" | custom-call | tf_op jit(solution)/shard_map/pallas_call | solution.py:1427
  201.8 0.0 copy-start
  201.9 1.4 constant_dynamic-slice_fusion
  203.2 1.8 copy.40
  205.0 0.0 copy-done
  205.0 0.9 copy.41
  205.9 0.5 copy-done.1
  206.4 0.8 copy.42
  207.2 0.3 copy-done.5
  207.5 0.7 copy.43
  208.2 0.2 copy-done.8
  208.4 0.6 copy.44
  209.1 0.0 copy-done.4
  209.1 0.7 copy.45
  209.8 0.2 copy-done.7
  210.0 0.6 copy.46
  210.6 0.0 copy-done.3
  210.6 0.7 copy.47
  211.3 0.4 copy-done.2
  211.7 0.7 copy.48
  (18 shorter events, 0.1 us)
Async XLA Ops:
  0.6 0.7 copy-start.13
  1.3 0.7 copy-start.14
  2.0 0.7 copy-start.11
  2.0 0.7 copy-start.12
  2.0 0.7 copy-start.10
  2.7 0.9 copy-start.9
  3.6 0.8 copy-start.6
  201.8 3.2 %copy-start = (f32[256,768]{1,0:T(8,128)S(1)}, f32[256,768]{1,0:T(8,128)}, u32[]{:S(2)}) copy-start(f32[256,768]{1,0:T(8,128)} %get-tuple-element.43) | copy-start | bytes 2359300
  205.0 1.4 copy-start.1
  206.4 1.1 copy-start.5
  207.5 0.9 copy-start.8
  207.5 1.5 copy-start.4
  209.1 0.9 copy-start.7
  209.1 1.5 copy-start.3
  210.6 1.1 copy-start.2

commit v5 on v4

--- a/solution.py
+++ b/solution.py
@@ -155,7 +155,16 @@
         self.far_plane = 3 - self.plane
         self.first = (z * 4 + self.first_plane, core)
         self.second = (z * 4 + self.second_plane, core)
+        self.far = (z * 4 + self.far_plane, core)
         self.twin = (chip, 1 - core)
+        self.mates = (
+            (self.first_plane, self.first),
+            (self.second_plane, self.second),
+            (self.far_plane, self.far),
+        )
+        self.line = [
+            (lax.rem(z + j, 4), (lax.rem(z + j, 4) * 4 + self.plane, core)) for j in (1, 2, 3)
+        ]
 
     def layer(self, mirrored):
         return mirrored + self.half * (3 - 2 * mirrored)
@@ -166,17 +175,9 @@
 
 def greet(spot):
     barrier = pltpu.get_barrier_semaphore()
-    for device in (spot.twin, spot.inner, spot.first, spot.second):
+    for device in [spot.twin] + [device for _, device in spot.mates + tuple(spot.line)]:
         pl.semaphore_signal(barrier, inc=1, device_id=device, device_id_type=MESH)
-
-    @pl.when(spot.is_middle)
-    def _():
-        pl.semaphore_signal(barrier, inc=1, device_id=spot.outer, device_id_type=MESH)
-        pl.semaphore_wait(barrier, 5)
-
-    @pl.when(spot.is_end)
-    def _():
-        pl.semaphore_wait(barrier, 4)
+    pl.semaphore_wait(barrier, 7)
 
 
 def remote(src, dst, send, recv, device):
@@ -188,6 +189,32 @@
         device_id=device,
         device_id_type=MESH,
     )
+
+
+class Exchange:
+    def __init__(self, places, mine, src, dst, send, recv):
+        self.places, self.mine = places, mine
+        self.src, self.dst = src, dst
+        self.send, self.recv = send, recv
+
+    def copy(self, i):
+        place, device = self.places[i]
+        return remote(
+            self.src(place), self.dst(self.mine), self.send.at[i], self.recv.at[self.mine], device
+        )
+
+    def start(self):
+        for i in range(3):
+            self.copy(i).start()
+
+    def arrive(self):
+        for place, device in self.places:
+            ref = self.dst(place)
+            remote(ref, ref, self.send.at[0], self.recv.at[place], device).wait_recv()
+
+    def drain(self):
+        for i in range(3):
+            self.copy(i).wait_send()
 
 
 class LineSum:
@@ -629,50 +656,63 @@
             tell(2, spot.outer)
 
 
+(
+    DO_STEPS, DO_COND, DO_MODT, DO_MODZ, DO_MODM, DO_MODROWS, DO_OWN, DO_GZ, DO_GS, DO_GX, DO_GY,
+    DO_LX, DO_LY, DO_LP, DO_LZ, DO_LANDED, DO_CWAIT, DO_SS, DO_SY, DO_SX, DO_SZ, DO_SFIN, DO_TE,
+    DO_TZ, DO_TTOT, DO_TY, DO_TX, DO_SWAP, DO_RETIRE, DO_ROWM, DO_ROWZ, DO_ROWT, DO_ROWD, DO_MASKS,
+    DO_STANDARDIZE, DO_MODULATE, DO_PROJECT, DO_TURNN, DO_TURNA, DO_ATTEND, DO_JOIN, DO_ADD,
+    DO_GATE, DO_EXPAND, DO_SENDH, DO_NEEDH, DO_DOWNT, DO_GHID, DO_SENDP, DO_CONTRACT, DO_CLOSE,
+    DO_NEEDP, DO_UPT, DO_BACK2, DO_NORMB, DO_SPLIT, DO_ATTB, DO_SENDQ, DO_NEEDG, DO_NEEDQ, DO_OUTT,
+    DO_QKVT, DO_BACK, DO_SENTQ,
+) = range(64)
+
 ORDER = (
-    ("masks",), ("standardize", 0), ("steps", 0), ("own", 0), ("gs", 0, 0), ("steps", 1), ("own", 1), ("lx", 0),
-    ("gs", 1, 0), ("gz", 0, 1), ("gz", 0, 2), ("steps", 2), ("gx", 0, 0), ("lx", 1), ("ly", 0), ("gz", 1, 1),
-    ("gz", 1, 2), ("gs", 0, 1), ("stepp", 1), ("gz", 0, 3), ("gx", 1, 0), ("stepp", 2), ("stepz", 1), ("gy", 0, 0),
-    ("gs", 0, 2), ("lp", 0, 1), ("lp", 0, 2), ("gx", 0, 1), ("lz", 0, 1), ("gy", 1, 0), ("gs", 1, 1), ("gz", 1, 3),
-    ("stepp", 3), ("gx", 0, 2), ("gy", 0, 1), ("gs", 1, 2), ("stepz", 2), ("lp", 0, 3), ("gx", 1, 1), ("gy", 0, 2),
-    ("gs", 0, 3), ("lz", 0, 2), ("ly", 1), ("gx", 1, 2), ("gy", 1, 1), ("stepz", 3), ("cond",), ("modpart", 0),
-    ("lp", 1, 2), ("gx", 0, 3), ("lp", 1, 1), ("gs", 1, 3), ("lz", 0, 3), ("gy", 1, 2), ("modpart", 1), ("mode", 0),
-    ("mode", 1), ("mode", 2), ("gy", 0, 3), ("gx", 1, 3), ("lz", 1, 1), ("lp", 1, 3), ("gy", 1, 3), ("lz", 1, 2),
-    ("modz", 0), ("own", 2), ("gs", 2, 0), ("lx", 2), ("modz", 1), ("lz", 1, 3), ("modz", 2), ("gx", 2, 0),
-    ("own", 3), ("gs", 3, 0), ("gz", 2, 2), ("gy", 2, 0), ("lx", 3), ("gz", 2, 1), ("gs", 2, 1), ("modfirst",),
-    ("ly", 2), ("gz", 3, 1), ("gx", 3, 0), ("gz", 3, 2), ("gx", 2, 1), ("lp", 2, 1), ("gs", 2, 2), ("gz", 2, 3),
-    ("modsecond",), ("gy", 3, 0), ("lz", 2, 1), ("gy", 2, 1), ("gs", 3, 1), ("lp", 2, 2), ("gx", 2, 2), ("gz", 3, 3),
-    ("modrows",), ("gs", 3, 2), ("modulate", 0), ("gate", 2), ("ly", 3), ("lp", 2, 3), ("landed", 0), ("project", 0),
-    ("gx", 3, 1), ("gy", 2, 2), ("lz", 2, 2), ("gx", 3, 2), ("turnn", 0), ("gs", 2, 3), ("attend", 0, 0),
-    ("lp", 3, 1), ("lp", 3, 2), ("attend", 0, 1), ("gy", 3, 1), ("gy", 3, 2), ("lz", 3, 1), ("gs", 3, 3),
-    ("attend", 0, 2), ("gx", 2, 3), ("join", 0), ("lp", 3, 3), ("gx", 3, 3), ("add", 0), ("lz", 2, 3), ("turna", 0),
-    ("standardize", 1), ("modulate", 1), ("gy", 2, 3), ("landed", 1), ("project", 1), ("lz", 3, 2), ("gy", 3, 3),
-    ("turnn", 1), ("attend", 1, 0), ("lz", 3, 3), ("attend", 1, 1), ("attend", 1, 2), ("join", 1), ("add", 1),
-    ("turna", 1), ("standardize", 2), ("modulate", 2), ("turnn", 2), ("landed", 2), ("expand", 0), ("expand", 1),
-    ("expand", 2), ("expand", 3), ("sendh",), ("needh",), ("cwait", 0), ("downt", 0), ("downt", 1), ("downt", 2),
-    ("downt", 3), ("te", 0, 0), ("ss", 0, 0), ("landed", 3), ("ghid", 0), ("te", 0, 1), ("ss", 0, 1), ("ghid", 1),
-    ("ghid", 2), ("ghid", 3), ("te", 0, 2), ("ss", 0, 2), ("sendp",), ("sy", 0, 0), ("tz", 0, 0), ("sy", 0, 1),
-    ("needp",), ("cwait", 1), ("upt", 3), ("te", 1, 0), ("upt", 0), ("tz", 0, 1), ("ss", 0, 3), ("upt", 1),
-    ("sy", 0, 2), ("upt", 2), ("tz", 0, 2), ("contract",), ("sx", 0, 0), ("sx", 0, 1), ("ss", 1, 0), ("close",),
-    ("back2", 0), ("back2", 1), ("sy", 0, 3), ("ttot", 0), ("tz", 1, 0), ("sx", 0, 2), ("back2", 2), ("ss", 1, 1),
-    ("back2", 3), ("sz", 0, 0), ("normb", 2), ("sy", 1, 0), ("te", 1, 1), ("sx", 0, 3), ("gate", 1), ("ty", 0),
-    ("sz", 0, 1), ("split", 1), ("te", 1, 2), ("ss", 1, 2), ("attb", 1, 0), ("sy", 1, 1), ("sz", 0, 2),
-    ("attb", 1, 1), ("tx", 0), ("sx", 1, 0), ("tz", 1, 1), ("tz", 1, 2), ("ss", 1, 3), ("attb", 1, 2), ("sy", 1, 2),
-    ("sfin", 0), ("swap", 0), ("sx", 1, 1), ("sendq", 1), ("retire", 0), ("ttot", 1), ("sy", 1, 3), ("sz", 1, 0),
-    ("sx", 1, 2), ("cwait", 2), ("needq", 1), ("outt", 1), ("te", 2, 0), ("qkvt", 1, 0), ("ty", 1), ("qkvt", 1, 1),
-    ("sz", 1, 1), ("sx", 1, 3), ("qkvt", 1, 2), ("te", 2, 1), ("ss", 2, 0), ("back", 1, 0), ("tx", 1), ("sz", 1, 2),
-    ("ss", 2, 1), ("back", 1, 1), ("back", 1, 2), ("ss", 2, 2), ("normb", 1), ("te", 2, 2), ("sy", 2, 0),
-    ("tz", 2, 0), ("sentq", 1), ("gate", 0), ("sfin", 1), ("swap", 1), ("split", 0), ("sy", 2, 1), ("attb", 0, 0),
-    ("tz", 2, 1), ("ss", 2, 3), ("attb", 0, 1), ("sy", 2, 2), ("tz", 2, 2), ("sx", 2, 0), ("attb", 0, 2),
-    ("sx", 2, 1), ("sendq", 0), ("retire", 1), ("sy", 2, 3), ("sx", 2, 2), ("sz", 2, 0), ("cwait", 3), ("needq", 0),
-    ("outt", 0), ("ttot", 2), ("te", 3, 0), ("qkvt", 0, 0), ("sx", 2, 3), ("qkvt", 0, 1), ("sz", 2, 1),
-    ("qkvt", 0, 2), ("ty", 2), ("te", 3, 1), ("ss", 3, 0), ("back", 0, 0), ("sz", 2, 2), ("ss", 3, 1), ("back", 0, 1),
-    ("tx", 2), ("back", 0, 2), ("te", 3, 2), ("normb", 0), ("rows", 0), ("tz", 3, 0), ("sy", 3, 0), ("sfin", 2),
-    ("swap", 2), ("ss", 3, 2), ("sentq", 0), ("sy", 3, 1), ("tz", 3, 1), ("retire", 2), ("rows", 1), ("sx", 3, 0),
-    ("tz", 3, 2), ("ss", 3, 3), ("sy", 3, 2), ("sx", 3, 1), ("sz", 3, 0), ("rows", 2), ("ttot", 3), ("sy", 3, 3),
-    ("sz", 3, 1), ("sx", 3, 2), ("sz", 3, 2), ("ty", 3), ("rowp", 1), ("rowz", 1), ("rowp", 2), ("sx", 3, 3),
-    ("tx", 3), ("sfin", 3), ("swap", 3), ("retire", 3), ("rowz", 2), ("rowp", 3), ("rowz", 3), ("rowt",), ("ada", 0),
-    ("ada", 1),
+    (DO_MASKS,), (DO_STANDARDIZE, 0), (DO_STEPS, 0), (DO_OWN, 0), (DO_GS, 0, 0), (DO_OWN, 1), (DO_GS, 1, 0),
+    (DO_STEPS, 1), (DO_LX, 0), (DO_GZ, 0, 1), (DO_GZ, 0, 2), (DO_GX, 0, 0), (DO_LX, 1), (DO_GZ, 1, 1), (DO_GZ, 1, 2),
+    (DO_GS, 0, 1), (DO_GZ, 0, 3), (DO_LY, 0), (DO_COND,), (DO_MODT, 0), (DO_MODT, 1), (DO_MODZ, 0), (DO_GX, 0, 1),
+    (DO_GZ, 1, 3), (DO_GY, 0, 0), (DO_GX, 1, 0), (DO_MODZ, 1), (DO_GS, 0, 2), (DO_LP, 0, 1), (DO_LP, 0, 2),
+    (DO_GS, 0, 3), (DO_GY, 0, 1), (DO_LZ, 0, 1), (DO_GY, 1, 0), (DO_GS, 1, 1), (DO_MODM, 0), (DO_GX, 0, 2),
+    (DO_GX, 0, 3), (DO_GX, 1, 1), (DO_LY, 1), (DO_MODROWS, 0), (DO_GS, 1, 2), (DO_MODULATE, 0), (DO_MODM, 1),
+    (DO_GY, 0, 2), (DO_LP, 0, 3), (DO_GY, 0, 3), (DO_LZ, 0, 2), (DO_GS, 1, 3), (DO_GY, 1, 1), (DO_LP, 1, 1),
+    (DO_LP, 1, 2), (DO_GX, 1, 2), (DO_LZ, 1, 1), (DO_OWN, 2), (DO_MODROWS, 1), (DO_GS, 2, 0), (DO_LZ, 0, 3),
+    (DO_LP, 1, 3), (DO_GX, 1, 3), (DO_LANDED, 0), (DO_PROJECT, 0), (DO_LX, 2), (DO_GY, 1, 2), (DO_LZ, 1, 2),
+    (DO_TURNN, 0), (DO_GZ, 2, 1), (DO_GZ, 2, 2), (DO_ATTEND, 0, 0), (DO_GX, 2, 0), (DO_ATTEND, 0, 1), (DO_GS, 2, 1),
+    (DO_GY, 1, 3), (DO_LY, 2), (DO_ATTEND, 0, 2), (DO_GZ, 2, 3), (DO_LZ, 1, 3), (DO_GY, 2, 0), (DO_JOIN, 0),
+    (DO_GS, 2, 2), (DO_ADD, 0), (DO_TURNA, 0), (DO_STANDARDIZE, 1), (DO_GX, 2, 1), (DO_MODULATE, 1), (DO_GATE, 2),
+    (DO_LP, 2, 1), (DO_LP, 2, 2), (DO_LZ, 2, 1), (DO_LANDED, 1), (DO_PROJECT, 1), (DO_GX, 2, 2), (DO_TURNN, 1),
+    (DO_GS, 2, 3), (DO_GY, 2, 1), (DO_ATTEND, 1, 0), (DO_OWN, 3), (DO_ATTEND, 1, 1), (DO_LP, 2, 3), (DO_GS, 3, 0),
+    (DO_GY, 2, 2), (DO_LZ, 2, 2), (DO_ATTEND, 1, 2), (DO_LX, 3), (DO_GX, 2, 3), (DO_JOIN, 1), (DO_GZ, 3, 1),
+    (DO_GZ, 3, 2), (DO_GS, 3, 1), (DO_ADD, 1), (DO_TURNA, 1), (DO_STANDARDIZE, 2), (DO_MODULATE, 2), (DO_GX, 3, 0),
+    (DO_LY, 3), (DO_TURNN, 2), (DO_LZ, 2, 3), (DO_GY, 2, 3), (DO_GZ, 3, 3), (DO_GX, 3, 1), (DO_GS, 3, 2),
+    (DO_LANDED, 2), (DO_EXPAND, 0), (DO_GY, 3, 0), (DO_SENDH, 0), (DO_EXPAND, 1), (DO_LP, 3, 1), (DO_LP, 3, 2),
+    (DO_LZ, 3, 1), (DO_SENDH, 1), (DO_EXPAND, 2), (DO_GY, 3, 1), (DO_SENDH, 2), (DO_GX, 3, 2), (DO_EXPAND, 3),
+    (DO_GS, 3, 3), (DO_SENDH, 3), (DO_CWAIT, 0), (DO_NEEDH, 0), (DO_DOWNT, 0), (DO_NEEDH, 1), (DO_DOWNT, 1),
+    (DO_NEEDH, 2), (DO_DOWNT, 2), (DO_LP, 3, 3), (DO_GY, 3, 2), (DO_LZ, 3, 2), (DO_NEEDH, 3), (DO_DOWNT, 3),
+    (DO_SS, 0, 0), (DO_TE, 0, 0), (DO_GX, 3, 3), (DO_TE, 0, 1), (DO_SS, 0, 1), (DO_TE, 0, 2), (DO_LZ, 3, 3),
+    (DO_SY, 0, 0), (DO_SS, 0, 2), (DO_TZ, 0, 0), (DO_GY, 3, 3), (DO_LANDED, 3), (DO_GHID, 0), (DO_GHID, 1),
+    (DO_TZ, 0, 1), (DO_SY, 0, 1), (DO_SENDP,), (DO_GHID, 2), (DO_SX, 0, 0), (DO_SS, 0, 3), (DO_GHID, 3),
+    (DO_TZ, 0, 2), (DO_NEEDP,), (DO_CWAIT, 1), (DO_SY, 0, 2), (DO_UPT, 3), (DO_UPT, 0), (DO_TE, 1, 0), (DO_SX, 0, 1),
+    (DO_UPT, 1), (DO_UPT, 2), (DO_SS, 1, 0), (DO_CONTRACT,), (DO_SZ, 0, 0), (DO_SX, 0, 2), (DO_SY, 0, 3), (DO_CLOSE,),
+    (DO_TTOT, 0), (DO_SS, 1, 1), (DO_BACK2, 0), (DO_TZ, 1, 0), (DO_BACK2, 1), (DO_SY, 1, 0), (DO_BACK2, 2),
+    (DO_TE, 1, 1), (DO_SX, 0, 3), (DO_SZ, 0, 1), (DO_SZ, 0, 2), (DO_TY, 0), (DO_SS, 1, 2), (DO_BACK2, 3),
+    (DO_NORMB, 2), (DO_TE, 1, 2), (DO_GATE, 1), (DO_SS, 1, 3), (DO_SPLIT, 1), (DO_SX, 1, 0), (DO_SY, 1, 1),
+    (DO_ATTB, 1, 0), (DO_TX, 0), (DO_TZ, 1, 1), (DO_TZ, 1, 2), (DO_SFIN, 0), (DO_SWAP, 0), (DO_SY, 1, 2),
+    (DO_ATTB, 1, 1), (DO_RETIRE, 0), (DO_SX, 1, 1), (DO_CWAIT, 2), (DO_NEEDG, 1), (DO_OUTT, 1), (DO_SY, 1, 3),
+    (DO_SZ, 1, 0), (DO_ATTB, 1, 2), (DO_TTOT, 1), (DO_TE, 2, 0), (DO_SX, 1, 2), (DO_SENDQ, 1), (DO_BACK, 1, 0),
+    (DO_SX, 1, 3), (DO_SZ, 1, 1), (DO_NEEDQ, 1), (DO_QKVT, 1, 0), (DO_QKVT, 1, 1), (DO_TY, 1), (DO_SZ, 1, 2),
+    (DO_QKVT, 1, 2), (DO_TE, 2, 1), (DO_SS, 2, 0), (DO_BACK, 1, 1), (DO_BACK, 1, 2), (DO_TZ, 2, 0), (DO_SS, 2, 1),
+    (DO_TX, 1), (DO_NORMB, 1), (DO_ROWM, 1), (DO_TE, 2, 2), (DO_SFIN, 1), (DO_SWAP, 1), (DO_SENTQ, 1), (DO_GATE, 0),
+    (DO_SY, 2, 0), (DO_SPLIT, 0), (DO_ATTB, 0, 0), (DO_TZ, 2, 1), (DO_TZ, 2, 2), (DO_SY, 2, 1), (DO_ATTB, 0, 1),
+    (DO_ROWZ, 1), (DO_SS, 2, 2), (DO_RETIRE, 1), (DO_SX, 2, 0), (DO_CWAIT, 3), (DO_NEEDG, 0), (DO_OUTT, 0),
+    (DO_SS, 2, 3), (DO_ATTB, 0, 2), (DO_TTOT, 2), (DO_SX, 2, 1), (DO_SENDQ, 0), (DO_BACK, 0, 0), (DO_SY, 2, 2),
+    (DO_NEEDQ, 0), (DO_QKVT, 0, 0), (DO_QKVT, 0, 1), (DO_QKVT, 0, 2), (DO_TE, 3, 0), (DO_SY, 2, 3), (DO_BACK, 0, 1),
+    (DO_TY, 2), (DO_SS, 3, 0), (DO_BACK, 0, 2), (DO_SX, 2, 2), (DO_ROWT, 1), (DO_SZ, 2, 0), (DO_NORMB, 0),
+    (DO_ROWM, 0), (DO_SX, 2, 3), (DO_SZ, 2, 1), (DO_SS, 3, 1), (DO_ROWD, 1), (DO_SENTQ, 0), (DO_TX, 2), (DO_TE, 3, 1),
+    (DO_SY, 3, 0), (DO_TZ, 3, 0), (DO_SZ, 2, 2), (DO_SS, 3, 2), (DO_ROWZ, 0), (DO_SS, 3, 3), (DO_SY, 3, 1),
+    (DO_SX, 3, 0), (DO_SFIN, 2), (DO_SWAP, 2), (DO_TZ, 3, 1), (DO_RETIRE, 2), (DO_SY, 3, 2), (DO_TE, 3, 2),
+    (DO_TZ, 3, 2), (DO_SX, 3, 1), (DO_ROWT, 0), (DO_SZ, 3, 0), (DO_ROWD, 0), (DO_SY, 3, 3), (DO_SX, 3, 2),
+    (DO_TTOT, 3), (DO_SX, 3, 3), (DO_SZ, 3, 1), (DO_SZ, 3, 2), (DO_TY, 3), (DO_TX, 3), (DO_SFIN, 3), (DO_SWAP, 3),
+    (DO_RETIRE, 3),
 )
 
 
@@ -683,10 +723,11 @@
 def layer_kernel(
     tokens,
     cotangent,
-    ids_row,
-    ids_col,
     steps,
-    bias,
+    seg_ids,
+    frame_ids,
+    patch_ids,
+    b_ada,
     w_ada,
     w_qkv_s,
     w_out_s,
@@ -696,8 +737,8 @@
     w_down,
     o_layer,
     o_tokens,
-    o_ada,
-    o_bias,
+    cond,
+    all_rows_mod,
     o_qkv_s,
     o_out_s,
     o_qkv_t,
@@ -716,11 +757,11 @@
     last_one,
     last_z,
     all_steps,
-    cond,
+    bias,
+    ids,
     mod,
     tally,
     rows_mod,
-    all_rows_mod,
     xhat,
     deviation,
     normed,
@@ -837,8 +878,9 @@
     def turned_copy(i):
         return to_twin(i, turned.at[i, 0], turned.at[i, 1])
 
-    def hidden_copy():
-        return to_twin(5, hidden_turned.at[0], hidden_turned.at[1])
+    def hidden_copy(i):
+        rows = pl.ds(768 * i, 768)
+        return to_twin(12 + i, hidden_turned.at[0, rows], hidden_turned.at[1, rows])
 
     def gated_copy(j):
         theirs = pl.multiple_of((1 - core) * 384, 128)
@@ -852,41 +894,48 @@
         theirs = pl.multiple_of((1 - core) * 1152, 128)
         return to_twin(10 + j, grad_qkv.at[:, pl.ds(theirs, 1152)], grad_qkv_twin.at[j])
 
-    def step_copy(index, ref, device):
-        return remote(ref, ref, step_send.at[index], step_recv.at[index], device)
-
-    def step_pair(plane):
-        return all_steps.at[spot.z, plane]
-
-    step_line = LineGather(
-        spot, lambda z: all_steps.at[z], step_send.at[pl.ds(4, 5)], step_recv.at[pl.ds(4, 4)]
+    def step_twin(owner):
+        ref = all_steps.at[spot.z, spot.plane, owner]
+        return remote(ref, ref, step_send.at[0], step_recv.at[0], spot.twin)
+
+    step_line = Exchange(
+        spot.line,
+        spot.z,
+        lambda z: all_steps.at[spot.z, spot.plane],
+        lambda z: all_steps.at[z, spot.plane],
+        step_send.at[pl.ds(1, 3)],
+        step_recv.at[pl.ds(4, 4)],
+    )
+    step_mates = Exchange(
+        spot.mates,
+        spot.plane,
+        lambda plane: all_steps.at[:, spot.plane],
+        lambda plane: all_steps.at[:, plane],
+        step_send.at[pl.ds(4, 3)],
+        step_recv.at[pl.ds(8, 4)],
     )
 
     def steps_open():
-        all_steps[spot.z, spot.plane, core] = steps[...]
-        step_copy(0, all_steps.at[spot.z, spot.plane, core], spot.twin).start()
-
-    def steps_first():
-        step_copy(0, all_steps.at[spot.z, spot.plane, 1 - core], spot.twin).wait_recv()
-        step_copy(1, step_pair(spot.plane), spot.first).start()
-        step_copy(2, step_pair(spot.plane), spot.second).start()
-
-    def steps_second():
-        step_copy(1, step_pair(spot.first_plane), spot.first).wait_recv()
-        step_copy(3, step_pair(spot.first_plane), spot.second).start()
-
-    def steps_z():
-        step_copy(2, step_pair(spot.second_plane), spot.second).wait_recv()
-        step_copy(3, step_pair(spot.far_plane), spot.second).wait_recv()
-        step_line.open()
+        row = lax.broadcasted_iota(jnp.int32, (8, 128), 0)
+        value = jnp.where(row == 0, steps[0, 0], jnp.where(row == 1, steps[0, 1], 0))
+        all_steps[spot.z, spot.plane, core] = value.astype(f32)
+        step_twin(core).start()
+
+    def steps_line():
+        step_twin(1 - core).wait_recv()
+        step_line.start()
+
+    def steps_mates():
+        step_line.arrive()
+        step_mates.start()
 
     def steps_drain():
-        step_copy(0, all_steps.at[spot.z, spot.plane, core], spot.twin).wait_send()
-        for index in (1, 2, 3):
-            step_copy(index, step_pair(spot.plane), spot.first).wait_send()
+        step_twin(core).wait_send()
         step_line.drain()
+        step_mates.drain()
 
     def make_cond():
+        step_mates.arrive()
         flat = all_steps[...].reshape(256, 128)
         clip = lax.broadcasted_iota(jnp.int32, (64, 256), 0)
         column = lax.broadcasted_iota(jnp.int32, (64, 256), 1)
@@ -905,148 +954,156 @@
         value = jnp.where(feature < half_width, jnp.cos(angle), jnp.sin(angle))
         cond[...] = (value / (1.0 + jnp.exp(-value))).astype(bf16)
 
-    spare = sums.at[1]
-    mod_out, mod_in, mod_sum = (spare.at[pl.ds(i, 12)] for i in (0, 12, 24))
-    mod_first, mod_second, mod_one, mod_two = (spare.at[pl.ds(i, 3)] for i in (51, 54, 57, 60))
-    mod_line = LineSum(
-        spot,
-        lambda z: spare.at[pl.ds(24 + 3 * z, 3)],
-        lambda i: spare.at[pl.ds(36 + 3 * i, 3)],
-        mod_send.at[pl.ds(0, 3)],
-        mod_recv.at[pl.ds(0, 5)],
-    )
-
-    def mod_copy(index):
-        src, dst, device = (
-            (mod_out, mod_in, spot.twin),
-            (mod_one, mod_first, spot.first),
-            (mod_two, mod_second, spot.second),
-        )[index]
-        return remote(src, dst, mod_send.at[3 + index], mod_recv.at[5 + index], device)
-
-    def mod_partial(owner, chunk):
-        rows = cond[pl.ds(pl.multiple_of(32 * owner, 32), 32), :24]
-        left, right = (
-            dot(rows, w_ada[:, at : at + 384]) + bias[:, at : at + 384]
-            for at in (384 * chunk, 3456 + 384 * chunk)
-        )
-        for z in range(4):
-            part = slice(8 * z, 8 * z + 8)
-            yield 3 * z + chunk // 3, jnp.concatenate([left[part], right[part]], axis=0)
-
-    def mod_twin():
-        for chunk in range(9):
-            rows = slice(16 * (chunk % 3), 16 * (chunk % 3) + 16)
-            for at, value in mod_partial(1 - core, chunk):
-                mod_out[at, rows] = value.astype(bf16)
-        mod_copy(0).start()
-
-    def mod_own():
-        mod_copy(0).wait_recv()
-        for chunk in range(9):
-            rows = slice(16 * (chunk % 3), 16 * (chunk % 3) + 16)
-            for at, value in mod_partial(core, chunk):
-                mod_sum[at, rows] = (value + mod_in[at, rows].astype(f32)).astype(bf16)
-
-    def mod_along_first():
-        def put(i, value):
-            mod_one[i] = value.astype(bf16)
-
-        mod_line.total(put)
-        mod_copy(1).start()
-
-    def mod_along_second():
-        mod_copy(1).wait_recv()
-        for i in range(3):
-            mod_two[i] = mod_one[i] + mod_first[i]
-        mod_copy(2).start()
-
-    def mod_rows():
-        mod_copy(2).wait_recv()
-        row = lax.broadcasted_iota(jnp.int32, (16, 384), 0)
-        for chunk in range(9):
-            at, rows = chunk // 3, slice(16 * (chunk % 3), 16 * (chunk % 3) + 16)
-            value = mod_two[at, rows].astype(f32) + mod_second[at, rows].astype(f32)
-            for clip in range(2):
-                for half in range(2):
-                    chosen = row == 8 * half + 2 * spot.plane + clip
-                    column = 3456 * half + 384 * chunk
-                    mod[clip : clip + 1, column : column + 384] = jnp.sum(
-                        jnp.where(chosen, value, 0.0), axis=0, keepdims=True
+    parts = (range(0, 1), range(1, 3))
+
+    def columns_of(j, half, chunk):
+        at = 2304 * j + 1152 * half + 384 * chunk
+        return slice(at, at + 384)
+
+    def rows_of(chunk):
+        return slice(16 * chunk, 16 * chunk + 16)
+
+    class ModPart:
+        def __init__(self, part):
+            self.part, self.n = part, len(parts[part])
+            base, n = 21 * part, self.n
+            self.out, self.into, self.sum = (sums.at[1, pl.ds(base + 4 * n * i, 4 * n)] for i in range(3))
+            self.own = sums.at[1, pl.ds(base + 16 * n, n)]
+            self.line = Exchange(
+                spot.line,
+                spot.z,
+                lambda z: sums.at[1, pl.ds(base + 8 * n + n * z, n)],
+                lambda z: sums.at[1, pl.ds(base + 12 * n + n * z, n)],
+                mod_send.at[part, pl.ds(1, 3)],
+                mod_recv.at[part, pl.ds(4, 4)],
+            )
+            self.mates = Exchange(
+                spot.mates,
+                spot.plane,
+                lambda plane: self.own,
+                lambda plane: sums.at[1, pl.ds(base + 17 * n + n * plane, n)],
+                mod_send.at[part, pl.ds(4, 3)],
+                mod_recv.at[part, pl.ds(8, 4)],
+            )
+
+        def swap(self):
+            part = self.part
+            return remote(self.out, self.into, mod_send.at[part, 0], mod_recv.at[part, 0], spot.twin)
+
+        def terms(self, owner):
+            rows = cond[pl.ds(pl.multiple_of(32 * owner, 32), 32), :24]
+            for i, j in enumerate(parts[self.part]):
+                for chunk in range(3):
+                    left, right = (
+                        dot(rows, w_ada[:, columns_of(j, half, chunk)])
+                        + bias[0:1, columns_of(j, half, chunk)]
+                        for half in range(2)
                     )
-
-    def mod_drain():
-        mod_line.drain()
-        for index in range(3):
-            mod_copy(index).wait_send()
-
-    row_line = LineGather(
-        spot,
-        lambda z: all_rows_mod.at[core, z],
-        row_send.at[pl.ds(4, 5)],
-        row_recv.at[pl.ds(4, 4)],
-    )
-
-    def row_copy(index):
-        src, dst, device = (
-            (rows_mod.at[0], rows_mod.at[1], spot.first),
-            (rows_mod.at[2], rows_mod.at[3], spot.second),
-            (all_rows_mod.at[core], all_rows_mod.at[core], spot.twin),
-        )[index]
-        return remote(src, dst, row_send.at[index], row_recv.at[index], device)
-
-    def rows_first():
-        row = lax.broadcasted_iota(jnp.int32, (16, 384), 0)
-        for chunk in range(9):
-            value = 0.0
-            for clip in range(2):
-                for half in range(2):
-                    chosen = row == 8 * half + 2 * spot.plane + clip
-                    column = 3456 * half + 384 * chunk
-                    value += jnp.where(chosen, tally[clip : clip + 1, column : column + 384], 0.0)
-            rows_mod[0, :, 384 * chunk : 384 * chunk + 384] = value.astype(bf16)
-        row_copy(0).start()
-
-    def rows_second():
-        row_copy(0).wait_recv()
-        rows_mod[2] = rows_mod[0] + rows_mod[1]
-        row_copy(1).start()
-
-    def rows_z():
-        row_copy(1).wait_recv()
-        all_rows_mod[core, spot.z] = rows_mod[2] + rows_mod[3]
-        row_line.open()
-
-    def rows_twin():
-        row_copy(2).start()
-
-    def ada(owner):
-        rows = cond[pl.ds(pl.multiple_of(32 * owner, 32), 32), :]
-        for chunk in range(9):
-            value = all_rows_mod[owner, :, :, 384 * chunk : 384 * chunk + 384].astype(f32)
-            for half in range(2):
-                part = value[:, 8 * half : 8 * half + 8].reshape(32, 384)
-                columns = slice(3456 * half + 384 * chunk, 3456 * half + 384 * chunk + 384)
-                product = contract_rows(rows, part.astype(bf16))[:24]
-                total = jnp.sum(part, axis=0, keepdims=True)
-                yield columns, product, total
-
-    def ada_own():
-        for columns, product, total in ada(core):
-            o_ada[:, columns] = product
-            o_bias[:, columns] = total
-
-    def ada_twin():
-        theirs = all_rows_mod.at[1 - core]
-        remote(theirs, theirs, row_send.at[2], row_recv.at[2], spot.twin).wait_recv()
-        for columns, product, total in ada(1 - core):
-            o_ada[:, columns] += product
-            o_bias[:, columns] += total
-
-    def rows_drain():
-        for index in range(3):
-            row_copy(index).wait_send()
-        row_line.drain()
+                    for z in range(4):
+                        own = slice(8 * z, 8 * z + 8)
+                        block = jnp.concatenate([left[own], right[own]], axis=0)
+                        yield self.n * z + i, rows_of(chunk), block
+
+        def for_twin(self):
+            for at, rows, value in self.terms(1 - core):
+                self.out[at, rows] = value.astype(bf16)
+            self.swap().start()
+
+        def for_line(self):
+            self.swap().wait_recv()
+            for at, rows, value in self.terms(core):
+                self.sum[at, rows] = (value + self.into[at, rows].astype(f32)).astype(bf16)
+            self.line.start()
+
+        def for_mates(self):
+            self.line.arrive()
+            for i in range(self.n):
+                value = self.line.src(spot.z)[i].astype(f32)
+                for z, _ in spot.line:
+                    value += self.line.dst(z)[i].astype(f32)
+                self.own[i] = value.astype(bf16)
+            self.mates.start()
+
+        def done(self):
+            self.mates.arrive()
+            row = lax.broadcasted_iota(jnp.int32, (16, 384), 0)
+            for i, j in enumerate(parts[self.part]):
+                for chunk in range(3):
+                    value = self.own[i, rows_of(chunk)].astype(f32)
+                    for plane, _ in spot.mates:
+                        value += self.mates.dst(plane)[i, rows_of(chunk)].astype(f32)
+                    for clip in range(2):
+                        for half in range(2):
+                            chosen = row == 8 * half + 2 * spot.plane + clip
+                            mod[clip : clip + 1, columns_of(j, half, chunk)] = jnp.sum(
+                                jnp.where(chosen, value, 0.0), axis=0, keepdims=True
+                            )
+
+        def drain(self):
+            self.swap().wait_send()
+            self.line.drain()
+            self.mates.drain()
+
+    class RowPart:
+        def __init__(self, part):
+            self.part, n = part, len(parts[part])
+            self.subs = subs = pl.ds(parts[part][0], n)
+            self.mates = Exchange(
+                spot.mates,
+                spot.plane,
+                lambda plane: rows_mod.at[spot.plane, subs],
+                lambda plane: rows_mod.at[plane, subs],
+                row_send.at[part, pl.ds(4, 3)],
+                row_recv.at[part, pl.ds(8, 4)],
+            )
+            self.line = Exchange(
+                spot.line,
+                spot.z,
+                lambda z: all_rows_mod.at[core, spot.z, subs],
+                lambda z: all_rows_mod.at[core, z, subs],
+                row_send.at[part, pl.ds(1, 3)],
+                row_recv.at[part, pl.ds(4, 4)],
+            )
+
+        def swap(self, owner):
+            ref = all_rows_mod.at[owner, :, self.subs]
+            return remote(ref, ref, row_send.at[self.part, 0], row_recv.at[self.part, 0], spot.twin)
+
+        def for_mates(self):
+            row = lax.broadcasted_iota(jnp.int32, (16, 384), 0)
+            for j in parts[self.part]:
+                for chunk in range(3):
+                    value = 0.0
+                    for clip in range(2):
+                        for half in range(2):
+                            chosen = row == 8 * half + 2 * spot.plane + clip
+                            own = tally[clip : clip + 1, columns_of(j, half, chunk)]
+                            value += jnp.where(chosen, own, 0.0)
+                    rows_mod[spot.plane, j, :, 384 * chunk : 384 * chunk + 384] = value.astype(bf16)
+            self.mates.start()
+
+        def for_line(self):
+            self.mates.arrive()
+            for j in parts[self.part]:
+                all_rows_mod[core, spot.z, j] = (rows_mod[0, j] + rows_mod[1, j]) + (
+                    rows_mod[2, j] + rows_mod[3, j]
+                )
+            self.line.start()
+
+        def for_twin(self):
+            self.line.arrive()
+            self.swap(core).start()
+
+        def done(self):
+            self.swap(1 - core).wait_recv()
+
+        def drain(self):
+            self.swap(core).wait_send()
+            self.mates.drain()
+            self.line.drain()
+
+    mod_parts = [ModPart(part) for part in range(2)]
+    row_parts = [RowPart(part) for part in range(2)]
 
     def by_rows(action):
         @pl.loop(0, tok // 64)
@@ -1055,20 +1112,29 @@
 
     def mod_part(j, component, rows):
         at = (3 * j + component) * width
-        second = ids_col[rows, 2:3] == 1
+        second = ids[rows, 2:3] == 1.0
         return jnp.where(second, mod[1:2, at : at + width], mod[0:1, at : at + width])
 
     def count(j, component, rows, value):
         at = (3 * j + component) * width
-        second = ids_col[rows, 2:3] == 1
+        second = ids[rows, 2:3] == 1.0
         tally[0:1, at : at + width] += jnp.sum(jnp.where(second, 0.0, value), axis=0, keepdims=True)
         tally[1:2, at : at + width] += jnp.sum(jnp.where(second, value, 0.0), axis=0, keepdims=True)
 
     def masks():
-        for j in range(2):
-            same = ids_col[:, j : j + 1] == ids_row[j : j + 1, :]
-            disallowed[j] = jnp.where(same, 0.0, MASKED)
+        spatial = (seg_ids[...] * 16 + frame_ids[...]).astype(f32)
+        temporal = (seg_ids[...] * 16 + patch_ids[...]).astype(f32)
+        row = lax.broadcasted_iota(jnp.int32, (8, tok), 0)
+        second = seg_ids[...].astype(f32)
+        stacked = jnp.where(row == 0, spatial, jnp.where(row == 1, temporal, second))
+        ids[...] = stacked.T
+        for j, keys in enumerate((spatial, temporal)):
+            disallowed[j] = jnp.where(ids[:, j : j + 1] == keys, 0.0, MASKED)
         tally[...] = jnp.zeros_like(tally)
+        share = b_ada.shape[1]
+        bias[...] = jnp.zeros_like(bias)
+        bias[0:1, :share] = b_ada[...].astype(f32)
+        bias[...] = pltpu.roll(bias[...], (2 * spot.chip + core) * share, 1)
 
     def standardize(j):
         def action(rows):
@@ -1226,9 +1292,12 @@
 
         by_rows(action)
 
-    def grad_hidden(first, last):
-        @pl.loop(first, last)
-        def _(i):
+    def grad_hidden(step):
+        first = 2 * lax.rem(step + 2 - 2 * core, 4)
+
+        @pl.loop(0, 2)
+        def _(part):
+            i = first + part
             columns = pl.ds(pl.multiple_of(i * 384, 128), 384)
             value = sum(
                 contract_cols(
@@ -1301,20 +1370,28 @@
     def each_twin_copy():
         for i in range(5):
             yield turned_copy(i)
-        yield hidden_copy()
+        for i in range(4):
+            yield hidden_copy(i)
         for j in range(3):
             yield gated_copy(j)
         yield grad_pre_copy()
 
     def forward_drain():
         steps_drain()
-        mod_drain()
+        for part in mod_parts:
+            part.drain()
         for gather in gathers:
             gather.swap().wait_send()
 
-    def send_hidden():
-        forward_drain()
-        hidden_copy().start()
+    def send_hidden(i):
+        if i == 0:
+            forward_drain()
+        hidden_copy(i).start()
+
+    def need_hidden(i):
+        if i == 0:
+            gated_copy(2).wait_recv()
+        hidden_copy(i).wait_recv()
 
     def retire(n):
         scatters[n].store(puts[n])
@@ -1329,79 +1406,73 @@
         copy(*indices).wait_recv()
 
     steps_of = {
-        "steps": (steps_first, steps_second, steps_z),
-        "stepp": step_line.pass_on,
-        "stepz": step_line.take,
-        "cond": make_cond,
-        "modpart": (mod_twin, mod_own),
-        "mode": mod_line.send_end,
-        "modz": mod_line.send_middle,
-        "modfirst": mod_along_first,
-        "modsecond": mod_along_second,
-        "modrows": mod_rows,
-        "own": lambda g: gathers[g].own(),
-        "gz": lambda g, k: gathers[g].pass_on(k),
-        "gs": lambda g, k: gathers[g].spread(k),
-        "gx": lambda g, k: gathers[g].along_first(k),
-        "gy": lambda g, k: gathers[g].along_second(k),
-        "lx": lambda g: gathers[g].last_along_first(),
-        "ly": lambda g: gathers[g].last_along_second(),
-        "lp": lambda g, k: gathers[g].line.pass_on(k),
-        "lz": lambda g, k: gathers[g].last_along_z(k),
-        "landed": lambda g: gathers[g].landed(),
-        "cwait": lambda n: scatters[n].wait_credit(),
-        "ss": lambda n, k: scatters[n].second_copy(k).start(),
-        "sy": lambda n, k: scatters[n].add_second(k),
-        "sx": lambda n, k: scatters[n].add_first(k),
-        "sz": lambda n, k: scatters[n].line.send_middle(k),
-        "sfin": lambda n: scatters[n].finish(),
-        "te": lambda n, k: scatters[n].last_line.send_end(k),
-        "tz": lambda n, k: scatters[n].last_line.send_middle(k),
-        "ttot": lambda n: scatters[n].last_total(),
-        "ty": lambda n: scatters[n].last_add_second(),
-        "tx": lambda n: scatters[n].last_finish(),
-        "swap": swap,
-        "retire": retire,
-        "rows": (rows_first, rows_second, rows_z),
-        "rowp": row_line.pass_on,
-        "rowz": row_line.take,
-        "rowt": rows_twin,
-        "ada": (ada_own, ada_twin),
-        "masks": masks,
-        "standardize": standardize,
-        "modulate": modulate,
-        "project": project,
-        "turnn": lambda j: turn(2 * j, normed),
-        "turna": lambda j: turn(2 * j + 1, attended),
-        "attend": lambda j, i: attend(j, 2 * i, 2 * i + 2),
-        "join": join,
-        "add": add_branch,
-        "gate": gate,
-        "expand": lambda i: expand(2 * i, 2 * i + 2),
-        "sendh": send_hidden,
-        "needh": lambda: (need(gated_copy, 2), need(hidden_copy)),
-        "downt": down_terms,
-        "ghid": lambda i: grad_hidden(2 * i, 2 * i + 2),
-        "sendp": lambda: grad_pre_copy().start(),
-        "contract": contract,
-        "close": close,
-        "needp": lambda: (need(grad_pre_copy), need(turned_copy, 4)),
-        "upt": up_terms,
-        "back2": lambda i: back_project(2, 4, slope, 2 * i, 2 * i + 2),
-        "normb": norm_back,
-        "split": split,
-        "attb": lambda j, i: attend_back(j, 2 * i, 2 * i + 2),
-        "sendq": lambda j: grad_qkv_copy(j).start(),
-        "needq": lambda j: (
-            need(turned_copy, 2 * j + 1),
-            need(gated_copy, j),
+        DO_STEPS: (steps_line, steps_mates),
+        DO_COND: make_cond,
+        DO_MODT: lambda part: mod_parts[part].for_twin(),
+        DO_MODZ: lambda part: mod_parts[part].for_line(),
+        DO_MODM: lambda part: mod_parts[part].for_mates(),
+        DO_MODROWS: lambda part: mod_parts[part].done(),
+        DO_OWN: lambda g: gathers[g].own(),
+        DO_GZ: lambda g, k: gathers[g].pass_on(k),
+        DO_GS: lambda g, k: gathers[g].spread(k),
+        DO_GX: lambda g, k: gathers[g].along_first(k),
+        DO_GY: lambda g, k: gathers[g].along_second(k),
+        DO_LX: lambda g: gathers[g].last_along_first(),
+        DO_LY: lambda g: gathers[g].last_along_second(),
+        DO_LP: lambda g, k: gathers[g].line.pass_on(k),
+        DO_LZ: lambda g, k: gathers[g].last_along_z(k),
+        DO_LANDED: lambda g: gathers[g].landed(),
+        DO_CWAIT: lambda n: scatters[n].wait_credit(),
+        DO_SS: lambda n, k: scatters[n].second_copy(k).start(),
+        DO_SY: lambda n, k: scatters[n].add_second(k),
+        DO_SX: lambda n, k: scatters[n].add_first(k),
+        DO_SZ: lambda n, k: scatters[n].line.send_middle(k),
+        DO_SFIN: lambda n: scatters[n].finish(),
+        DO_TE: lambda n, k: scatters[n].last_line.send_end(k),
+        DO_TZ: lambda n, k: scatters[n].last_line.send_middle(k),
+        DO_TTOT: lambda n: scatters[n].last_total(),
+        DO_TY: lambda n: scatters[n].last_add_second(),
+        DO_TX: lambda n: scatters[n].last_finish(),
+        DO_SWAP: swap,
+        DO_RETIRE: retire,
+        DO_ROWM: lambda part: row_parts[part].for_mates(),
+        DO_ROWZ: lambda part: row_parts[part].for_line(),
+        DO_ROWT: lambda part: row_parts[part].for_twin(),
+        DO_ROWD: lambda part: row_parts[part].done(),
+        DO_MASKS: masks,
+        DO_STANDARDIZE: standardize,
+        DO_MODULATE: modulate,
+        DO_PROJECT: project,
+        DO_TURNN: lambda j: turn(2 * j, normed),
+        DO_TURNA: lambda j: turn(2 * j + 1, attended),
+        DO_ATTEND: lambda j, i: attend(j, 2 * i, 2 * i + 2),
+        DO_JOIN: join,
+        DO_ADD: add_branch,
+        DO_GATE: gate,
+        DO_EXPAND: lambda i: expand(2 * i, 2 * i + 2),
+        DO_SENDH: send_hidden,
+        DO_NEEDH: need_hidden,
+        DO_DOWNT: down_terms,
+        DO_GHID: grad_hidden,
+        DO_SENDP: lambda: grad_pre_copy().start(),
+        DO_CONTRACT: contract,
+        DO_CLOSE: close,
+        DO_NEEDP: lambda: (need(grad_pre_copy), need(turned_copy, 4)),
+        DO_UPT: up_terms,
+        DO_BACK2: lambda i: back_project(2, 4, slope, 2 * i, 2 * i + 2),
+        DO_NORMB: norm_back,
+        DO_SPLIT: split,
+        DO_ATTB: lambda j, i: attend_back(j, 2 * i, 2 * i + 2),
+        DO_SENDQ: lambda j: grad_qkv_copy(j).start(),
+        DO_NEEDG: lambda j: (need(turned_copy, 2 * j + 1), need(gated_copy, j)),
+        DO_NEEDQ: lambda j: (
             need(turned_copy, 2 * j),
             need(grad_qkv_copy, j),
         ),
-        "outt": out_terms,
-        "qkvt": qkv_terms,
-        "back": lambda j, i: back_project(j, 3, grad_qkv, 2 * i, 2 * i + 2),
-        "sentq": lambda j: grad_qkv_copy(j).wait_send(),
+        DO_OUTT: out_terms,
+        DO_QKVT: qkv_terms,
+        DO_BACK: lambda j, i: back_project(j, 3, grad_qkv, 2 * i, 2 * i + 2),
+        DO_SENTQ: lambda j: grad_qkv_copy(j).wait_send(),
     }
     for g, gather in enumerate(gathers):
         gather.open(pieces[g])
@@ -1412,29 +1483,66 @@
             step[indices[0]]()
         else:
             step(*indices)
-    rows_drain()
+    for part in row_parts:
+        part.drain()
     for gather in gathers:
         gather.drain()
     for copy in each_twin_copy():
         copy.wait_send()
 
 
-def layer(tokens, cotangent, ids_row, ids_col, steps, bias, w_ada, *shards):
+def finish_kernel(cond, all_rows_mod, *refs):
+    sources, o_ada, o_bias = refs[:8], refs[8], refs[9]
+    results, held, total, sem = refs[10:18], refs[18:26], refs[26], refs[27]
+
+    def copies(first, second, kind):
+        return [
+            pltpu.make_async_copy(src, dst, sem.at[kind, i])
+            for i, (src, dst) in enumerate(zip(first, second, strict=True))
+        ]
+
+    arriving, leaving = copies(sources, held, 0), copies(held, results, 1)
+    for copy in arriving:
+        copy.start()
+    total[...] = jnp.zeros_like(total)
+    for j in range(3):
+        for half in range(2):
+            for chunk in range(3):
+                at = 2304 * j + 1152 * half + 384 * chunk
+                part = all_rows_mod[:, :, j, :, 384 * chunk : 384 * chunk + 384].astype(jnp.float32)
+                part = part[:, :, 8 * half : 8 * half + 8].reshape(64, 384)
+                low = part.astype(jnp.bfloat16)
+                o_ada[:, at : at + 384] = contract_rows(cond[...], low)[:24]
+                total[0:1, at : at + 384] = jnp.sum(part, axis=0, keepdims=True)
+        if j == 0:
+            for copy, onward in zip(arriving, leaving, strict=True):
+                copy.wait()
+                onward.start()
+    place = lax.axis_index("wide") * 2 + lax.axis_index("narrow")
+    share, columns = o_bias.shape[1], total.shape[1]
+    turned = pltpu.roll(total[...], lax.rem(columns - place * share, columns), 1)
+    o_bias[...] = turned[0:1, :share]
+    for copy in leaving:
+        copy.wait()
+
+
+def layer(tokens, cotangent, steps, seg_ids, frame_ids, patch_ids, b_ada, w_ada, *shards):
     f32, bf16 = jnp.float32, jnp.bfloat16
     tok, width = tokens.shape
     block = (4, 48, 384)
     dma, vmem = pltpu.SemaphoreType.DMA, pltpu.VMEM
-    return pl.pallas_call(
+    in_vmem, in_hbm = pl.BlockSpec(memory_space=vmem), pl.BlockSpec(memory_space=pltpu.HBM)
+    outs = pl.pallas_call(
         layer_kernel,
         out_shape=[
             jax.ShapeDtypeStruct((tok, width), bf16),
             jax.ShapeDtypeStruct((tok, width), f32),
-            jax.ShapeDtypeStruct(w_ada.shape, f32),
-            jax.ShapeDtypeStruct((1, w_ada.shape[1]), f32),
+            jax.ShapeDtypeStruct((64, 128), bf16),
+            jax.ShapeDtypeStruct((2, 4, 3, 16, 1152), bf16),
         ]
         + [jax.ShapeDtypeStruct(shard.shape, f32) for shard in shards],
-        in_specs=[pl.BlockSpec(memory_space=vmem)] * 13,
-        out_specs=[pl.BlockSpec(memory_space=vmem)] * 10,
+        in_specs=[in_vmem] * 2 + [pl.BlockSpec(memory_space=pltpu.SMEM)] + [in_vmem] * 11,
+        out_specs=[in_vmem] * 10,
         scratch_shapes=[
             vmem((4, 2, 16) + block, bf16),
             vmem((4,) + block, f32),
@@ -1448,11 +1556,11 @@
             vmem((2, 48, 384), bf16),
             vmem((2, 5) + block, bf16),
             vmem((4, 4, 2, 8, 128), f32),
-            vmem((64, 128), bf16),
+            vmem((8, w_ada.shape[1]), f32),
+            vmem((tok, 8), f32),
             vmem((8, 6912), f32),
             vmem((8, 6912), f32),
-            vmem((4, 16, 3456), bf16),
-            vmem((2, 4, 16, 3456), bf16),
+            vmem((4, 3, 16, 1152), bf16),
             vmem((3, tok, width), bf16),
             vmem((tok, 128), f32),
             vmem((tok, width), bf16),
@@ -1478,19 +1586,33 @@
             dma((4, 17)),
             dma((4, 21)),
             pltpu.SemaphoreType.REGULAR((2, 4)),
+            dma((16,)),
+            dma((16,)),
+            dma((7,)),
             dma((12,)),
-            dma((12,)),
-            dma((9,)),
-            dma((8,)),
-            dma((6,)),
-            dma((8,)),
-            dma((9,)),
-            dma((8,)),
+            dma((2, 7)),
+            dma((2, 12)),
+            dma((2, 7)),
+            dma((2, 12)),
         ],
         compiler_params=pltpu.CompilerParams(
             collective_id=0, has_side_effects=True, vmem_limit_bytes=64 * 2**20
         ),
-    )(tokens, cotangent, ids_row, ids_col, steps, bias, w_ada, *shards)
+    )(tokens, cotangent, steps, seg_ids, frame_ids, patch_ids, b_ada, w_ada, *shards)
+    sources = (*outs[:2], *outs[4:])
+    return pl.pallas_call(
+        finish_kernel,
+        out_shape=[
+            jax.ShapeDtypeStruct(w_ada.shape, f32),
+            jax.ShapeDtypeStruct((1, w_ada.shape[1] // 32), f32),
+        ]
+        + [jax.ShapeDtypeStruct(source.shape, source.dtype) for source in sources],
+        in_specs=[in_vmem] * 2 + [in_hbm] * 8,
+        out_specs=[in_vmem] * 2 + [in_hbm] * 8,
+        scratch_shapes=[vmem(source.shape, source.dtype) for source in sources]
+        + [vmem((8, w_ada.shape[1]), f32), dma((2, 8))],
+        compiler_params=pltpu.CompilerParams(vmem_limit_bytes=60 * 2**20),
+    )(outs[2], outs[3], *sources)
 
 
 def on_grid(
@@ -1509,21 +1631,19 @@
     w_down,
     cotangent,
 ):
-    place = lax.axis_index(("wide", "narrow"))
-    share = b_ada.shape[0]
-    ids = jnp.stack([seg_ids * 16 + frame_ids, seg_ids * 16 + patch_ids, seg_ids])
-    steps = jnp.broadcast_to(
-        jnp.pad(timesteps.astype(jnp.float32), (0, 6))[:, None], (8, 128)
-    )
-    bias = lax.dynamic_update_slice(
-        jnp.zeros((1, w_ada.shape[1]), jnp.float32),
-        b_ada.astype(jnp.float32)[None],
-        (0, place * share),
-    )
     shards = (w_qkv_spatial, w_out_spatial, w_qkv_temporal, w_out_temporal, w_up, w_down)
-    outs = layer(tokens, cotangent, ids, ids.T, steps, bias, w_ada, *shards)
-    bias_share = lax.dynamic_slice(outs[3][0], (place * share,), (share,))
-    return (*outs[:3], bias_share, *outs[4:])
+    grad_ada, grad_bias, out, grad_tokens, *grads = layer(
+        tokens,
+        cotangent,
+        timesteps[None],
+        seg_ids[None],
+        frame_ids[None],
+        patch_ids[None],
+        b_ada[None],
+        w_ada,
+        *shards,
+    )
+    return (out, grad_tokens, grad_ada, grad_bias.reshape(-1), *grads)
 
 
 def on_device(

time: 213 us -> 186 us (0.87)
  Pallas kernels: 197 us -> 183 us
  local copies, waits for them, and re-layouts: 14.2 us -> 1.21 us
    pallas_call x1, Pallas kernels: 197 us -> 179 us  [layer(): pl.pallas_call(layer_kernel, out_shape=[jax.ShapeDtypeStruct((tok, width)...]
    unnamed x39 -> x2, local copies, waits for them, and re-layouts: 11.2 us -> 0.65 us
    pallas_call x0 -> x1, Pallas kernels: none -> 4.7 us  [layer(): pl.pallas_call(finish_kernel, out_shape=[jax.ShapeDtypeStruct(w_ada.shape...]
where the time goes in v5:
time: 186 us; the launch traced here: 185 us
  Pallas kernels  183 us (98%)
    pallas_call x1, Pallas kernels, layer(): pl.pallas_call(layer_kernel, out_shape=[jax.ShapeDtypeStruct((tok, width)...  179 us
    pallas_call x1, Pallas kernels, layer(): pl.pallas_call(finish_kernel, out_shape=[jax.ShapeDtypeStruct(w_ada.shape...  4.7 us

profile of v5, /device:TPU:0, one launch (start us, length us, event | category | flops | bytes accessed | tf_op | source)
XLA Modules:
  0.0 185.5 jit_solution(2954978710576191502)
XLA Ops:
  0.6 0.0 copy-start
  0.7 0.6 copy-done
  1.3 0.6 broadcast_in_dim.19.b_ada
  1.9 178.7 %shard_map.213 = (bf16[256,768]{1,0:T(8,128)(2,1)}, f32[256,768]{1,0:T(8,128)}, bf16[64,128]{1,0:T(8,128)(2,1)}, bf16[2,4,3,16,1152]{4,3,2,1,0:T(8,128)(2,1)}, f...) custom-call(bf16[256,768]{1,0:T(8,128)(2,1)} %tokens.1, ...), custom_call_target="tpu_custom_call" | custom-call | tf_op jit(solution)/shard_map/pallas_call | solution.py:1535
  180.6 4.7 %shard_map.214 = (f32[24,6912]{1,0:T(8,128)}, f32[1,216]{1,0:T(1,128)}, bf16[256,768]{1,0:T(8,128)(2,1)}, f32[256,768]{1,0:T(8,128)}, f32[24,2304]{1,0:T(8,128)}...) custom-call(bf16[64,128]{1,0:T(8,128)(2,1)} %get-tuple-element.30.co, ...), custom_call_target="tpu_custom_call" | custom-call | tf_op jit(solution)/shard_map/pallas_call | solution.py:1603
Async XLA Ops:
  0.6 0.7 copy-start

commit v6 on v5

--- a/solution.py
+++ b/solution.py
@@ -314,20 +314,24 @@
 
 
 class Gather:
-    def __init__(self, spot, held, stage, apart, swap_sems, send, recv):
-        self.spot, self.held = spot, held
+    def __init__(self, spot, held, stage, apart, swap_sems, send, recv, count):
+        self.spot, self.held, self.count = spot, held, count
+        self.split = count < 4
         self.stage, self.apart, self.swap_sems = stage, apart, swap_sems
         self.send, self.recv = send, recv
         self.whole = apart.shape[1] == 48
         self.line = LineGather(
             spot,
-            lambda z: held.at[spot.core, pl.ds(4 * z, 4), 3],
+            lambda z: self.last_layer(spot.core, z),
             send.at[pl.ds(24, 5)],
             recv.at[pl.ds(23, 4)],
         )
 
     def block(self, z, plane):
-        return self.held.at[self.spot.core, z * 4 + plane, 0:3]
+        return self.held.at[self.spot.core, z * 4 + plane, 0 : self.count]
+
+    def last_layer(self, half, z):
+        return self.held.at[half, pl.ds(z * 4, 4), 3]
 
     def last(self, plane):
         return self.held.at[self.spot.core, self.spot.z * 4 + plane, 3]
@@ -361,8 +365,9 @@
         self.held[spot.core, spot.chip] = self.stage[...].astype(jnp.bfloat16)
         self.z_own(True).start()
         pl.when(spot.is_middle)(lambda: self.z_own(False).start())
-        self.last_first().start()
-        self.last_second(False).start()
+        if self.split:
+            self.last_first().start()
+            self.last_second(False).start()
 
     def z_own(self, inward):
         spot = self.spot
@@ -394,7 +399,7 @@
 
     def twin_copy(self, half, k):
         z = self.spot.arrival(k)
-        ref = self.held.at[half, pl.ds(z * 4, 4), 0:3]
+        ref = self.held.at[half, pl.ds(z * 4, 4), 0 : self.count]
         return self.copy(ref, 17 + k, 16 + z, self.spot.twin)
 
     def last_first(self):
@@ -407,7 +412,7 @@
 
     def last_twin(self, half, k):
         z = self.spot.arrival(k)
-        ref = self.held.at[half, pl.ds(z * 4, 4), 3]
+        ref = self.last_layer(half, z)
         return self.copy(ref, 29 + k, 27 + z, self.spot.twin)
 
     def get(self, k):
@@ -459,7 +464,8 @@
     def landed(self):
         for k in range(4):
             self.twin_copy(1 - self.spot.core, k).wait_recv()
-            self.last_twin(1 - self.spot.core, k).wait_recv()
+            if self.split:
+                self.last_twin(1 - self.spot.core, k).wait_recv()
 
     def drain(self):
         spot = self.spot
@@ -476,11 +482,13 @@
             self.second_copy(k).wait_send()
             self.second_pass(k).wait_send()
             self.twin_copy(spot.core, k).wait_send()
-            self.last_twin(spot.core, k).wait_send()
-        self.last_first().wait_send()
-        self.last_second(False).wait_send()
-        self.last_second(True).wait_send()
-        self.line.drain()
+            if self.split:
+                self.last_twin(spot.core, k).wait_send()
+        if self.split:
+            self.last_first().wait_send()
+            self.last_second(False).wait_send()
+            self.last_second(True).wait_send()
+            self.line.drain()
 
 
 class Scatter:
@@ -496,32 +504,31 @@
         self.owed, self.whole = owed, theirs.shape[1] == 48
         self.line = LineSum(
             spot,
-            lambda z: sums.at[pl.ds(12 * z, 3)],
+            lambda z: sums.at[4 * z, 0:3],
             lambda i: from_z.at[i],
             send.at[pl.ds(8, 3)],
             recv.at[pl.ds(8, 5)],
         )
         self.last_line = LineSum(
             spot,
-            lambda z: sums.at[pl.ds(48 + 4 * z, 4)],
+            lambda z: sums.at[pl.ds(4 * z, 4), 3],
             lambda i: last_z.at[i],
             send.at[pl.ds(12, 3)],
             recv.at[pl.ds(14, 5)],
         )
 
-    def place(self, chip, chunk):
+    def place(self, chip):
         spot = self.spot
         z, y, x = chip // 4, (chip // 2) % 2, chip % 2
         other_y, other_x = lax.rem(spot.y + y, 2), lax.rem(spot.x + x, 2)
         second = other_y * (1 - spot.core) + other_x * spot.core
         first = other_x * (1 - spot.core) + other_y * spot.core
-        block = 4 * z + 2 * second + first
-        return 48 + block if chunk == 3 else 3 * block + chunk
+        return 4 * z + 2 * second + first
 
     def second_copy(self, k):
         z = self.line.layer(k)
         return remote(
-            self.sums.at[pl.ds(12 * z + 6, 6)],
+            self.sums.at[pl.ds(4 * z + 2, 2), 0:3],
             self.from_second.at[z],
             self.send.at[k],
             self.recv.at[z],
@@ -531,7 +538,7 @@
     def first_copy(self, k):
         z = self.line.layer(k)
         return remote(
-            self.sums.at[pl.ds(12 * z + 3, 3)],
+            self.sums.at[4 * z + 1, 0:3],
             self.from_first.at[z],
             self.send.at[4 + k],
             self.recv.at[4 + z],
@@ -540,7 +547,7 @@
 
     def last_second_copy(self):
         return remote(
-            self.sums.at[pl.ds(48 + 4 * self.spot.z + 2, 2)],
+            self.sums.at[pl.ds(4 * self.spot.z + 2, 2), 3],
             self.last_pair,
             self.send.at[15],
             self.recv.at[19],
@@ -549,7 +556,7 @@
 
     def last_first_copy(self):
         return remote(
-            self.sums.at[48 + 4 * self.spot.z + 1],
+            self.sums.at[4 * self.spot.z + 1, 3],
             self.last_one,
             self.send.at[16],
             self.recv.at[20],
@@ -574,16 +581,17 @@
     def add_second(self, k):
         z = self.line.layer(k)
         self.second_copy(k).wait_recv()
-        for i in (3, 4, 5, 0, 1, 2):
-            self.sums[12 * z + i] += self.from_second[z, i]
-            if i == 5:
+        for first in (1, 0):
+            for chunk in range(3):
+                self.sums[4 * z + first, chunk] += self.from_second[z, first, chunk]
+            if first:
                 self.first_copy(k).start()
 
     def add_first(self, k):
         z = self.line.layer(k)
         self.first_copy(k).wait_recv()
-        for i in range(3):
-            self.sums[12 * z + i] += self.from_first[z, i]
+        for chunk in range(3):
+            self.sums[4 * z, chunk] += self.from_first[z, chunk]
         if k < 3:
             self.line.send_end(k)
 
@@ -594,24 +602,24 @@
         self.line.total(put)
 
     def last_total(self):
-        at = 48 + 4 * self.spot.z
+        at = 4 * self.spot.z
 
         def put(i, value):
-            self.sums[at + i] = value.astype(jnp.bfloat16)
+            self.sums[at + i, 3] = value.astype(jnp.bfloat16)
 
         self.last_line.total(put)
         self.last_second_copy().start()
 
     def last_add_second(self):
-        at = 48 + 4 * self.spot.z
+        at = 4 * self.spot.z
         self.last_second_copy().wait_recv()
-        self.sums[at + 1] += self.last_pair[1]
+        self.sums[at + 1, 3] += self.last_pair[1]
         self.last_first_copy().start()
-        self.sums[at] += self.last_pair[0]
+        self.sums[at, 3] += self.last_pair[0]
 
     def last_finish(self):
         self.last_first_copy().wait_recv()
-        self.final[3] = self.sums[48 + 4 * self.spot.z].astype(jnp.float32) + self.last_one[
+        self.final[3] = self.sums[4 * self.spot.z, 3].astype(jnp.float32) + self.last_one[
             ...
         ].astype(jnp.float32)
 
@@ -657,67 +665,70 @@
 
 
 (
-    DO_STEPS, DO_COND, DO_MODT, DO_MODZ, DO_MODM, DO_MODROWS, DO_OWN, DO_GZ, DO_GS, DO_GX, DO_GY,
-    DO_LX, DO_LY, DO_LP, DO_LZ, DO_LANDED, DO_CWAIT, DO_SS, DO_SY, DO_SX, DO_SZ, DO_SFIN, DO_TE,
-    DO_TZ, DO_TTOT, DO_TY, DO_TX, DO_SWAP, DO_RETIRE, DO_ROWM, DO_ROWZ, DO_ROWT, DO_ROWD, DO_MASKS,
-    DO_STANDARDIZE, DO_MODULATE, DO_PROJECT, DO_TURNN, DO_TURNA, DO_ATTEND, DO_JOIN, DO_ADD,
-    DO_GATE, DO_EXPAND, DO_SENDH, DO_NEEDH, DO_DOWNT, DO_GHID, DO_SENDP, DO_CONTRACT, DO_CLOSE,
-    DO_NEEDP, DO_UPT, DO_BACK2, DO_NORMB, DO_SPLIT, DO_ATTB, DO_SENDQ, DO_NEEDG, DO_NEEDQ, DO_OUTT,
-    DO_QKVT, DO_BACK, DO_SENTQ,
-) = range(64)
+    DO_STEPS, DO_COND, DO_MODT, DO_MODZ, DO_MODS, DO_MODM, DO_MODROWS, DO_OWN, DO_GZ, DO_GS, DO_GX,
+    DO_GY, DO_LX, DO_LY, DO_LP, DO_LZ, DO_LANDED, DO_CWAIT, DO_SS, DO_SY, DO_SX, DO_SZ, DO_SFIN,
+    DO_TE, DO_TZ, DO_TTOT, DO_TY, DO_TX, DO_SWAP, DO_RETIRE, DO_ROWM, DO_ROWZ, DO_ROWP, DO_ROWT,
+    DO_ROWD, DO_MASKS, DO_STANDARDIZE, DO_MODULATE, DO_PROJECT, DO_TURNN, DO_TURNA, DO_ATTEND,
+    DO_JOIN, DO_ADD, DO_GATE, DO_EXPAND, DO_SENDH, DO_NEEDH, DO_DOWNT, DO_GHID, DO_SENDP,
+    DO_CONTRACT, DO_CLOSE, DO_NEEDP, DO_UPT, DO_BACK2, DO_NORMB, DO_SPLIT, DO_ATTB, DO_SENDQ,
+    DO_NEEDG, DO_NEEDQ, DO_OUTT, DO_QKVT, DO_BACK, DO_SENTQ,
+) = range(66)
 
 ORDER = (
-    (DO_MASKS,), (DO_STANDARDIZE, 0), (DO_STEPS, 0), (DO_OWN, 0), (DO_GS, 0, 0), (DO_OWN, 1), (DO_GS, 1, 0),
-    (DO_STEPS, 1), (DO_LX, 0), (DO_GZ, 0, 1), (DO_GZ, 0, 2), (DO_GX, 0, 0), (DO_LX, 1), (DO_GZ, 1, 1), (DO_GZ, 1, 2),
-    (DO_GS, 0, 1), (DO_GZ, 0, 3), (DO_LY, 0), (DO_COND,), (DO_MODT, 0), (DO_MODT, 1), (DO_MODZ, 0), (DO_GX, 0, 1),
-    (DO_GZ, 1, 3), (DO_GY, 0, 0), (DO_GX, 1, 0), (DO_MODZ, 1), (DO_GS, 0, 2), (DO_LP, 0, 1), (DO_LP, 0, 2),
-    (DO_GS, 0, 3), (DO_GY, 0, 1), (DO_LZ, 0, 1), (DO_GY, 1, 0), (DO_GS, 1, 1), (DO_MODM, 0), (DO_GX, 0, 2),
-    (DO_GX, 0, 3), (DO_GX, 1, 1), (DO_LY, 1), (DO_MODROWS, 0), (DO_GS, 1, 2), (DO_MODULATE, 0), (DO_MODM, 1),
-    (DO_GY, 0, 2), (DO_LP, 0, 3), (DO_GY, 0, 3), (DO_LZ, 0, 2), (DO_GS, 1, 3), (DO_GY, 1, 1), (DO_LP, 1, 1),
-    (DO_LP, 1, 2), (DO_GX, 1, 2), (DO_LZ, 1, 1), (DO_OWN, 2), (DO_MODROWS, 1), (DO_GS, 2, 0), (DO_LZ, 0, 3),
-    (DO_LP, 1, 3), (DO_GX, 1, 3), (DO_LANDED, 0), (DO_PROJECT, 0), (DO_LX, 2), (DO_GY, 1, 2), (DO_LZ, 1, 2),
-    (DO_TURNN, 0), (DO_GZ, 2, 1), (DO_GZ, 2, 2), (DO_ATTEND, 0, 0), (DO_GX, 2, 0), (DO_ATTEND, 0, 1), (DO_GS, 2, 1),
-    (DO_GY, 1, 3), (DO_LY, 2), (DO_ATTEND, 0, 2), (DO_GZ, 2, 3), (DO_LZ, 1, 3), (DO_GY, 2, 0), (DO_JOIN, 0),
-    (DO_GS, 2, 2), (DO_ADD, 0), (DO_TURNA, 0), (DO_STANDARDIZE, 1), (DO_GX, 2, 1), (DO_MODULATE, 1), (DO_GATE, 2),
-    (DO_LP, 2, 1), (DO_LP, 2, 2), (DO_LZ, 2, 1), (DO_LANDED, 1), (DO_PROJECT, 1), (DO_GX, 2, 2), (DO_TURNN, 1),
-    (DO_GS, 2, 3), (DO_GY, 2, 1), (DO_ATTEND, 1, 0), (DO_OWN, 3), (DO_ATTEND, 1, 1), (DO_LP, 2, 3), (DO_GS, 3, 0),
-    (DO_GY, 2, 2), (DO_LZ, 2, 2), (DO_ATTEND, 1, 2), (DO_LX, 3), (DO_GX, 2, 3), (DO_JOIN, 1), (DO_GZ, 3, 1),
-    (DO_GZ, 3, 2), (DO_GS, 3, 1), (DO_ADD, 1), (DO_TURNA, 1), (DO_STANDARDIZE, 2), (DO_MODULATE, 2), (DO_GX, 3, 0),
-    (DO_LY, 3), (DO_TURNN, 2), (DO_LZ, 2, 3), (DO_GY, 2, 3), (DO_GZ, 3, 3), (DO_GX, 3, 1), (DO_GS, 3, 2),
-    (DO_LANDED, 2), (DO_EXPAND, 0), (DO_GY, 3, 0), (DO_SENDH, 0), (DO_EXPAND, 1), (DO_LP, 3, 1), (DO_LP, 3, 2),
-    (DO_LZ, 3, 1), (DO_SENDH, 1), (DO_EXPAND, 2), (DO_GY, 3, 1), (DO_SENDH, 2), (DO_GX, 3, 2), (DO_EXPAND, 3),
-    (DO_GS, 3, 3), (DO_SENDH, 3), (DO_CWAIT, 0), (DO_NEEDH, 0), (DO_DOWNT, 0), (DO_NEEDH, 1), (DO_DOWNT, 1),
-    (DO_NEEDH, 2), (DO_DOWNT, 2), (DO_LP, 3, 3), (DO_GY, 3, 2), (DO_LZ, 3, 2), (DO_NEEDH, 3), (DO_DOWNT, 3),
-    (DO_SS, 0, 0), (DO_TE, 0, 0), (DO_GX, 3, 3), (DO_TE, 0, 1), (DO_SS, 0, 1), (DO_TE, 0, 2), (DO_LZ, 3, 3),
-    (DO_SY, 0, 0), (DO_SS, 0, 2), (DO_TZ, 0, 0), (DO_GY, 3, 3), (DO_LANDED, 3), (DO_GHID, 0), (DO_GHID, 1),
-    (DO_TZ, 0, 1), (DO_SY, 0, 1), (DO_SENDP,), (DO_GHID, 2), (DO_SX, 0, 0), (DO_SS, 0, 3), (DO_GHID, 3),
-    (DO_TZ, 0, 2), (DO_NEEDP,), (DO_CWAIT, 1), (DO_SY, 0, 2), (DO_UPT, 3), (DO_UPT, 0), (DO_TE, 1, 0), (DO_SX, 0, 1),
-    (DO_UPT, 1), (DO_UPT, 2), (DO_SS, 1, 0), (DO_CONTRACT,), (DO_SZ, 0, 0), (DO_SX, 0, 2), (DO_SY, 0, 3), (DO_CLOSE,),
-    (DO_TTOT, 0), (DO_SS, 1, 1), (DO_BACK2, 0), (DO_TZ, 1, 0), (DO_BACK2, 1), (DO_SY, 1, 0), (DO_BACK2, 2),
-    (DO_TE, 1, 1), (DO_SX, 0, 3), (DO_SZ, 0, 1), (DO_SZ, 0, 2), (DO_TY, 0), (DO_SS, 1, 2), (DO_BACK2, 3),
-    (DO_NORMB, 2), (DO_TE, 1, 2), (DO_GATE, 1), (DO_SS, 1, 3), (DO_SPLIT, 1), (DO_SX, 1, 0), (DO_SY, 1, 1),
-    (DO_ATTB, 1, 0), (DO_TX, 0), (DO_TZ, 1, 1), (DO_TZ, 1, 2), (DO_SFIN, 0), (DO_SWAP, 0), (DO_SY, 1, 2),
-    (DO_ATTB, 1, 1), (DO_RETIRE, 0), (DO_SX, 1, 1), (DO_CWAIT, 2), (DO_NEEDG, 1), (DO_OUTT, 1), (DO_SY, 1, 3),
-    (DO_SZ, 1, 0), (DO_ATTB, 1, 2), (DO_TTOT, 1), (DO_TE, 2, 0), (DO_SX, 1, 2), (DO_SENDQ, 1), (DO_BACK, 1, 0),
-    (DO_SX, 1, 3), (DO_SZ, 1, 1), (DO_NEEDQ, 1), (DO_QKVT, 1, 0), (DO_QKVT, 1, 1), (DO_TY, 1), (DO_SZ, 1, 2),
-    (DO_QKVT, 1, 2), (DO_TE, 2, 1), (DO_SS, 2, 0), (DO_BACK, 1, 1), (DO_BACK, 1, 2), (DO_TZ, 2, 0), (DO_SS, 2, 1),
-    (DO_TX, 1), (DO_NORMB, 1), (DO_ROWM, 1), (DO_TE, 2, 2), (DO_SFIN, 1), (DO_SWAP, 1), (DO_SENTQ, 1), (DO_GATE, 0),
-    (DO_SY, 2, 0), (DO_SPLIT, 0), (DO_ATTB, 0, 0), (DO_TZ, 2, 1), (DO_TZ, 2, 2), (DO_SY, 2, 1), (DO_ATTB, 0, 1),
-    (DO_ROWZ, 1), (DO_SS, 2, 2), (DO_RETIRE, 1), (DO_SX, 2, 0), (DO_CWAIT, 3), (DO_NEEDG, 0), (DO_OUTT, 0),
-    (DO_SS, 2, 3), (DO_ATTB, 0, 2), (DO_TTOT, 2), (DO_SX, 2, 1), (DO_SENDQ, 0), (DO_BACK, 0, 0), (DO_SY, 2, 2),
-    (DO_NEEDQ, 0), (DO_QKVT, 0, 0), (DO_QKVT, 0, 1), (DO_QKVT, 0, 2), (DO_TE, 3, 0), (DO_SY, 2, 3), (DO_BACK, 0, 1),
-    (DO_TY, 2), (DO_SS, 3, 0), (DO_BACK, 0, 2), (DO_SX, 2, 2), (DO_ROWT, 1), (DO_SZ, 2, 0), (DO_NORMB, 0),
-    (DO_ROWM, 0), (DO_SX, 2, 3), (DO_SZ, 2, 1), (DO_SS, 3, 1), (DO_ROWD, 1), (DO_SENTQ, 0), (DO_TX, 2), (DO_TE, 3, 1),
-    (DO_SY, 3, 0), (DO_TZ, 3, 0), (DO_SZ, 2, 2), (DO_SS, 3, 2), (DO_ROWZ, 0), (DO_SS, 3, 3), (DO_SY, 3, 1),
-    (DO_SX, 3, 0), (DO_SFIN, 2), (DO_SWAP, 2), (DO_TZ, 3, 1), (DO_RETIRE, 2), (DO_SY, 3, 2), (DO_TE, 3, 2),
-    (DO_TZ, 3, 2), (DO_SX, 3, 1), (DO_ROWT, 0), (DO_SZ, 3, 0), (DO_ROWD, 0), (DO_SY, 3, 3), (DO_SX, 3, 2),
-    (DO_TTOT, 3), (DO_SX, 3, 3), (DO_SZ, 3, 1), (DO_SZ, 3, 2), (DO_TY, 3), (DO_TX, 3), (DO_SFIN, 3), (DO_SWAP, 3),
-    (DO_RETIRE, 3),
+    (DO_CWAIT, 0), (DO_CWAIT, 1), (DO_MASKS,), (DO_STANDARDIZE, 0), (DO_STEPS, 0), (DO_OWN, 0), (DO_GS, 0, 0),
+    (DO_OWN, 1), (DO_GS, 1, 0), (DO_STEPS, 1), (DO_LX, 0), (DO_GZ, 0, 1), (DO_GZ, 0, 2), (DO_GS, 0, 1), (DO_GZ, 1, 1),
+    (DO_GZ, 1, 2), (DO_GX, 0, 0), (DO_LY, 0), (DO_GS, 0, 2), (DO_GZ, 0, 3), (DO_COND,), (DO_MODT, 0), (DO_MODT, 1),
+    (DO_MODZ, 0), (DO_GX, 0, 1), (DO_GZ, 1, 3), (DO_GS, 1, 1), (DO_MODZ, 1), (DO_GY, 0, 0), (DO_LP, 0, 1),
+    (DO_LP, 0, 2), (DO_LZ, 0, 1), (DO_GX, 0, 2), (DO_GY, 0, 1), (DO_GS, 1, 2), (DO_MODS, 0), (DO_GS, 0, 3),
+    (DO_MODS, 1), (DO_MODM, 0), (DO_GY, 0, 2), (DO_LP, 0, 3), (DO_GX, 1, 0), (DO_MODS, 2), (DO_GX, 0, 3),
+    (DO_GS, 1, 3), (DO_LZ, 0, 2), (DO_MODROWS, 0), (DO_MODULATE, 0), (DO_GY, 1, 0), (DO_OWN, 2), (DO_GX, 1, 1),
+    (DO_LZ, 0, 3), (DO_GY, 0, 3), (DO_MODM, 1), (DO_LANDED, 0), (DO_PROJECT, 0), (DO_OWN, 3), (DO_GZ, 2, 1),
+    (DO_GZ, 2, 2), (DO_GX, 1, 2), (DO_LX, 2), (DO_TURNN, 0), (DO_ATTEND, 0, 0), (DO_GX, 1, 3), (DO_GY, 1, 1),
+    (DO_ATTEND, 0, 1), (DO_MODROWS, 1), (DO_GZ, 3, 1), (DO_GZ, 3, 2), (DO_GS, 2, 0), (DO_GY, 1, 2), (DO_LX, 3),
+    (DO_ATTEND, 0, 2), (DO_LY, 2), (DO_GZ, 2, 3), (DO_GS, 2, 1), (DO_GY, 1, 3), (DO_JOIN, 0), (DO_ADD, 0),
+    (DO_GS, 2, 2), (DO_TURNA, 0), (DO_STANDARDIZE, 1), (DO_GZ, 3, 3), (DO_MODULATE, 1), (DO_GATE, 2), (DO_GX, 2, 0),
+    (DO_LANDED, 1), (DO_PROJECT, 1), (DO_LP, 2, 1), (DO_LP, 2, 2), (DO_GX, 2, 1), (DO_LZ, 2, 1), (DO_TURNN, 1),
+    (DO_GS, 3, 0), (DO_ATTEND, 1, 0), (DO_LY, 3), (DO_GS, 2, 3), (DO_GY, 2, 0), (DO_ATTEND, 1, 1), (DO_GX, 2, 2),
+    (DO_GY, 2, 1), (DO_ATTEND, 1, 2), (DO_LP, 2, 3), (DO_GS, 3, 1), (DO_JOIN, 1), (DO_LZ, 2, 2), (DO_ADD, 1),
+    (DO_GX, 2, 3), (DO_LP, 3, 1), (DO_TURNA, 1), (DO_STANDARDIZE, 2), (DO_LP, 3, 2), (DO_MODULATE, 2), (DO_GS, 3, 2),
+    (DO_GY, 2, 2), (DO_LZ, 3, 1), (DO_TURNN, 2), (DO_GS, 3, 3), (DO_LZ, 2, 3), (DO_GY, 2, 3), (DO_LP, 3, 3),
+    (DO_GX, 3, 0), (DO_LANDED, 2), (DO_EXPAND, 0), (DO_GX, 3, 1), (DO_LZ, 3, 2), (DO_SENDH, 0), (DO_EXPAND, 1),
+    (DO_GX, 3, 2), (DO_SENDH, 1), (DO_GX, 3, 3), (DO_EXPAND, 2), (DO_GY, 3, 0), (DO_LZ, 3, 3), (DO_SENDH, 2),
+    (DO_EXPAND, 3), (DO_GY, 3, 1), (DO_SENDH, 3), (DO_NEEDH, 0), (DO_DOWNT, 0), (DO_GY, 3, 2), (DO_NEEDH, 1),
+    (DO_DOWNT, 1), (DO_GY, 3, 3), (DO_NEEDH, 2), (DO_DOWNT, 2), (DO_NEEDH, 3), (DO_DOWNT, 3), (DO_TE, 0, 0),
+    (DO_SS, 0, 0), (DO_LANDED, 3), (DO_GHID, 0), (DO_GHID, 1), (DO_TE, 0, 1), (DO_SS, 0, 1), (DO_SENDP,),
+    (DO_GHID, 2), (DO_GHID, 3), (DO_SS, 0, 2), (DO_NEEDP,), (DO_UPT, 3), (DO_TE, 0, 2), (DO_UPT, 0), (DO_SY, 0, 0),
+    (DO_TZ, 0, 0), (DO_UPT, 1), (DO_UPT, 2), (DO_SS, 0, 3), (DO_SY, 0, 1), (DO_TE, 1, 0), (DO_CONTRACT,),
+    (DO_TZ, 0, 1), (DO_CLOSE,), (DO_BACK2, 0), (DO_SX, 0, 0), (DO_SS, 1, 0), (DO_SY, 0, 2), (DO_TZ, 0, 2),
+    (DO_BACK2, 1), (DO_BACK2, 2), (DO_SX, 0, 1), (DO_BACK2, 3), (DO_NORMB, 2), (DO_TE, 1, 1), (DO_SS, 1, 1),
+    (DO_TZ, 1, 0), (DO_SY, 0, 3), (DO_GATE, 1), (DO_SX, 0, 2), (DO_SPLIT, 1), (DO_SZ, 0, 0), (DO_SY, 1, 0),
+    (DO_TTOT, 0), (DO_ATTB, 1, 0), (DO_SZ, 0, 1), (DO_SS, 1, 2), (DO_ATTB, 1, 1), (DO_SX, 0, 3), (DO_TE, 1, 2),
+    (DO_SY, 1, 1), (DO_NEEDG, 1), (DO_OUTT, 1), (DO_SX, 1, 0), (DO_SS, 1, 3), (DO_TZ, 1, 1), (DO_TY, 0),
+    (DO_SZ, 0, 2), (DO_TZ, 1, 2), (DO_ATTB, 1, 2), (DO_SENDQ, 1), (DO_BACK, 1, 0), (DO_SY, 1, 2), (DO_SX, 1, 1),
+    (DO_NEEDQ, 1), (DO_QKVT, 1, 0), (DO_TX, 0), (DO_QKVT, 1, 1), (DO_SFIN, 0), (DO_SWAP, 0), (DO_QKVT, 1, 2),
+    (DO_SY, 1, 3), (DO_RETIRE, 0), (DO_SZ, 1, 0), (DO_CWAIT, 2), (DO_SX, 1, 2), (DO_SS, 2, 0), (DO_BACK, 1, 1),
+    (DO_TE, 2, 0), (DO_TTOT, 1), (DO_BACK, 1, 2), (DO_SZ, 1, 1), (DO_NORMB, 1), (DO_SX, 1, 3), (DO_TE, 2, 1),
+    (DO_SS, 2, 1), (DO_ROWM, 1), (DO_SENTQ, 1), (DO_GATE, 0), (DO_SZ, 1, 2), (DO_SY, 2, 0), (DO_SPLIT, 0), (DO_TY, 1),
+    (DO_ATTB, 0, 0), (DO_TE, 2, 2), (DO_TZ, 2, 0), (DO_ATTB, 0, 1), (DO_SFIN, 1), (DO_SS, 2, 2), (DO_SY, 2, 1),
+    (DO_NEEDG, 0), (DO_OUTT, 0), (DO_TZ, 2, 1), (DO_ROWZ, 1), (DO_ATTB, 0, 2), (DO_SX, 2, 0), (DO_SS, 2, 3),
+    (DO_TX, 1), (DO_TZ, 2, 2), (DO_SWAP, 1), (DO_SENDQ, 0), (DO_BACK, 0, 0), (DO_RETIRE, 1), (DO_SX, 2, 1),
+    (DO_CWAIT, 3), (DO_ROWP, 1, 1), (DO_NEEDQ, 0), (DO_QKVT, 0, 0), (DO_TE, 3, 0), (DO_SY, 2, 2), (DO_QKVT, 0, 1),
+    (DO_QKVT, 0, 2), (DO_SS, 3, 0), (DO_SZ, 2, 0), (DO_BACK, 0, 1), (DO_SY, 2, 3), (DO_TE, 3, 1), (DO_ROWP, 1, 2),
+    (DO_TTOT, 2), (DO_BACK, 0, 2), (DO_SZ, 2, 1), (DO_SX, 2, 2), (DO_ROWP, 1, 3), (DO_NORMB, 0), (DO_SS, 3, 1),
+    (DO_ROWM, 0), (DO_SENTQ, 0), (DO_SZ, 2, 2), (DO_TZ, 3, 0), (DO_SY, 3, 0), (DO_SX, 2, 3), (DO_TY, 2), (DO_ROWT, 1),
+    (DO_TE, 3, 2), (DO_SS, 3, 2), (DO_ROWD, 1), (DO_TZ, 3, 1), (DO_SX, 3, 0), (DO_SS, 3, 3), (DO_SFIN, 2),
+    (DO_TZ, 3, 2), (DO_SY, 3, 1), (DO_TX, 2), (DO_ROWZ, 0), (DO_SWAP, 2), (DO_RETIRE, 2), (DO_SY, 3, 2),
+    (DO_SX, 3, 1), (DO_SZ, 3, 0), (DO_TTOT, 3), (DO_ROWP, 0, 1), (DO_ROWP, 0, 2), (DO_SY, 3, 3), (DO_SX, 3, 2),
+    (DO_TY, 3), (DO_SZ, 3, 1), (DO_SZ, 3, 2), (DO_ROWP, 0, 3), (DO_SX, 3, 3), (DO_TX, 3), (DO_SFIN, 3), (DO_SWAP, 3),
+    (DO_ROWT, 0), (DO_RETIRE, 3), (DO_ROWD, 0),
 )
 
 
 def dot(left, right):
     return jnp.dot(left, right, preferred_element_type=jnp.float32)
+
+
+GATHER_CHUNKS = (3, 4, 3, 3)
 
 
 def layer_kernel(
@@ -832,13 +843,14 @@
             swap_sems.at[g],
             gather_send.at[g],
             gather_recv.at[g],
+            GATHER_CHUNKS[g],
         )
         for g in range(4)
     ]
     scatters = [
         Scatter(
             spot,
-            sums.at[n % 2],
+            held.at[2, n - 2] if n >= 2 else sums.at[n],
             from_second.at[n % 2],
             from_first.at[n % 2],
             from_z.at[n % 2],
@@ -966,24 +978,37 @@
     class ModPart:
         def __init__(self, part):
             self.part, self.n = part, len(parts[part])
-            base, n = 21 * part, self.n
-            self.out, self.into, self.sum = (sums.at[1, pl.ds(base + 4 * n * i, 4 * n)] for i in range(3))
-            self.own = sums.at[1, pl.ds(base + 16 * n, n)]
-            self.line = Exchange(
-                spot.line,
-                spot.z,
-                lambda z: sums.at[1, pl.ds(base + 8 * n + n * z, n)],
-                lambda z: sums.at[1, pl.ds(base + 12 * n + n * z, n)],
-                mod_send.at[part, pl.ds(1, 3)],
-                mod_recv.at[part, pl.ds(4, 4)],
-            )
+            n, base = self.n, 6 * part
+
+            def region(i):
+                return pl.ds(base + n * i, n)
+
+            self.out, self.into, self.sum = (sums.at[1, region(i)] for i in range(3))
+            self.own = sums.at[1, 5, pl.ds(part, n)]
+            if part:
+                self.line = LineSum(
+                    spot,
+                    lambda z: sums.at[1, region(2), z],
+                    lambda i: sums.at[1, region(3), i] if i < 4 else self.own,
+                    mod_send.at[part, pl.ds(1, 3)],
+                    mod_recv.at[part, pl.ds(1, 5)],
+                )
+            else:
+                self.line = Exchange(
+                    spot.line,
+                    spot.z,
+                    lambda z: sums.at[1, region(2), z],
+                    lambda z: sums.at[1, region(3), z],
+                    mod_send.at[part, pl.ds(1, 3)],
+                    mod_recv.at[part, pl.ds(1, 4)],
+                )
             self.mates = Exchange(
                 spot.mates,
                 spot.plane,
                 lambda plane: self.own,
-                lambda plane: sums.at[1, pl.ds(base + 17 * n + n * plane, n)],
+                lambda plane: sums.at[1, region(4), plane],
                 mod_send.at[part, pl.ds(4, 3)],
-                mod_recv.at[part, pl.ds(8, 4)],
+                mod_recv.at[part, pl.ds(6, 4)],
             )
 
         def swap(self):
@@ -1002,26 +1027,36 @@
                     for z in range(4):
                         own = slice(8 * z, 8 * z + 8)
                         block = jnp.concatenate([left[own], right[own]], axis=0)
-                        yield self.n * z + i, rows_of(chunk), block
+                        yield (i, z, rows_of(chunk)), block
 
         def for_twin(self):
-            for at, rows, value in self.terms(1 - core):
-                self.out[at, rows] = value.astype(bf16)
+            for at, value in self.terms(1 - core):
+                self.out[at] = value.astype(bf16)
             self.swap().start()
 
         def for_line(self):
             self.swap().wait_recv()
-            for at, rows, value in self.terms(core):
-                self.sum[at, rows] = (value + self.into[at, rows].astype(f32)).astype(bf16)
-            self.line.start()
+            for at, value in self.terms(core):
+                self.sum[at] = (value + self.into[at].astype(f32)).astype(bf16)
+            if self.part:
+                for k in range(3):
+                    self.line.send_end(k)
+            else:
+                self.line.start()
 
         def for_mates(self):
-            self.line.arrive()
-            for i in range(self.n):
-                value = self.line.src(spot.z)[i].astype(f32)
-                for z, _ in spot.line:
-                    value += self.line.dst(z)[i].astype(f32)
+            def put(i, value):
                 self.own[i] = value.astype(bf16)
+
+            if self.part:
+                self.line.total(put)
+            else:
+                self.line.arrive()
+                for i in range(self.n):
+                    value = self.line.src(spot.z)[i].astype(f32)
+                    for z, _ in spot.line:
+                        value += self.line.dst(z)[i].astype(f32)
+                    put(i, value)
             self.mates.start()
 
         def done(self):
@@ -1053,16 +1088,14 @@
                 spot.plane,
                 lambda plane: rows_mod.at[spot.plane, subs],
                 lambda plane: rows_mod.at[plane, subs],
-                row_send.at[part, pl.ds(4, 3)],
-                row_recv.at[part, pl.ds(8, 4)],
+                row_send.at[part, pl.ds(1, 3)],
+                row_recv.at[part, pl.ds(1, 4)],
             )
-            self.line = Exchange(
-                spot.line,
-                spot.z,
-                lambda z: all_rows_mod.at[core, spot.z, subs],
+            self.line = LineGather(
+                spot,
                 lambda z: all_rows_mod.at[core, z, subs],
-                row_send.at[part, pl.ds(1, 3)],
-                row_recv.at[part, pl.ds(4, 4)],
+                row_send.at[part, pl.ds(4, 5)],
+                row_recv.at[part, pl.ds(5, 4)],
             )
 
         def swap(self, owner):
@@ -1088,10 +1121,11 @@
                 all_rows_mod[core, spot.z, j] = (rows_mod[0, j] + rows_mod[1, j]) + (
                     rows_mod[2, j] + rows_mod[3, j]
                 )
-            self.line.start()
+            self.line.open()
 
         def for_twin(self):
-            self.line.arrive()
+            for k in (1, 2, 3):
+                self.line.take(k)
             self.swap(core).start()
 
         def done(self):
@@ -1247,14 +1281,13 @@
         )
         value = value.astype(bf16).reshape(4, 4, 48, 384)
         for plane in range(4):
-            sums[0, pl.ds(scatter.place(4 * z + plane, 0), 3)] = value[plane, :3]
-            sums[0, scatter.place(4 * z + plane, 3)] = value[plane, 3]
+            scatter.sums[scatter.place(4 * z + plane)] = value[plane]
 
     def column_terms(n, chunk, left, right, right_twin):
         value = dot(turned[left, 0], right) + dot(turned[left, 1], right_twin)
         value = value.astype(bf16).reshape(16, 48, 384)
         for chip in range(16):
-            sums[n % 2, scatters[n].place(chip, chunk)] = value[chip]
+            scatters[n].sums[scatters[n].place(chip), chunk] = value[chip]
 
     def up_terms(chunk):
         column_terms(
@@ -1393,6 +1426,12 @@
             gated_copy(2).wait_recv()
         hidden_copy(i).wait_recv()
 
+    def need_gated(j):
+        if j == 1:
+            gathers[2].drain()
+        need(turned_copy, 2 * j + 1)
+        need(gated_copy, j)
+
     def retire(n):
         scatters[n].store(puts[n])
         scatters[n].drain()
@@ -1410,6 +1449,7 @@
         DO_COND: make_cond,
         DO_MODT: lambda part: mod_parts[part].for_twin(),
         DO_MODZ: lambda part: mod_parts[part].for_line(),
+        DO_MODS: lambda k: mod_parts[1].line.send_middle(k),
         DO_MODM: lambda part: mod_parts[part].for_mates(),
         DO_MODROWS: lambda part: mod_parts[part].done(),
         DO_OWN: lambda g: gathers[g].own(),
@@ -1437,6 +1477,7 @@
         DO_RETIRE: retire,
         DO_ROWM: lambda part: row_parts[part].for_mates(),
         DO_ROWZ: lambda part: row_parts[part].for_line(),
+        DO_ROWP: lambda part, k: row_parts[part].line.pass_on(k),
         DO_ROWT: lambda part: row_parts[part].for_twin(),
         DO_ROWD: lambda part: row_parts[part].done(),
         DO_MASKS: masks,
@@ -1464,7 +1505,7 @@
         DO_SPLIT: split,
         DO_ATTB: lambda j, i: attend_back(j, 2 * i, 2 * i + 2),
         DO_SENDQ: lambda j: grad_qkv_copy(j).start(),
-        DO_NEEDG: lambda j: (need(turned_copy, 2 * j + 1), need(gated_copy, j)),
+        DO_NEEDG: need_gated,
         DO_NEEDQ: lambda j: (
             need(turned_copy, 2 * j),
             need(grad_qkv_copy, j),
@@ -1485,8 +1526,8 @@
             step(*indices)
     for part in row_parts:
         part.drain()
-    for gather in gathers:
-        gather.drain()
+    for g in (0, 1, 3):
+        gathers[g].drain()
     for copy in each_twin_copy():
         copy.wait_send()
 
@@ -1548,8 +1589,8 @@
             vmem((4,) + block, f32),
             vmem((3, 4, 24, 384), f32),
             vmem((2, 48, 384), f32),
-            vmem((2, 64, 48, 384), bf16),
-            vmem((2, 4, 6, 48, 384), bf16),
+            vmem((2, 16) + block, bf16),
+            vmem((2, 4, 2, 3, 48, 384), bf16),
             vmem((2, 4, 3, 48, 384), bf16),
             vmem((2, 5, 3, 48, 384), bf16),
             vmem((2, 2, 48, 384), bf16),
@@ -1591,9 +1632,9 @@
             dma((7,)),
             dma((12,)),
             dma((2, 7)),
-            dma((2, 12)),
-            dma((2, 7)),
-            dma((2, 12)),
+            dma((2, 10)),
+            dma((2, 9)),
+            dma((2, 9)),
         ],
         compiler_params=pltpu.CompilerParams(
             collective_id=0, has_side_effects=True, vmem_limit_bytes=64 * 2**20

time: 186 us -> 176 us (0.946)
  Pallas kernels: 183 us -> 173 us
    pallas_call x1, Pallas kernels: 179 us -> 169 us  [layer(): pl.pallas_call(layer_kernel, out_shape=[jax.ShapeDtypeStruct((tok, width)...]
where the time goes in v6:
time: 176 us
  Pallas kernels  173 us (98%)
    pallas_call x1, Pallas kernels, layer(): pl.pallas_call(layer_kernel, out_shape=[jax.ShapeDtypeStruct((tok, width)...  169 us
    pallas_call x1, Pallas kernels, layer(): pl.pallas_call(finish_kernel, out_shape=[jax.ShapeDtypeStruct(w_ada.shape...  4.7 us

profile of v6, /device:TPU:0, one launch (start us, length us, event | category | flops | bytes accessed | tf_op | source)
XLA Modules:
  0.0 175.5 jit_solution(13214847331618752458)
XLA Ops:
  0.6 0.0 copy-start
  0.7 0.6 copy-done
  1.3 0.6 broadcast_in_dim.19.b_ada
  1.9 168.8 %shard_map.213 = (bf16[256,768]{1,0:T(8,128)(2,1)}, f32[256,768]{1,0:T(8,128)}, bf16[64,128]{1,0:T(8,128)(2,1)}, bf16[2,4,3,16,1152]{4,3,2,1,0:T(8,128)(2,1)}, f...) custom-call(bf16[256,768]{1,0:T(8,128)(2,1)} %tokens.1, ...), custom_call_target="tpu_custom_call" | custom-call | tf_op jit(solution)/shard_map/pallas_call | solution.py:1576
  170.6 4.7 %shard_map.214 = (f32[24,6912]{1,0:T(8,128)}, f32[1,216]{1,0:T(1,128)}, bf16[256,768]{1,0:T(8,128)(2,1)}, f32[256,768]{1,0:T(8,128)}, f32[24,2304]{1,0:T(8,128)}...) custom-call(bf16[64,128]{1,0:T(8,128)(2,1)} %get-tuple-element.30.co, ...), custom_call_target="tpu_custom_call" | custom-call | tf_op jit(solution)/shard_map/pallas_call | solution.py:1644
Async XLA Ops:
  0.6 0.7 copy-start

commit v7 on v6

--- a/solution.py
+++ b/solution.py
@@ -173,10 +173,11 @@
         return (self.z, self.layer(1 - self.middle), self.layer(2), self.layer(3))[k]
 
 
-def greet(spot):
+def greet(spot, meanwhile):
     barrier = pltpu.get_barrier_semaphore()
     for device in [spot.twin] + [device for _, device in spot.mates + tuple(spot.line)]:
         pl.semaphore_signal(barrier, inc=1, device_id=device, device_id_type=MESH)
+    meanwhile()
     pl.semaphore_wait(barrier, 7)
 
 
@@ -354,7 +355,6 @@
         core = self.spot.core
         for chunk in range(self.apart.shape[0]):
             self.apart[chunk] = piece(1 - core, chunk).astype(jnp.float32)
-        self.swap().start()
         place = self.mine()
         for chunk in range(self.apart.shape[0]):
             place[chunk] = piece(core, chunk).astype(jnp.float32)
@@ -676,50 +676,50 @@
 
 ORDER = (
     (DO_CWAIT, 0), (DO_CWAIT, 1), (DO_MASKS,), (DO_STANDARDIZE, 0), (DO_STEPS, 0), (DO_OWN, 0), (DO_GS, 0, 0),
-    (DO_OWN, 1), (DO_GS, 1, 0), (DO_STEPS, 1), (DO_LX, 0), (DO_GZ, 0, 1), (DO_GZ, 0, 2), (DO_GS, 0, 1), (DO_GZ, 1, 1),
-    (DO_GZ, 1, 2), (DO_GX, 0, 0), (DO_LY, 0), (DO_GS, 0, 2), (DO_GZ, 0, 3), (DO_COND,), (DO_MODT, 0), (DO_MODT, 1),
-    (DO_MODZ, 0), (DO_GX, 0, 1), (DO_GZ, 1, 3), (DO_GS, 1, 1), (DO_MODZ, 1), (DO_GY, 0, 0), (DO_LP, 0, 1),
-    (DO_LP, 0, 2), (DO_LZ, 0, 1), (DO_GX, 0, 2), (DO_GY, 0, 1), (DO_GS, 1, 2), (DO_MODS, 0), (DO_GS, 0, 3),
-    (DO_MODS, 1), (DO_MODM, 0), (DO_GY, 0, 2), (DO_LP, 0, 3), (DO_GX, 1, 0), (DO_MODS, 2), (DO_GX, 0, 3),
-    (DO_GS, 1, 3), (DO_LZ, 0, 2), (DO_MODROWS, 0), (DO_MODULATE, 0), (DO_GY, 1, 0), (DO_OWN, 2), (DO_GX, 1, 1),
-    (DO_LZ, 0, 3), (DO_GY, 0, 3), (DO_MODM, 1), (DO_LANDED, 0), (DO_PROJECT, 0), (DO_OWN, 3), (DO_GZ, 2, 1),
-    (DO_GZ, 2, 2), (DO_GX, 1, 2), (DO_LX, 2), (DO_TURNN, 0), (DO_ATTEND, 0, 0), (DO_GX, 1, 3), (DO_GY, 1, 1),
-    (DO_ATTEND, 0, 1), (DO_MODROWS, 1), (DO_GZ, 3, 1), (DO_GZ, 3, 2), (DO_GS, 2, 0), (DO_GY, 1, 2), (DO_LX, 3),
-    (DO_ATTEND, 0, 2), (DO_LY, 2), (DO_GZ, 2, 3), (DO_GS, 2, 1), (DO_GY, 1, 3), (DO_JOIN, 0), (DO_ADD, 0),
-    (DO_GS, 2, 2), (DO_TURNA, 0), (DO_STANDARDIZE, 1), (DO_GZ, 3, 3), (DO_MODULATE, 1), (DO_GATE, 2), (DO_GX, 2, 0),
-    (DO_LANDED, 1), (DO_PROJECT, 1), (DO_LP, 2, 1), (DO_LP, 2, 2), (DO_GX, 2, 1), (DO_LZ, 2, 1), (DO_TURNN, 1),
-    (DO_GS, 3, 0), (DO_ATTEND, 1, 0), (DO_LY, 3), (DO_GS, 2, 3), (DO_GY, 2, 0), (DO_ATTEND, 1, 1), (DO_GX, 2, 2),
-    (DO_GY, 2, 1), (DO_ATTEND, 1, 2), (DO_LP, 2, 3), (DO_GS, 3, 1), (DO_JOIN, 1), (DO_LZ, 2, 2), (DO_ADD, 1),
-    (DO_GX, 2, 3), (DO_LP, 3, 1), (DO_TURNA, 1), (DO_STANDARDIZE, 2), (DO_LP, 3, 2), (DO_MODULATE, 2), (DO_GS, 3, 2),
-    (DO_GY, 2, 2), (DO_LZ, 3, 1), (DO_TURNN, 2), (DO_GS, 3, 3), (DO_LZ, 2, 3), (DO_GY, 2, 3), (DO_LP, 3, 3),
-    (DO_GX, 3, 0), (DO_LANDED, 2), (DO_EXPAND, 0), (DO_GX, 3, 1), (DO_LZ, 3, 2), (DO_SENDH, 0), (DO_EXPAND, 1),
-    (DO_GX, 3, 2), (DO_SENDH, 1), (DO_GX, 3, 3), (DO_EXPAND, 2), (DO_GY, 3, 0), (DO_LZ, 3, 3), (DO_SENDH, 2),
-    (DO_EXPAND, 3), (DO_GY, 3, 1), (DO_SENDH, 3), (DO_NEEDH, 0), (DO_DOWNT, 0), (DO_GY, 3, 2), (DO_NEEDH, 1),
-    (DO_DOWNT, 1), (DO_GY, 3, 3), (DO_NEEDH, 2), (DO_DOWNT, 2), (DO_NEEDH, 3), (DO_DOWNT, 3), (DO_TE, 0, 0),
-    (DO_SS, 0, 0), (DO_LANDED, 3), (DO_GHID, 0), (DO_GHID, 1), (DO_TE, 0, 1), (DO_SS, 0, 1), (DO_SENDP,),
-    (DO_GHID, 2), (DO_GHID, 3), (DO_SS, 0, 2), (DO_NEEDP,), (DO_UPT, 3), (DO_TE, 0, 2), (DO_UPT, 0), (DO_SY, 0, 0),
-    (DO_TZ, 0, 0), (DO_UPT, 1), (DO_UPT, 2), (DO_SS, 0, 3), (DO_SY, 0, 1), (DO_TE, 1, 0), (DO_CONTRACT,),
-    (DO_TZ, 0, 1), (DO_CLOSE,), (DO_BACK2, 0), (DO_SX, 0, 0), (DO_SS, 1, 0), (DO_SY, 0, 2), (DO_TZ, 0, 2),
-    (DO_BACK2, 1), (DO_BACK2, 2), (DO_SX, 0, 1), (DO_BACK2, 3), (DO_NORMB, 2), (DO_TE, 1, 1), (DO_SS, 1, 1),
-    (DO_TZ, 1, 0), (DO_SY, 0, 3), (DO_GATE, 1), (DO_SX, 0, 2), (DO_SPLIT, 1), (DO_SZ, 0, 0), (DO_SY, 1, 0),
-    (DO_TTOT, 0), (DO_ATTB, 1, 0), (DO_SZ, 0, 1), (DO_SS, 1, 2), (DO_ATTB, 1, 1), (DO_SX, 0, 3), (DO_TE, 1, 2),
-    (DO_SY, 1, 1), (DO_NEEDG, 1), (DO_OUTT, 1), (DO_SX, 1, 0), (DO_SS, 1, 3), (DO_TZ, 1, 1), (DO_TY, 0),
-    (DO_SZ, 0, 2), (DO_TZ, 1, 2), (DO_ATTB, 1, 2), (DO_SENDQ, 1), (DO_BACK, 1, 0), (DO_SY, 1, 2), (DO_SX, 1, 1),
-    (DO_NEEDQ, 1), (DO_QKVT, 1, 0), (DO_TX, 0), (DO_QKVT, 1, 1), (DO_SFIN, 0), (DO_SWAP, 0), (DO_QKVT, 1, 2),
-    (DO_SY, 1, 3), (DO_RETIRE, 0), (DO_SZ, 1, 0), (DO_CWAIT, 2), (DO_SX, 1, 2), (DO_SS, 2, 0), (DO_BACK, 1, 1),
-    (DO_TE, 2, 0), (DO_TTOT, 1), (DO_BACK, 1, 2), (DO_SZ, 1, 1), (DO_NORMB, 1), (DO_SX, 1, 3), (DO_TE, 2, 1),
-    (DO_SS, 2, 1), (DO_ROWM, 1), (DO_SENTQ, 1), (DO_GATE, 0), (DO_SZ, 1, 2), (DO_SY, 2, 0), (DO_SPLIT, 0), (DO_TY, 1),
-    (DO_ATTB, 0, 0), (DO_TE, 2, 2), (DO_TZ, 2, 0), (DO_ATTB, 0, 1), (DO_SFIN, 1), (DO_SS, 2, 2), (DO_SY, 2, 1),
-    (DO_NEEDG, 0), (DO_OUTT, 0), (DO_TZ, 2, 1), (DO_ROWZ, 1), (DO_ATTB, 0, 2), (DO_SX, 2, 0), (DO_SS, 2, 3),
-    (DO_TX, 1), (DO_TZ, 2, 2), (DO_SWAP, 1), (DO_SENDQ, 0), (DO_BACK, 0, 0), (DO_RETIRE, 1), (DO_SX, 2, 1),
-    (DO_CWAIT, 3), (DO_ROWP, 1, 1), (DO_NEEDQ, 0), (DO_QKVT, 0, 0), (DO_TE, 3, 0), (DO_SY, 2, 2), (DO_QKVT, 0, 1),
-    (DO_QKVT, 0, 2), (DO_SS, 3, 0), (DO_SZ, 2, 0), (DO_BACK, 0, 1), (DO_SY, 2, 3), (DO_TE, 3, 1), (DO_ROWP, 1, 2),
-    (DO_TTOT, 2), (DO_BACK, 0, 2), (DO_SZ, 2, 1), (DO_SX, 2, 2), (DO_ROWP, 1, 3), (DO_NORMB, 0), (DO_SS, 3, 1),
-    (DO_ROWM, 0), (DO_SENTQ, 0), (DO_SZ, 2, 2), (DO_TZ, 3, 0), (DO_SY, 3, 0), (DO_SX, 2, 3), (DO_TY, 2), (DO_ROWT, 1),
-    (DO_TE, 3, 2), (DO_SS, 3, 2), (DO_ROWD, 1), (DO_TZ, 3, 1), (DO_SX, 3, 0), (DO_SS, 3, 3), (DO_SFIN, 2),
-    (DO_TZ, 3, 2), (DO_SY, 3, 1), (DO_TX, 2), (DO_ROWZ, 0), (DO_SWAP, 2), (DO_RETIRE, 2), (DO_SY, 3, 2),
-    (DO_SX, 3, 1), (DO_SZ, 3, 0), (DO_TTOT, 3), (DO_ROWP, 0, 1), (DO_ROWP, 0, 2), (DO_SY, 3, 3), (DO_SX, 3, 2),
-    (DO_TY, 3), (DO_SZ, 3, 1), (DO_SZ, 3, 2), (DO_ROWP, 0, 3), (DO_SX, 3, 3), (DO_TX, 3), (DO_SFIN, 3), (DO_SWAP, 3),
+    (DO_OWN, 1), (DO_GS, 1, 0), (DO_STEPS, 1), (DO_GZ, 0, 1), (DO_GS, 0, 1), (DO_GZ, 0, 2), (DO_LX, 1), (DO_GX, 0, 0),
+    (DO_GZ, 1, 1), (DO_GZ, 1, 2), (DO_GS, 1, 1), (DO_COND,), (DO_MODT, 0), (DO_MODT, 1), (DO_GZ, 0, 3), (DO_GS, 0, 2),
+    (DO_MODZ, 0), (DO_GZ, 1, 3), (DO_MODZ, 1), (DO_GX, 0, 1), (DO_GY, 0, 0), (DO_GS, 1, 2), (DO_LY, 1), (DO_GS, 0, 3),
+    (DO_MODS, 0), (DO_MODM, 0), (DO_MODS, 1), (DO_GX, 0, 2), (DO_OWN, 2), (DO_GY, 0, 1), (DO_LP, 1, 2), (DO_GX, 0, 3),
+    (DO_MODS, 2), (DO_LP, 1, 1), (DO_LZ, 1, 1), (DO_LX, 2), (DO_GS, 1, 3), (DO_MODROWS, 0), (DO_MODULATE, 0),
+    (DO_GZ, 2, 1), (DO_GY, 0, 2), (DO_GZ, 2, 2), (DO_GX, 1, 0), (DO_LZ, 1, 2), (DO_GX, 1, 1), (DO_GY, 0, 3),
+    (DO_LP, 1, 3), (DO_MODM, 1), (DO_LY, 2), (DO_GX, 1, 2), (DO_LANDED, 0), (DO_PROJECT, 0), (DO_GY, 1, 0),
+    (DO_GZ, 2, 3), (DO_GX, 1, 3), (DO_TURNN, 0), (DO_MODROWS, 1), (DO_GY, 1, 1), (DO_GS, 2, 0), (DO_ATTEND, 0, 0),
+    (DO_GY, 1, 2), (DO_LZ, 1, 3), (DO_LP, 2, 1), (DO_LP, 2, 2), (DO_GS, 2, 1), (DO_ATTEND, 0, 1), (DO_GY, 1, 3),
+    (DO_LZ, 2, 1), (DO_GS, 2, 2), (DO_OWN, 3), (DO_ATTEND, 0, 2), (DO_GS, 2, 3), (DO_JOIN, 0), (DO_ADD, 0),
+    (DO_LP, 2, 3), (DO_TURNA, 0), (DO_GX, 2, 0), (DO_STANDARDIZE, 1), (DO_MODULATE, 1), (DO_LZ, 2, 2), (DO_GZ, 3, 1),
+    (DO_GZ, 3, 2), (DO_GATE, 2), (DO_GX, 2, 1), (DO_LX, 3), (DO_LANDED, 1), (DO_PROJECT, 1), (DO_GX, 2, 2),
+    (DO_TURNN, 1), (DO_GY, 2, 0), (DO_GX, 2, 3), (DO_ATTEND, 1, 0), (DO_GY, 2, 1), (DO_LZ, 2, 3), (DO_GZ, 3, 3),
+    (DO_GS, 3, 0), (DO_LY, 3), (DO_ATTEND, 1, 1), (DO_GY, 2, 2), (DO_GS, 3, 1), (DO_GY, 2, 3), (DO_ATTEND, 1, 2),
+    (DO_GS, 3, 2), (DO_JOIN, 1), (DO_ADD, 1), (DO_GS, 3, 3), (DO_TURNA, 1), (DO_LP, 3, 1), (DO_LP, 3, 2),
+    (DO_STANDARDIZE, 2), (DO_MODULATE, 2), (DO_GX, 3, 0), (DO_TURNN, 2), (DO_LZ, 3, 1), (DO_LANDED, 2),
+    (DO_EXPAND, 0), (DO_SENDH, 0), (DO_GX, 3, 1), (DO_EXPAND, 1), (DO_GX, 3, 2), (DO_SENDH, 1), (DO_EXPAND, 2),
+    (DO_LP, 3, 3), (DO_LZ, 3, 2), (DO_GX, 3, 3), (DO_SENDH, 2), (DO_EXPAND, 3), (DO_GY, 3, 0), (DO_SENDH, 3),
+    (DO_GY, 3, 1), (DO_NEEDH, 0), (DO_DOWNT, 0), (DO_NEEDH, 1), (DO_DOWNT, 1), (DO_GY, 3, 2), (DO_NEEDH, 2),
+    (DO_DOWNT, 2), (DO_GY, 3, 3), (DO_NEEDH, 3), (DO_DOWNT, 3), (DO_TE, 0, 0), (DO_SS, 0, 0), (DO_TE, 0, 1),
+    (DO_LZ, 3, 3), (DO_LANDED, 3), (DO_SS, 0, 1), (DO_GHID, 0), (DO_GHID, 1), (DO_SENDP,), (DO_GHID, 2),
+    (DO_TE, 0, 2), (DO_SS, 0, 2), (DO_GHID, 3), (DO_SY, 0, 0), (DO_NEEDP,), (DO_UPT, 3), (DO_TZ, 0, 0), (DO_UPT, 0),
+    (DO_TE, 1, 0), (DO_UPT, 1), (DO_SY, 0, 1), (DO_UPT, 2), (DO_SS, 0, 3), (DO_CONTRACT,), (DO_SX, 0, 0),
+    (DO_TZ, 0, 1), (DO_CLOSE,), (DO_SY, 0, 2), (DO_BACK2, 0), (DO_TE, 1, 1), (DO_TZ, 0, 2), (DO_SX, 0, 1),
+    (DO_SS, 1, 0), (DO_BACK2, 1), (DO_BACK2, 2), (DO_SY, 0, 3), (DO_BACK2, 3), (DO_TZ, 1, 0), (DO_SX, 0, 2),
+    (DO_SS, 1, 1), (DO_NORMB, 2), (DO_GATE, 1), (DO_SZ, 0, 0), (DO_SS, 1, 2), (DO_SPLIT, 1), (DO_SY, 1, 0),
+    (DO_TTOT, 0), (DO_ATTB, 1, 0), (DO_SX, 0, 3), (DO_SY, 1, 1), (DO_TE, 1, 2), (DO_TZ, 1, 1), (DO_TZ, 1, 2),
+    (DO_ATTB, 1, 1), (DO_SZ, 0, 1), (DO_SZ, 0, 2), (DO_SX, 1, 0), (DO_SS, 1, 3), (DO_NEEDG, 1), (DO_OUTT, 1),
+    (DO_ATTB, 1, 2), (DO_SY, 1, 2), (DO_SX, 1, 1), (DO_TY, 0), (DO_SENDQ, 1), (DO_BACK, 1, 0), (DO_TTOT, 1),
+    (DO_NEEDQ, 1), (DO_QKVT, 1, 0), (DO_SY, 1, 3), (DO_SFIN, 0), (DO_QKVT, 1, 1), (DO_SZ, 1, 0), (DO_SX, 1, 2),
+    (DO_TX, 0), (DO_SWAP, 0), (DO_QKVT, 1, 2), (DO_TY, 1), (DO_BACK, 1, 1), (DO_SZ, 1, 1), (DO_RETIRE, 0),
+    (DO_SX, 1, 3), (DO_CWAIT, 2), (DO_TE, 2, 0), (DO_SS, 2, 0), (DO_BACK, 1, 2), (DO_TE, 2, 1), (DO_TX, 1),
+    (DO_NORMB, 1), (DO_SZ, 1, 2), (DO_ROWM, 1), (DO_SS, 2, 1), (DO_SENTQ, 1), (DO_GATE, 0), (DO_TE, 2, 2),
+    (DO_SPLIT, 0), (DO_ATTB, 0, 0), (DO_SY, 2, 0), (DO_TZ, 2, 0), (DO_ATTB, 0, 1), (DO_ROWZ, 1), (DO_SY, 2, 1),
+    (DO_TZ, 2, 1), (DO_SFIN, 1), (DO_SWAP, 1), (DO_SS, 2, 2), (DO_NEEDG, 0), (DO_OUTT, 0), (DO_SX, 2, 0),
+    (DO_RETIRE, 1), (DO_ATTB, 0, 2), (DO_CWAIT, 3), (DO_TE, 3, 0), (DO_TZ, 2, 2), (DO_SS, 2, 3), (DO_SENDQ, 0),
+    (DO_SX, 2, 1), (DO_BACK, 0, 0), (DO_ROWP, 1, 1), (DO_ROWP, 1, 2), (DO_NEEDQ, 0), (DO_SY, 2, 2), (DO_QKVT, 0, 0),
+    (DO_QKVT, 0, 1), (DO_SZ, 2, 0), (DO_QKVT, 0, 2), (DO_TE, 3, 1), (DO_SS, 3, 0), (DO_BACK, 0, 1), (DO_BACK, 0, 2),
+    (DO_SY, 2, 3), (DO_SX, 2, 2), (DO_TZ, 3, 0), (DO_TTOT, 2), (DO_SS, 3, 1), (DO_ROWP, 1, 3), (DO_NORMB, 0),
+    (DO_ROWM, 0), (DO_SZ, 2, 1), (DO_TE, 3, 2), (DO_SENTQ, 0), (DO_SZ, 2, 2), (DO_SY, 3, 0), (DO_SX, 2, 3),
+    (DO_SS, 3, 2), (DO_TY, 2), (DO_ROWT, 1), (DO_TZ, 3, 1), (DO_TZ, 3, 2), (DO_ROWD, 1), (DO_SS, 3, 3), (DO_SX, 3, 0),
+    (DO_SFIN, 2), (DO_SY, 3, 1), (DO_ROWZ, 0), (DO_TX, 2), (DO_SWAP, 2), (DO_RETIRE, 2), (DO_SY, 3, 2), (DO_TTOT, 3),
+    (DO_SZ, 3, 0), (DO_SX, 3, 1), (DO_ROWP, 0, 1), (DO_ROWP, 0, 2), (DO_SY, 3, 3), (DO_SX, 3, 2), (DO_TY, 3),
+    (DO_SZ, 3, 1), (DO_SZ, 3, 2), (DO_ROWP, 0, 3), (DO_SX, 3, 3), (DO_TX, 3), (DO_SFIN, 3), (DO_SWAP, 3),
     (DO_ROWT, 0), (DO_RETIRE, 3), (DO_ROWD, 0),
 )
 
@@ -728,7 +728,7 @@
     return jnp.dot(left, right, preferred_element_type=jnp.float32)
 
 
-GATHER_CHUNKS = (3, 4, 3, 3)
+GATHER_CHUNKS = (4, 3, 3, 3)
 
 
 def layer_kernel(
@@ -746,16 +746,25 @@
     w_out_t,
     w_up,
     w_down,
+    r_layer,
+    r_tokens,
+    cond,
+    all_rows_mod,
+    r_qkv_s,
+    r_out_s,
+    r_qkv_t,
+    r_out_t,
+    r_up,
+    r_down,
     o_layer,
     o_tokens,
-    cond,
-    all_rows_mod,
     o_qkv_s,
     o_out_s,
     o_qkv_t,
     o_out_t,
     o_up,
     o_down,
+    leave_sems,
     held,
     stage,
     apart,
@@ -772,7 +781,6 @@
     ids,
     mod,
     tally,
-    rows_mod,
     xhat,
     deviation,
     normed,
@@ -812,7 +820,6 @@
     spot = Spot()
     core = spot.core
     grad_qkv, grad_normed = hidden, stream
-    greet(spot)
 
     def attention_piece(w_qkv, w_out):
         def piece(half, chunk):
@@ -927,11 +934,10 @@
         step_recv.at[pl.ds(8, 4)],
     )
 
-    def steps_open():
+    def steps_prepare():
         row = lax.broadcasted_iota(jnp.int32, (8, 128), 0)
         value = jnp.where(row == 0, steps[0, 0], jnp.where(row == 1, steps[0, 1], 0))
         all_steps[spot.z, spot.plane, core] = value.astype(f32)
-        step_twin(core).start()
 
     def steps_line():
         step_twin(1 - core).wait_recv()
@@ -1005,8 +1011,8 @@
             self.mates = Exchange(
                 spot.mates,
                 spot.plane,
-                lambda plane: self.own,
-                lambda plane: sums.at[1, region(4), plane],
+                lambda plane: sums.at[1, region(4), plane, 16:32],
+                lambda plane: sums.at[1, region(4), plane, 0:16],
                 mod_send.at[part, pl.ds(4, 3)],
                 mod_recv.at[part, pl.ds(6, 4)],
             )
@@ -1057,22 +1063,28 @@
                     for z, _ in spot.line:
                         value += self.line.dst(z)[i].astype(f32)
                     put(i, value)
+            for plane, _ in spot.mates:
+                self.mates.src(plane)[...] = self.picked(plane).astype(bf16)
             self.mates.start()
+
+        def picked(self, plane):
+            to = lax.broadcasted_iota(jnp.int32, (16, 48), 0)
+            at = lax.broadcasted_iota(jnp.int32, (16, 48), 1)
+            wanted = 16 * (to >> 2) + 8 * ((to >> 1) & 1) + 2 * plane + (to & 1)
+            pick = (at == wanted).astype(bf16)
+            return jnp.stack([dot(pick, self.own[i]) for i in range(self.n)])
 
         def done(self):
             self.mates.arrive()
-            row = lax.broadcasted_iota(jnp.int32, (16, 384), 0)
+            total = self.picked(spot.plane)
+            for plane, _ in spot.mates:
+                total += self.mates.dst(plane)[...].astype(f32)
             for i, j in enumerate(parts[self.part]):
                 for chunk in range(3):
-                    value = self.own[i, rows_of(chunk)].astype(f32)
-                    for plane, _ in spot.mates:
-                        value += self.mates.dst(plane)[i, rows_of(chunk)].astype(f32)
-                    for clip in range(2):
-                        for half in range(2):
-                            chosen = row == 8 * half + 2 * spot.plane + clip
-                            mod[clip : clip + 1, columns_of(j, half, chunk)] = jnp.sum(
-                                jnp.where(chosen, value, 0.0), axis=0, keepdims=True
-                            )
+                    for half in range(2):
+                        for clip in range(2):
+                            row = 4 * chunk + 2 * half + clip
+                            mod[clip : clip + 1, columns_of(j, half, chunk)] = total[i, row : row + 1]
 
         def drain(self):
             self.swap().wait_send()
@@ -1086,8 +1098,8 @@
             self.mates = Exchange(
                 spot.mates,
                 spot.plane,
-                lambda plane: rows_mod.at[spot.plane, subs],
-                lambda plane: rows_mod.at[plane, subs],
+                lambda plane: all_rows_mod.at[core, spot.z, subs, spot.plane],
+                lambda plane: all_rows_mod.at[core, spot.z, subs, plane],
                 row_send.at[part, pl.ds(1, 3)],
                 row_recv.at[part, pl.ds(1, 4)],
             )
@@ -1105,22 +1117,17 @@
         def for_mates(self):
             row = lax.broadcasted_iota(jnp.int32, (16, 384), 0)
             for j in parts[self.part]:
+                value = 0.0
                 for chunk in range(3):
-                    value = 0.0
-                    for clip in range(2):
-                        for half in range(2):
-                            chosen = row == 8 * half + 2 * spot.plane + clip
+                    for half in range(2):
+                        for clip in range(2):
                             own = tally[clip : clip + 1, columns_of(j, half, chunk)]
-                            value += jnp.where(chosen, own, 0.0)
-                    rows_mod[spot.plane, j, :, 384 * chunk : 384 * chunk + 384] = value.astype(bf16)
+                            value += jnp.where(row == 4 * chunk + 2 * half + clip, own, 0.0)
+                all_rows_mod[core, spot.z, j, spot.plane] = value.astype(bf16)
             self.mates.start()
 
         def for_line(self):
             self.mates.arrive()
-            for j in parts[self.part]:
-                all_rows_mod[core, spot.z, j] = (rows_mod[0, j] + rows_mod[1, j]) + (
-                    rows_mod[2, j] + rows_mod[3, j]
-                )
             self.line.open()
 
         def for_twin(self):
@@ -1165,9 +1172,9 @@
         for j, keys in enumerate((spatial, temporal)):
             disallowed[j] = jnp.where(ids[:, j : j + 1] == keys, 0.0, MASKED)
         tally[...] = jnp.zeros_like(tally)
-        share = b_ada.shape[1]
+        share = b_ada.shape[0]
         bias[...] = jnp.zeros_like(bias)
-        bias[0:1, :share] = b_ada[...].astype(f32)
+        bias[0:1, :share] = b_ada[...].astype(f32).reshape(1, share)
         bias[...] = pltpu.roll(bias[...], (2 * spot.chip + core) * share, 1)
 
     def standardize(j):
@@ -1432,8 +1439,27 @@
         need(turned_copy, 2 * j + 1)
         need(gated_copy, j)
 
+    leaving = [
+        pltpu.make_async_copy(src, dst, leave_sems.at[i])
+        for i, (src, dst) in enumerate(
+            (
+                (o_layer, r_layer),
+                (o_tokens, r_tokens),
+                (o_down, r_down),
+                (o_up, r_up),
+                (o_qkv_t, r_qkv_t),
+                (o_out_t, r_out_t),
+                (o_qkv_s, r_qkv_s),
+                (o_out_s, r_out_s),
+            )
+        )
+    ]
+    of_group = (leaving[2:3], leaving[3:4], leaving[4:6], leaving[6:8])
+
     def retire(n):
         scatters[n].store(puts[n])
+        for copy in of_group[n]:
+            copy.start()
         scatters[n].drain()
         if n < 2:
             scatters[n].release()
@@ -1497,7 +1523,7 @@
         DO_GHID: grad_hidden,
         DO_SENDP: lambda: grad_pre_copy().start(),
         DO_CONTRACT: contract,
-        DO_CLOSE: close,
+        DO_CLOSE: lambda: (close(), leaving[0].start()),
         DO_NEEDP: lambda: (need(grad_pre_copy), need(turned_copy, 4)),
         DO_UPT: up_terms,
         DO_BACK2: lambda i: back_project(2, 4, slope, 2 * i, 2 * i + 2),
@@ -1513,11 +1539,18 @@
         DO_OUTT: out_terms,
         DO_QKVT: qkv_terms,
         DO_BACK: lambda j, i: back_project(j, 3, grad_qkv, 2 * i, 2 * i + 2),
-        DO_SENTQ: lambda j: grad_qkv_copy(j).wait_send(),
+        DO_SENTQ: lambda j: (grad_qkv_copy(j).wait_send(), j == 0 and leaving[1].start()),
     }
-    for g, gather in enumerate(gathers):
-        gather.open(pieces[g])
-    steps_open()
+    def prepare():
+        for g, gather in enumerate(gathers):
+            gather.open(pieces[g])
+        steps_prepare()
+
+    greet(spot, prepare)
+    gathers[0].swap().start()
+    step_twin(core).start()
+    for gather in gathers[1:]:
+        gather.swap().start()
     for name, *indices in ORDER:
         step = steps_of[name]
         if isinstance(step, tuple):
@@ -1530,6 +1563,8 @@
         gathers[g].drain()
     for copy in each_twin_copy():
         copy.wait_send()
+    for copy in leaving:
+        copy.wait()
 
 
 def finish_kernel(cond, all_rows_mod, *refs):
@@ -1546,15 +1581,22 @@
     for copy in arriving:
         copy.start()
     total[...] = jnp.zeros_like(total)
+    clip = lax.broadcasted_iota(jnp.int32, (64, 512), 0)
+    at = lax.broadcasted_iota(jnp.int32, (64, 512), 1)
+    spread = (clip == 2 * (at >> 4) + (at & 1)).astype(jnp.bfloat16)
+    weights = contract_rows(cond[...], spread)[:32]
+    row = lax.broadcasted_iota(jnp.int32, (32, 512), 0)
+    kind = (lax.broadcasted_iota(jnp.int32, (32, 512), 1) & 15) >> 1
+    weights = jnp.where(row == 24, 1.0, weights)
     for j in range(3):
+        values = all_rows_mod[:, :, j].reshape(512, 384)
         for half in range(2):
             for chunk in range(3):
-                at = 2304 * j + 1152 * half + 384 * chunk
-                part = all_rows_mod[:, :, j, :, 384 * chunk : 384 * chunk + 384].astype(jnp.float32)
-                part = part[:, :, 8 * half : 8 * half + 8].reshape(64, 384)
-                low = part.astype(jnp.bfloat16)
-                o_ada[:, at : at + 384] = contract_rows(cond[...], low)[:24]
-                total[0:1, at : at + 384] = jnp.sum(part, axis=0, keepdims=True)
+                columns = slice(2304 * j + 1152 * half + 384 * chunk, 2304 * j + 1152 * half + 384 * chunk + 384)
+                own = jnp.where(kind == 2 * chunk + half, weights, 0.0).astype(jnp.bfloat16)
+                product = dot(own, values)
+                o_ada[:, columns] = product[:24]
+                total[0:1, columns] = product[24:25]
         if j == 0:
             for copy, onward in zip(arriving, leaving, strict=True):
                 copy.wait()
@@ -1579,12 +1621,16 @@
             jax.ShapeDtypeStruct((tok, width), bf16),
             jax.ShapeDtypeStruct((tok, width), f32),
             jax.ShapeDtypeStruct((64, 128), bf16),
-            jax.ShapeDtypeStruct((2, 4, 3, 16, 1152), bf16),
+            jax.ShapeDtypeStruct((2, 4, 3, 4, 16, 384), bf16),
         ]
         + [jax.ShapeDtypeStruct(shard.shape, f32) for shard in shards],
         in_specs=[in_vmem] * 2 + [pl.BlockSpec(memory_space=pltpu.SMEM)] + [in_vmem] * 11,
-        out_specs=[in_vmem] * 10,
+        out_specs=[in_hbm] * 2 + [in_vmem] * 2 + [in_hbm] * 6,
         scratch_shapes=[
+            vmem((tok, width), bf16),
+            vmem((tok, width), f32),
+            *(vmem(shard.shape, f32) for shard in shards),
+            dma((8,)),
             vmem((4, 2, 16) + block, bf16),
             vmem((4,) + block, f32),
             vmem((3, 4, 24, 384), f32),
@@ -1601,7 +1647,6 @@
             vmem((tok, 8), f32),
             vmem((8, 6912), f32),
             vmem((8, 6912), f32),
-            vmem((4, 3, 16, 1152), bf16),
             vmem((3, tok, width), bf16),
             vmem((tok, 128), f32),
             vmem((tok, width), bf16),
@@ -1680,7 +1725,7 @@
         seg_ids[None],
         frame_ids[None],
         patch_ids[None],
-        b_ada[None],
+        b_ada,
         w_ada,
         *shards,
     )

time: 176 us -> 169 us (0.960)
  Pallas kernels: 173 us -> 168 us
    pallas_call x1, Pallas kernels: 169 us -> 163 us  [layer(): pl.pallas_call(layer_kernel, out_shape=[jax.ShapeDtypeStruct((tok, width)...]
where the time goes in v7:
time: 169 us
  Pallas kernels  168 us (99%)
    pallas_call x1, Pallas kernels, layer(): pl.pallas_call(layer_kernel, out_shape=[jax.ShapeDtypeStruct((tok, width)...  163 us
    pallas_call x1, Pallas kernels, layer(): pl.pallas_call(finish_kernel, out_shape=[jax.ShapeDtypeStruct(w_ada.shape...  4.81 us

profile of v7, /device:TPU:0, one launch (start us, length us, event | category | flops | bytes accessed | tf_op | source)
XLA Modules:
  0.0 168.9 jit_solution(13384736662495989666)
XLA Ops:
  0.6 163.3 %shard_map.213 = (bf16[256,768]{1,0:T(8,128)(2,1)}, f32[256,768]{1,0:T(8,128)}, bf16[64,128]{1,0:T(8,128)(2,1)}, bf16[2,4,3,4,16,384]{5,4,3,2,1,0:T(8,128)(2,1)}...) custom-call(bf16[256,768]{1,0:T(8,128)(2,1)} %tokens.1, ...), custom_call_target="tpu_custom_call" | custom-call | tf_op jit(solution)/shard_map/pallas_call | solution.py:1618
  163.9 4.8 %shard_map.214 = (f32[24,6912]{1,0:T(8,128)}, f32[1,216]{1,0:T(1,128)}, bf16[256,768]{1,0:T(8,128)(2,1)}, f32[256,768]{1,0:T(8,128)}, f32[24,2304]{1,0:T(8,128)}...) custom-call(bf16[64,128]{1,0:T(8,128)(2,1)} %get-tuple-element.30.co, ...), custom_call_target="tpu_custom_call" | custom-call | tf_op jit(solution)/shard_map/pallas_call | solution.py:1689

commit v8 on v7

--- a/solution.py
+++ b/solution.py
@@ -1567,9 +1567,10 @@
         copy.wait()
 
 
-def finish_kernel(cond, all_rows_mod, *refs):
-    sources, o_ada, o_bias = refs[:8], refs[8], refs[9]
-    results, held, total, sem = refs[10:18], refs[18:26], refs[26], refs[27]
+def finish_kernel(*refs):
+    sources, r_ada, o_bias, results = refs[:10], refs[10], refs[11], refs[12:20]
+    held, o_ada, total, sem, ada_sem = refs[20:30], refs[30], refs[31], refs[32], refs[33]
+    cond, all_rows_mod = held[:2]
 
     def copies(first, second, kind):
         return [
@@ -1577,17 +1578,22 @@
             for i, (src, dst) in enumerate(zip(first, second, strict=True))
         ]
 
-    arriving, leaving = copies(sources, held, 0), copies(held, results, 1)
+    arriving, leaving = copies(sources, held, 0), copies(held[2:], results, 1)
     for copy in arriving:
         copy.start()
     total[...] = jnp.zeros_like(total)
     clip = lax.broadcasted_iota(jnp.int32, (64, 512), 0)
     at = lax.broadcasted_iota(jnp.int32, (64, 512), 1)
     spread = (clip == 2 * (at >> 4) + (at & 1)).astype(jnp.bfloat16)
+    arriving[0].wait()
     weights = contract_rows(cond[...], spread)[:32]
     row = lax.broadcasted_iota(jnp.int32, (32, 512), 0)
     kind = (lax.broadcasted_iota(jnp.int32, (32, 512), 1) & 15) >> 1
     weights = jnp.where(row == 24, 1.0, weights)
+    for copy, onward in zip(arriving[2:], leaving, strict=True):
+        copy.wait()
+        onward.start()
+    arriving[1].wait()
     for j in range(3):
         values = all_rows_mod[:, :, j].reshape(512, 384)
         for half in range(2):
@@ -1597,10 +1603,9 @@
                 product = dot(own, values)
                 o_ada[:, columns] = product[:24]
                 total[0:1, columns] = product[24:25]
-        if j == 0:
-            for copy, onward in zip(arriving, leaving, strict=True):
-                copy.wait()
-                onward.start()
+        part = slice(2304 * j, 2304 * j + 2304)
+        leaving.append(pltpu.make_async_copy(o_ada.at[:, part], r_ada.at[:, part], ada_sem.at[j]))
+        leaving[-1].start()
     place = lax.axis_index("wide") * 2 + lax.axis_index("narrow")
     share, columns = o_bias.shape[1], total.shape[1]
     turned = pltpu.roll(total[...], lax.rem(columns - place * share, columns), 1)
@@ -1693,10 +1698,10 @@
             jax.ShapeDtypeStruct((1, w_ada.shape[1] // 32), f32),
         ]
         + [jax.ShapeDtypeStruct(source.shape, source.dtype) for source in sources],
-        in_specs=[in_vmem] * 2 + [in_hbm] * 8,
-        out_specs=[in_vmem] * 2 + [in_hbm] * 8,
-        scratch_shapes=[vmem(source.shape, source.dtype) for source in sources]
-        + [vmem((8, w_ada.shape[1]), f32), dma((2, 8))],
+        in_specs=[in_hbm] * 10,
+        out_specs=[in_hbm, in_vmem] + [in_hbm] * 8,
+        scratch_shapes=[vmem(source.shape, source.dtype) for source in (outs[2], outs[3], *sources)]
+        + [vmem(w_ada.shape, f32), vmem((8, w_ada.shape[1]), f32), dma((2, 10)), dma((3,))],
         compiler_params=pltpu.CompilerParams(vmem_limit_bytes=60 * 2**20),
     )(outs[2], outs[3], *sources)
 

time: 169 us -> 169 us (level)
  no operation moved by 1% of the time
where the time goes in v8:
time: 169 us
  Pallas kernels  168 us (99%)
    pallas_call x1, Pallas kernels, layer(): pl.pallas_call(layer_kernel, out_shape=[jax.ShapeDtypeStruct((tok, width)...  163 us
    pallas_call x1, Pallas kernels, layer(): pl.pallas_call(finish_kernel, out_shape=[jax.ShapeDtypeStruct(w_ada.shape...  4.56 us

profile of v8, /device:TPU:0, one launch (start us, length us, event | category | flops | bytes accessed | tf_op | source)
XLA Modules:
  0.0 168.7 jit_solution(10677837453934144770)
XLA Ops:
  0.6 163.3 %shard_map.213 = (bf16[256,768]{1,0:T(8,128)(2,1)}, f32[256,768]{1,0:T(8,128)}, bf16[64,128]{1,0:T(8,128)(2,1)}, bf16[2,4,3,4,16,384]{5,4,3,2,1,0:T(8,128)(2,1)}...) custom-call(bf16[256,768]{1,0:T(8,128)(2,1)} %tokens.1, ...), custom_call_target="tpu_custom_call" | custom-call | tf_op jit(solution)/shard_map/pallas_call | solution.py:1623
  163.9 4.6 %shard_map.214 = (f32[24,6912]{1,0:T(8,128)}, f32[1,216]{1,0:T(1,128)}, bf16[256,768]{1,0:T(8,128)(2,1)}, f32[256,768]{1,0:T(8,128)}, f32[24,2304]{1,0:T(8,128)}...) custom-call(bf16[64,128]{1,0:T(8,128)(2,1)} %get-tuple-element.30.re, ...), custom_call_target="tpu_custom_call" | custom-call | tf_op jit(solution)/shard_map/pallas_call | solution.py:1694
